TPU v7x, 256 devices: a whole 4x4x8 slice. The times are simulated.
256 devices in a mesh: role: 2 (over y_hi), pipe: 16 (over y_lo, x, core), tp: 8 (over z).
Axes of the slice: x: 4, y: 4 (y_hi: 2, y_lo: 2; y = y_hi * 2 + y_lo), z: 8, core: 2. Of those that a mesh axis runs over, the one named last changes fastest.
Arguments:
- hidden: bfloat16 [2, 4096, 8192], P('role', 'pipe', 'tp'), may hold values from -256 to 256
- norm_gain: float32 [8192], P('tp'), may hold values from 0.1 to 1.9
- kv_weight: bfloat16 [8192, 2048], P('tp'), may hold values from -0.0625 to 0.0625
- queries: bfloat16 [2, 4096, 8192], P('role', 'pipe', 'tp'), may hold values from -128 to 128
- kv_cache: bfloat16 [2, 65536, 2048], P('role', 'pipe', 'tp'), may hold values from -5 to 5
- cache_len: int32 [2, 4096], P('role', 'pipe'), may hold values from 2 to 4096, as said below
- block_table: int32 [4352], P('pipe'), may hold values from 0 to 15, as said below
Outputs:
- attention: bfloat16 [2, 4096, 8192], P('role', 'pipe', 'tp')
- received: bfloat16 [2, 139264, 2048], P('role', 'pipe', 'tp')
Inputs may be any that keep to these rules, and one draw needn't show every extreme that they name: `block_table`: entry p * 272 + b names the decode owner (a pipe index) of block b of prefill owner p. No prefill owner sends more than 34 blocks to one decode owner, and in every draw one decode owner receives exactly 34 blocks from every prefill owner. `cache_len`: in pool 0 all 256 rows of one pipe index hold the same value, that prefill owner's span offset; in pool 1 each row holds its own cached length. The value 4096 occurs in both pools of every draw.
All inputs are finite; a program needn't handle non-finite values.
Results may differ from a plain program's by a relative error of at most 0.025.
Values may be sent and summed in bfloat16 or wider, within the bound.
No kernel may reach another device: no remote copies, remote signals or barrier semaphores. Data moves between devices by JAX's collectives and lax.ppermute only.
A program may use at most 64 MiB of HBM per device.

v0:
```python
import jax
import jax.numpy as jnp
from jax import lax
from jax.sharding import PartitionSpec as P

D = 8192
QH = 64
KVH = 8
HD = 128
ROWS = 256
CAP = 4096
BLK = 16
NBLK = 272


ROPE_BASE = 500000.0
EPSILON = 1e-05
NEG_FILL = -1e30


def shifted(block, axis, distance):
    devices = range(lax.axis_size(axis))
    route = [(i - distance, i) for i in devices if i - distance in devices]
    return lax.ppermute(block, axis, route)


def rotate_keys(key_rows, positions):
    rotary_half_width = key_rows.shape[-1] // 2
    frequency = ROPE_BASE ** (
        -2.0 * jnp.arange(rotary_half_width, dtype=jnp.float32) / key_rows.shape[-1]
    )
    angles = positions.astype(jnp.float32)[:, None] * frequency[None, :]
    cosine = jnp.cos(angles)[:, None, :]
    sine_part = jnp.sin(angles)[:, None, :]
    front_half = key_rows[..., :rotary_half_width]
    back_half = key_rows[..., rotary_half_width:]
    return jnp.concatenate(
        [front_half * cosine - back_half * sine_part, back_half * cosine + front_half * sine_part],
        axis=-1,
    )


def attend_rows(query_rows, kv_rows, visible):
    rows_total = query_rows.shape[0]
    block_rows = min(rows_total, 64)
    blocks_count = rows_total // block_rows
    score_scale = query_rows.shape[-1] ** (-0.5)
    key_part = kv_rows[:, :, 0]
    value_part = kv_rows[:, :, 1]

    def one_block(block_index):
        start_row = block_index * block_rows
        query_block = lax.dynamic_slice_in_dim(query_rows, start_row, block_rows, 0)
        mask_block = lax.dynamic_slice_in_dim(visible, start_row, block_rows, 0)
        scores = (
            jnp.einsum("rhgd,shd->rhgs", query_block, key_part, preferred_element_type=jnp.float32)
            * score_scale
        )
        scores = jnp.where(mask_block[:, None, None, :], scores, NEG_FILL)
        top_score = jnp.max(scores, axis=-1, keepdims=True)
        weights = jnp.exp(scores - top_score)
        weight_sum = jnp.sum(weights, axis=-1)
        mixed_rows = jnp.einsum(
            "rhgs,shd->rhgd",
            weights.astype(jnp.bfloat16),
            value_part,
            preferred_element_type=jnp.float32,
        )
        return (mixed_rows / weight_sum[..., None]).astype(jnp.bfloat16)

    blocks = lax.map(one_block, jnp.arange(blocks_count, dtype=jnp.int32))
    return blocks.reshape(rows_total, -1)


def dispatch_block_list(blocks, table, owners, capacity):
    onehot = (table[:, None] == jnp.arange(owners, dtype=jnp.int32)[None, :]).astype(jnp.int32)
    before = jnp.cumsum(onehot, axis=0) - onehot
    cache_slot_index = jnp.sum(before * onehot, axis=1)
    target = table * capacity + cache_slot_index
    selector = target[None, :] == jnp.arange(owners * capacity, dtype=jnp.int32)[:, None]
    buffer = jnp.dot(
        selector.astype(jnp.bfloat16), blocks, preferred_element_type=jnp.float32
    ).astype(jnp.bfloat16)
    return buffer.reshape(owners, capacity, -1)


def local(hidden, norm_gain, kv_weight, queries, kv_cache, cache_len, block_table):
    hidden_rows = hidden[0]
    query_flat = queries[0]
    cache_rows = kv_cache[0]
    lengths = cache_len[0]
    role_index = lax.axis_index("role")
    owners = lax.axis_size("pipe")
    capacity = 2 * NBLK // owners
    heads_here = cache_rows.shape[1] // (2 * HD)
    row_ids = jnp.arange(ROWS, dtype=jnp.int32)
    features = hidden_rows.astype(jnp.float32)
    square_sum = lax.psum(jnp.sum(features * features, axis=1), "tp")
    inverse_root_mean_square = lax.rsqrt(square_sum / D + EPSILON)
    normed = (features * inverse_root_mean_square[:, None] * norm_gain[None, :]).astype(
        jnp.bfloat16
    )
    projected = lax.psum_scatter(
        lax.dot_general(
            kv_weight, normed, (((0,), (1,)), ((), ())), preferred_element_type=jnp.float32
        ).astype(jnp.bfloat16),
        "tp",
        scatter_dimension=0,
        tiled=True,
    ).astype(jnp.float32)
    projected = projected.T.reshape(ROWS, heads_here, 2, HD)
    positions = lengths + jnp.where(role_index == 0, row_ids, 0)
    rotated = rotate_keys(projected[:, :, 0], positions)
    new_kv = jnp.stack([rotated, projected[:, :, 1]], axis=2).astype(jnp.bfloat16)
    cache_four = cache_rows.reshape(CAP, heads_here, 2, HD)
    block_ids = jnp.arange(NBLK, dtype=jnp.int32)
    live_rows = jnp.where(
        block_ids < CAP // BLK, jnp.clip(lengths[0] - block_ids * BLK, 0, BLK), BLK
    )
    row_live = jnp.arange(BLK, dtype=jnp.int32)[None, :] < live_rows[:, None]
    blocks = jnp.concatenate([cache_four, new_kv], axis=0).reshape(NBLK, BLK, -1)
    blocks = jnp.where(row_live[:, :, None], blocks, jnp.zeros_like(blocks)).reshape(NBLK, -1)
    send_blocks = dispatch_block_list(blocks, block_table, owners, capacity)
    routed_blocks = lax.all_to_all(send_blocks, "pipe", split_axis=0, concat_axis=0, tiled=True)
    got_blocks = shifted(routed_blocks, "role", 1)
    paged = jnp.where(role_index == 0, send_blocks, got_blocks).reshape(-1, heads_here * 2 * HD)
    query_rows = query_flat.reshape(ROWS, heads_here, QH // KVH, HD)
    cache_visible = jnp.arange(CAP, dtype=jnp.int32)[None, :] < lengths[:, None]
    kv_rows = jnp.concatenate([cache_four, new_kv], axis=0)
    fresh_visible = jnp.where(
        role_index == 0, row_ids[None, :] <= row_ids[:, None], row_ids[None, :] == row_ids[:, None]
    )
    visible = jnp.concatenate([cache_visible, fresh_visible], axis=1)
    result = attend_rows(query_rows, kv_rows, visible)
    return (result[None], paged[None])


def solution(mesh):
    in_specs = (
        P("role", "pipe", "tp"),
        P("tp"),
        P("tp", None),
        P("role", "pipe", "tp"),
        P("role", "pipe", "tp"),
        P("role", "pipe"),
        P("pipe"),
    )
    out_specs = (P("role", "pipe", "tp"), P("role", "pipe", "tp"))
    return jax.shard_map(local, mesh=mesh, in_specs=in_specs, out_specs=out_specs, check_vma=False)
```

profile of v0, /device:TPU:1, one launch (start us, length us, event | category | flops | bytes accessed | tf_op | source)
XLA Modules:
  0.0 305.0 jit_solution(8759933350811548477)
XLA Ops:
  7.2 0.0 copy-start
  7.2 0.0 reduce-scatter.2.cloned.1.call-start
  7.2 1.4 fusion.29
  8.6 17.3 %psum.7 = f32[256]{0:T(256)S(1)} all-reduce(f32[256]{0:T(256)S(1)} %fusion.29), channel_id=1, replica_groups=mesh['role'=2,'pipe'=16,'tp'=8] {'tp'}, use_global_device_ids=true, to_apply=%region_1.0 | all-reduce | flops 256 | bytes 2048 | tf_op jit(solution)/shard_map/psum | solution.py:98
  25.9 4.7 %fusion.26 = bf16[2048,256]{0,1:T(8,128)(2,1)} fusion(bf16[1024,2048]{1,0:T(8,128)(2,1)} %param.11, bf16[1,256,1024]{2,1,0:T(8,128)(2,1)} %param.9, f32[1024]{0:T(1024)} %param.10, f32[256]{0:T(256)S(1)} %add_rsqrt_fusion), kind=kOutput, calls=%fused_computation.23 | convolution fusion | flops 1075314688 | bytes 5772288 | tf_op jit(solution)/shard_map/dot_general | solution.py:104
  30.6 0.0 copy-start.3
  30.6 0.0 copy-start.2
  30.6 0.0 reduce-scatter.2.cloned.1.call-update
  30.6 0.0 copy-done
  30.6 2.9 copy.19
  33.5 0.0 copy-done.3
  33.5 0.5 slice.42
  34.0 0.7 clamp_select_fusion
  34.7 0.1 iota_compare_fusion.5
  34.8 1.4 broadcast_in_dim.33
  36.1 0.8 copy.33
  36.9 0.0 copy-done.2
  37.0 0.9 reduce-window.6
  37.8 0.2 slice_reduce_fusion
  38.1 0.1 bitcast_bitcast_fusion
  38.2 28.3 %reduce-scatter.2.cloned.1.call-done = bf16[256,256]{0,1:T(8,128)(2,1)} async-done(((bf16[2048,256]{0,1:T(8,128)(2,1)}), bf16[256,256]{0,1:T(8,128)(2,1)}) %reduce-scatter.2.cloned.1.call-update) | async-done | bytes 131088 | tf_op jit(solution)/shard_map/reduce_scatter | solution.py:103
  66.6 1.0 copy.29
  67.6 0.3 fusion.43
  67.9 1.8 maximum_maximum_fusion
  69.7 4.5 %copy.26 = bf16[4352,1,2,128]{3,2,0,1:T(2,128)(2,1)} copy(bf16[4352,1,2,128]{0,3,2,1:T(8,128)(2,1)S(1)} %maximum_maximum_fusion) | data formatting | bytes 4456448 | tf_op jit(solution)/shard_map/concatenate | solution.py:129
  74.2 6.0 %reshape.229 = bf16[272,4096]{1,0:T(8,128)(2,1)} reshape(bf16[4352,1,2,128]{3,2,0,1:T(2,128)(2,1)} %copy.26) | data formatting | bytes 4456448 | tf_op jit(solution)/shard_map/reshape | solution.py:121
  80.2 6.2 %convolution_convert_fusion = bf16[544,4096]{1,0:T(8,128)(2,1)} fusion(pred[272,4096]{1,0:T(8,128)(4,1)S(1)} %bitcast.122, bf16[272,4096]{1,0:T(8,128)(2,1)} %reshape.229, s32[272]{0:T(512)S(1)} %multiply_add_fusion), kind=kOutput, calls=%fused_computation.18 | convolution fusion | flops 1215644160 | bytes 7799872 | tf_op jit(solution)/shard_map/dot_general | solution.py:81
  86.4 5.6 %reshape.230 = bf16[16,34,4096]{2,1,0:T(8,128)(2,1)} reshape(bf16[544,4096]{1,0:T(8,128)(2,1)} %convolution_convert_fusion) | data formatting | bytes 8912896 | tf_op jit(solution)/shard_map/reshape | solution.py:84
  92.0 0.0 copy-start.1
  92.0 10.5 %all-to-all-start = ((bf16[16,34,4096]{2,1,0:T(8,128)(2,1)}), bf16[16,34,4096]{2,1,0:T(8,128)(2,1)}, u32[]{:S(2)}, u32[]{:S(2)}) async-start(bf16[16,34,4096]{2,1,0:T(8,128)(2,1)} %reshape.230), calls=%async_computation.1 | async-start | bytes 10485760 | tf_op jit(solution)/shard_map/all_to_all | solution.py:124
  102.5 0.0 copy-done.1
  102.5 0.9 copy.32
  103.4 0.7 iota_compare_fusion
  104.1 0.1 pad_add_fusion
  104.2 1.5 slice_bitcast_fusion
  105.7 1.7 copy.22
  107.4 1.7 copy.23
  109.1 63.5 %all-to-all-done = bf16[16,34,4096]{2,1,0:T(8,128)(2,1)} async-done(((bf16[16,34,4096]{2,1,0:T(8,128)(2,1)}), bf16[16,34,4096]{2,1,0:T(8,128)(2,1)}, u32[]{:S(2)}, u32[]{:S(2)}) %all-to-all-start) | async-done | bytes 4456480 | tf_op jit(solution)/shard_map/all_to_all | solution.py:124
  172.6 7.0 %copy.27 = bf16[16,34,4096]{2,0,1:T(8,128)(2,1)} copy(bf16[16,34,4096]{2,1,0:T(8,128)(2,1)} %all-to-all-done) | data formatting | bytes 8912896 | tf_op jit(solution)/shard_map/all_to_all | solution.py:124
  179.6 6.5 %collective-permute-start = (bf16[16,34,4096]{2,0,1:T(8,128)(2,1)}, bf16[16,34,4096]{2,0,1:T(8,128)(2,1)}, u32[]{:S(2)}, u32[]{:S(2)}) collective-permute-start(bf16[16,34,4096]{2,0,1:T(8,128)(2,1)} %copy.27), channel_id=1, source_target_pairs={{0,128},{1,129},{2,130},{3,131},{4,132},{5,133},{6,134},{7,135},{8... | collective-permute-start | bytes 13369352 | tf_op jit(solution)/shard_map/ppermute | solution.py:24
  186.1 33.1 %while.10 = (s32[]{:T(128)}, bf16[4,64,1,8,128]{4,3,1,2,0:T(8,128)(2,1)}, s32[4]{0:T(128)S(1)}, pred[256,4352]{1,0:T(8,128)(4,1)S(1)}, bf16[256,1,8,128]{3,2,0,1...) while((s32[]{:T(128)}, ...), condition=%wide.region_6.7_spmd, body=%wide.region_3.6_spmd.sunk | while | flops 1156578304 | bytes 30075068 | solution.py:71
  186.1 0.7 dynamic_slice.22
  187.5 3.5 %fusion.59 = (f32[64,8]{1,0:T(8,128)S(1)}, f32[64,1,8,4352]{3,2,0,1:T(8,128)S(1)}) fusion(bf16[4352,1,128]{2,0,1:T(8,128)(2,1)S(1)} %get-tuple-element.150, bf16[256,1,8,128]{3,2,0,1:T(8,128)(2,1)} %get-tuple-element.149, s32[]{:T(128)S(6)} %select_n.68, pred[64,4352]{1,0:T(8,128)(4,1)S(1)} %constant_dynamic-slice_fusion.2), kind=kOutput, calls=%fused_computation.73.clone.1 | convolution fusion | flops 577109504 | bytes 10438660 | tf_op jit(solution)/shard_map/while/body/eval_jaxpr/rhgd,shd->rhgs/dot_general | solution.py:56
  191.0 1.3 fusion.60
  192.3 2.1 fusion.61
  194.4 0.7 dynamic_slice.22
  195.8 3.5 %fusion.59 = (f32[64,8]{1,0:T(8,128)S(1)}, f32[64,1,8,4352]{3,2,0,1:T(8,128)S(1)}) fusion(bf16[4352,1,128]{2,0,1:T(8,128)(2,1)S(1)} %get-tuple-element.150, bf16[256,1,8,128]{3,2,0,1:T(8,128)(2,1)} %get-tuple-element.149, s32[]{:T(128)S(6)} %select_n.68, pred[64,4352]{1,0:T(8,128)(4,1)S(1)} %constant_dynamic-slice_fusion.2), kind=kOutput, calls=%fused_computation.73.clone.1 | convolution fusion | flops 577109504 | bytes 10438660 | tf_op jit(solution)/shard_map/while/body/eval_jaxpr/rhgd,shd->rhgs/dot_general | solution.py:56
  199.2 1.3 fusion.60
  200.6 2.1 fusion.61
  202.7 0.7 dynamic_slice.22
  204.1 3.5 %fusion.59 = (f32[64,8]{1,0:T(8,128)S(1)}, f32[64,1,8,4352]{3,2,0,1:T(8,128)S(1)}) fusion(bf16[4352,1,128]{2,0,1:T(8,128)(2,1)S(1)} %get-tuple-element.150, bf16[256,1,8,128]{3,2,0,1:T(8,128)(2,1)} %get-tuple-element.149, s32[]{:T(128)S(6)} %select_n.68, pred[64,4352]{1,0:T(8,128)(4,1)S(1)} %constant_dynamic-slice_fusion.2), kind=kOutput, calls=%fused_computation.73.clone.1 | convolution fusion | flops 577109504 | bytes 10438660 | tf_op jit(solution)/shard_map/while/body/eval_jaxpr/rhgd,shd->rhgs/dot_general | solution.py:56
  207.5 1.3 fusion.60
  208.9 2.1 fusion.61
  211.0 0.7 dynamic_slice.22
  212.3 3.5 %fusion.59 = (f32[64,8]{1,0:T(8,128)S(1)}, f32[64,1,8,4352]{3,2,0,1:T(8,128)S(1)}) fusion(bf16[4352,1,128]{2,0,1:T(8,128)(2,1)S(1)} %get-tuple-element.150, bf16[256,1,8,128]{3,2,0,1:T(8,128)(2,1)} %get-tuple-element.149, s32[]{:T(128)S(6)} %select_n.68, pred[64,4352]{1,0:T(8,128)(4,1)S(1)} %constant_dynamic-slice_fusion.2), kind=kOutput, calls=%fused_computation.73.clone.1 | convolution fusion | flops 577109504 | bytes 10438660 | tf_op jit(solution)/shard_map/while/body/eval_jaxpr/rhgd,shd->rhgs/dot_general | solution.py:56
  215.8 1.3 fusion.60
  217.2 2.1 fusion.61
  219.2 2.1 broadcast_in_dim_reshape.6
  221.3 58.0 %collective-permute-done = bf16[16,34,4096]{2,0,1:T(8,128)(2,1)} collective-permute-done((bf16[16,34,4096]{2,0,1:T(8,128)(2,1)}, bf16[16,34,4096]{2,0,1:T(8,128)(2,1)}, u32[]{:S(2)}, u32[]{:S(2)}) %collective-permute-start) | collective-permute-done | bytes 4456480 | tf_op jit(solution)/shard_map/ppermute | solution.py:24
  279.3 11.1 %copy_select_fusion = bf16[16,34,4096]{2,1,0:T(8,128)(2,1)} fusion(bf16[16,34,4096]{2,1,0:T(8,128)(2,1)} %reshape.230, bf16[16,34,4096]{2,0,1:T(8,128)(2,1)} %collective-permute-done, pred[]{:T(512)S(6)} %eq.49), kind=kLoop, calls=%fused_computation.19 | loop fusion | flops 2228224 | bytes 13369345 | tf_op jit(solution)/shard_map/jit(_where)/select_n | solution.py:126
  290.3 7.8 %broadcast_in_dim_reshape.7 = bf16[1,8704,256]{2,1,0:T(8,128)(2,1)} reshape(bf16[16,34,4096]{2,1,0:T(8,128)(2,1)} %copy_select_fusion) | data formatting | bytes 8912896 | tf_op jit(solution)/shard_map/broadcast_in_dim;reshape | solution.py:135
  (17 shorter events, 0.3 us)
Async XLA Ops:
  7.2 23.5 %copy-start = (bf16[1,4096,256]{2,1,0:T(8,128)(2,1)S(1)}, bf16[1,4096,256]{2,1,0:T(8,128)(2,1)}, u32[]{:S(2)}) copy-start(bf16[1,4096,256]{2,1,0:T(8,128)(2,1)} %param.13) | copy-start | bytes 6291460
  7.2 59.4 %reduce-scatter.2.cloned.1.call-start = ((), (), s32[]{:S(2)}) async-start(), calls=%async_computation.2 | async-start | bytes 1179648 | tf_op jit(solution)/shard_map/reduce_scatter | solution.py:103
  30.6 2.9 copy-start.3
  30.6 6.3 %copy-start.2 = (s32[272]{0:T(512)S(1)}, s32[272]{0:T(512)}, u32[]{:S(2)}) copy-start(s32[272]{0:T(512)} %param.15) | copy-start | bytes 3268
  92.0 10.5 %copy-start.1 = (bf16[1,256,1024]{2,1,0:T(8,128)(2,1)S(1)}, bf16[1,256,1024]{2,1,0:T(8,128)(2,1)}, u32[]{:S(2)}) copy-start(bf16[1,256,1024]{2,1,0:T(8,128)(2,1)} %param.12) | copy-start | bytes 1572868
  92.0 80.6 %all-to-all-start = ((bf16[16,34,4096]{2,1,0:T(8,128)(2,1)}), bf16[16,34,4096]{2,1,0:T(8,128)(2,1)}, u32[]{:S(2)}, u32[]{:S(2)}) async-start(bf16[16,34,4096]{2,1,0:T(8,128)(2,1)} %reshape.230), calls=%async_computation.1 | async-start | bytes 10485760 | tf_op jit(solution)/shard_map/all_to_all | solution.py:124
  179.6 99.6 %collective-permute-start = (bf16[16,34,4096]{2,0,1:T(8,128)(2,1)}, bf16[16,34,4096]{2,0,1:T(8,128)(2,1)}, u32[]{:S(2)}, u32[]{:S(2)}) collective-permute-start(bf16[16,34,4096]{2,0,1:T(8,128)(2,1)} %copy.27), channel_id=1, source_target_pairs={{0,128},{1,129},{2,130},{3,131},{4,132},{5,133},{6,134},{7,135},{8... | collective-permute-start | bytes 13369352 | tf_op jit(solution)/shard_map/ppermute | solution.py:24
Sparse Core Ops, SparseCore 0:
  30.7 35.7 reduce-scatter.1
where the time goes:
time: 307 us; the launch traced here: 305 us
  waiting for transfers between devices  150 us (49%)
  local copies, waits for them, and re-layouts  48.2 us (16%)
  matrix products  33 us (11%)
  other arithmetic  22.5 us (7%)
  blocking collectives  17.3 us (6%)
  starting transfers between devices  17 us (6%)
  between operations  14.2 us (5%)
    all_to_all x1, waiting for transfers between devices, local(): lax.all_to_all(send_blocks, 'pipe', split_axis=0, concat_axis=0, tiled=True)  63.5 us
    ppermute x1, waiting for transfers between devices, shifted(): return lax.ppermute(block, axis, route)  58 us
    reduce_scatter x1, waiting for transfers between devices, local(): lax.psum_scatter(lax.dot_general(kv_weight, normed, (((0,), (1,)), ((), (...  28.3 us
    psum x1, blocking collectives, local(): square_sum = lax.psum(jnp.sum(features * features, axis=1), 'tp')  17.3 us
    dot_general x4, matrix products, one_block(): jnp.einsum('rhgd,shd->rhgs', query_block, key_part, preferred_element_typ...  13.8 us
    select_n x1, other arithmetic, local(): jnp.where(role_index == 0, send_blocks, got_blocks)  11.1 us
    all_to_all x1, starting transfers between devices, local(): lax.all_to_all(send_blocks, 'pipe', split_axis=0, concat_axis=0, tiled=True)  10.5 us
    another operation x2, local copies, waits for them, and re-layouts, local(): return (result[None], paged[None])  9.86 us
  transfers between devices with their start and end apart: 3, of which 3 were waited for; matrix products, arithmetic and copies ran while one was open for 15% of the time, Pallas kernels for 0%

commit v1 on v0

v1 whole, which is shorter than its diff:
```python
import jax
import jax.numpy as jnp
from jax import lax
from jax.experimental import pallas as pl
from jax.experimental.pallas import tpu as pltpu
from jax.sharding import PartitionSpec as P

D = 8192
QH = 64
KVH = 8
HD = 128
ROWS = 256
CAP = 4096
BLK = 16
NBLK = 272
CAPB = 34
N_PIPE = 16
CBLK = CAP // BLK
SLOTS = N_PIPE * CAPB
DIGITS = 16
GROUP = QH // KVH

ROPE_BASE = 500000.0
EPSILON = 1e-05
NEG_FILL = -1e30
EXP_SCALE = HD**-0.5 * 1.4426950408889634
MIB = 1024 * 1024

VM = pl.BlockSpec(memory_space=pltpu.VMEM)
SM = pl.BlockSpec(memory_space=pltpu.SMEM)
ANY = pl.BlockSpec(memory_space=pl.ANY)


def params(mib=40):
    return pltpu.CompilerParams(vmem_limit_bytes=mib * MIB)


def cross(x):
    pairs = [(p, N_PIPE + (p ^ 8)) for p in range(N_PIPE)]
    return lax.ppermute(x, ("role", "pipe"), pairs)


def pipe_move(x, move):
    pairs = []
    for y in range(2):
        for c in range(4):
            for core in range(2):
                ny, nc, ncore = move(y, c, core)
                pairs.append(((y * 4 + c) * 2 + core, (ny * 4 + nc) * 2 + ncore))
    return lax.ppermute(x, "pipe", pairs)


def pipe_exchange(x):
    parts = x.reshape((N_PIPE, CAPB) + x.shape[1:])
    return lax.all_to_all(parts, "pipe", 0, 0, tiled=True).reshape(x.shape)


def project_kernel(h_ref, gain_ref, w_ref, out_ref, scaled, digits):
    @pl.when(pl.program_id(0) == 0)
    def _():
        h = h_ref[...].astype(jnp.float32)
        scaled[...] = (h * gain_ref[...]).astype(jnp.bfloat16)
        total = jnp.sum(h * h, axis=1, keepdims=True)
        across = jnp.transpose(jnp.broadcast_to(total, (ROWS, 128)))
        rest = across[0:1, :] * (2.0**-27)
        rows = []
        for _ in range(DIGITS):
            rest = rest * 32.0
            digit = jnp.floor(rest)
            rest = rest - digit
            rows.append(digit)
        digits[...] = jnp.concatenate(rows, axis=0).astype(jnp.bfloat16)

    out_ref[0, :ROWS, :] = jnp.dot(
        scaled[...], w_ref[...], preferred_element_type=jnp.float32
    ).astype(jnp.bfloat16)
    out_ref[0, ROWS:, :] = digits[...]


def project(hidden, gain, weight):
    feats = hidden.shape[1]
    heads = weight.shape[1] // (2 * HD)
    return pl.pallas_call(
        project_kernel,
        grid=(heads,),
        in_specs=[
            pl.BlockSpec((ROWS, feats), lambda i: (0, 0)),
            pl.BlockSpec((1, feats), lambda i: (0, 0)),
            pl.BlockSpec((feats, 2 * HD), lambda i: (0, i)),
        ],
        out_specs=pl.BlockSpec((1, ROWS + DIGITS, 2 * HD), lambda i: (i, 0, 0)),
        out_shape=jax.ShapeDtypeStruct((heads, ROWS + DIGITS, 2 * HD), jnp.bfloat16),
        scratch_shapes=[
            pltpu.VMEM((ROWS, feats), jnp.bfloat16),
            pltpu.VMEM((DIGITS, ROWS), jnp.bfloat16),
        ],
        compiler_params=params(),
        name="project",
    )(hidden, gain, weight)


def fresh_kernel(sum_ref, cos_ref, sin_ref, out_ref):
    digits = sum_ref[ROWS:, :].astype(jnp.float32)
    total = jnp.zeros((1, ROWS), jnp.float32)
    for k in range(DIGITS - 1, -1, -1):
        total = total + digits[k : k + 1, :] * (2.0 ** (27 - 5 * (k + 1)))
    inverse = lax.rsqrt(total / D + EPSILON)
    inverse = jnp.transpose(jnp.broadcast_to(inverse, (HD, ROWS)))
    key = sum_ref[:ROWS, :HD].astype(jnp.float32) * inverse
    value = sum_ref[:ROWS, HD:].astype(jnp.float32) * inverse
    key = key * cos_ref[...] + pltpu.roll(key, HD // 2, 1) * sin_ref[...]
    out_ref[:, :HD] = key.astype(jnp.bfloat16)
    out_ref[:, HD:] = value.astype(jnp.bfloat16)


def fresh_rows(summed, cosine, sine):
    return pl.pallas_call(
        fresh_kernel,
        in_specs=[VM, VM, VM],
        out_specs=VM,
        out_shape=jax.ShapeDtypeStruct((ROWS, 2 * HD), jnp.bfloat16),
        compiler_params=params(),
        name="fresh",
    )(summed, cosine, sine)


def index_kernel(info_ref, table_ref, out_ref):
    role = info_ref[0]
    me = info_ref[1]
    other = lax.rem(me + 8, N_PIPE)
    table = table_ref[...]
    block = lax.broadcasted_iota(jnp.int32, (NBLK, 1), 0)
    earlier = (
        lax.broadcasted_iota(jnp.int32, (NBLK, NBLK), 1)
        < lax.broadcasted_iota(jnp.int32, (NBLK, NBLK), 0)
    ).astype(jnp.bfloat16)
    owner_ids = lax.broadcasted_iota(jnp.int32, (NBLK, N_PIPE), 1)
    slot_ids = lax.broadcasted_iota(jnp.int32, (1, SLOTS), 1)
    sent_row = jnp.where(role == 0, me, other)
    turn = jnp.where(role == 0, 8, 0)
    sent = jnp.zeros((NBLK, 1), jnp.int32)
    own = jnp.zeros((NBLK, 1), jnp.int32)
    fresh = jnp.full((BLK, SLOTS), -1, jnp.int32)
    fresh_block = lax.broadcasted_iota(jnp.int32, (BLK, 1), 0)
    for p in range(N_PIPE):
        column = table[:, p : p + 1]
        onehot = column == owner_ids
        before = jnp.dot(
            earlier, onehot.astype(jnp.bfloat16), preferred_element_type=jnp.float32
        )
        slot = jnp.sum(jnp.where(onehot, before, 0.0), axis=1, keepdims=True)
        slot = slot.astype(jnp.int32)
        target = lax.rem(column + turn, N_PIPE) * CAPB + slot
        sent = jnp.where(sent_row == p, target, sent)
        own = jnp.where(me == p, column * CAPB + slot, own)
        place = jnp.where(column == me, p * CAPB + slot, -1)[CBLK:, :]
        fresh = jnp.where(place == slot_ids, fresh_block + p * BLK, fresh)

    def source(target):
        return jnp.max(jnp.where(target == slot_ids, block, -1), axis=0, keepdims=True)

    sent_source = source(sent)
    out_ref[0:1, :] = jnp.where(
        jnp.logical_and(sent_source >= 0, sent_source < CBLK), sent_source, CBLK
    )
    own_source = source(own)
    own_cached = jnp.where(
        jnp.logical_and(own_source >= 0, own_source < CBLK), own_source, SLOTS
    )
    turned = lax.rem(slot_ids + 8 * CAPB, SLOTS)
    out_ref[1:2, :] = jnp.where(role == 0, own_cached, turned)
    out_ref[2:3, :] = jnp.where(role == 0, own_cached, slot_ids)
    out_ref[3:4, :] = jnp.where(
        role == 0,
        jnp.maximum(own_source - CBLK, -1),
        jnp.max(fresh, axis=0, keepdims=True),
    )


def slot_index(info, table):
    return pl.pallas_call(
        index_kernel,
        in_specs=[SM, VM],
        out_specs=VM,
        out_shape=jax.ShapeDtypeStruct((4, SLOTS), jnp.int32),
        compiler_params=params(),
        name="slot_index",
    )(info, table)


def dispatch_kernel(info_ref, index_ref, own_ref, crossed_ref, out_ref, held, sem):
    @pl.when(info_ref[0] == 0)
    def _():
        copy = pltpu.make_async_copy(own_ref, held.at[pl.ds(0, CBLK)], sem)
        copy.start()
        copy.wait()

    @pl.when(info_ref[0] != 0)
    def _():
        copy = pltpu.make_async_copy(crossed_ref, held.at[pl.ds(0, CBLK)], sem)
        copy.start()
        copy.wait()

    held[CBLK] = jnp.zeros(held.shape[1:], held.dtype)

    def step(r, _):
        out_ref[r] = held[index_ref[0, r]]
        return 0

    lax.fori_loop(0, SLOTS, step, 0, unroll=16)


def dispatch(info, index, own, crossed, name):
    shape = own.shape[1:]
    return pl.pallas_call(
        dispatch_kernel,
        in_specs=[SM, SM, ANY, ANY],
        out_specs=VM,
        out_shape=jax.ShapeDtypeStruct((SLOTS,) + shape, jnp.bfloat16),
        scratch_shapes=[
            pltpu.VMEM((CBLK + 1,) + shape, jnp.bfloat16),
            pltpu.SemaphoreType.DMA,
        ],
        compiler_params=params(),
        name=name,
    )(info, index, own, crossed)


def place_kernel(info_ref, index_ref, *refs):
    own = refs[0:3]
    got = refs[3:6]
    own_fresh = refs[6]
    pieces = refs[7:15]
    partner_ref = refs[15]
    out_ref = refs[16]
    held = refs[17:20]
    fresh = refs[20]
    sems = refs[21]
    me = info_ref[1]
    y = lax.div(me, 8)
    column = lax.rem(lax.div(me, 2), 4)
    core = lax.rem(me, 2)

    @pl.when(info_ref[0] == 0)
    def _():
        copies = [
            pltpu.make_async_copy(own[k], held[k].at[pl.ds(0, CBLK)], sems.at[k])
            for k in range(3)
        ]
        copies.append(pltpu.make_async_copy(own_fresh, fresh.at[pl.ds(0, BLK)], sems.at[3]))
        for copy in copies:
            copy.start()
        for copy in copies:
            copy.wait()

    @pl.when(info_ref[0] != 0)
    def _():
        copies = [
            pltpu.make_async_copy(got[k], held[k].at[pl.ds(0, SLOTS)], sems.at[k])
            for k in range(3)
        ]
        count = 3
        for k in range(16):
            row = k % 8
            owner_y = 1 - y if row < 4 else y
            owner_column = lax.rem(column + 4 - (0, 1, 3, 2)[row % 4], 4)
            owner_core = core if k < 8 else 1 - core
            owner = (owner_y * 4 + owner_column) * 2 + owner_core
            source = pieces[row] if k < 8 else partner_ref.at[row]
            copies.append(
                pltpu.make_async_copy(
                    source, fresh.at[pl.ds(owner * BLK, BLK)], sems.at[count]
                )
            )
            count += 1
        for copy in copies:
            copy.start()
        for copy in copies:
            copy.wait()

    for ref in held:
        ref[SLOTS] = jnp.zeros(ref.shape[1:], ref.dtype)

    def step(r, _):
        first = index_ref[1, r]
        new = index_ref[3, r]
        key = jnp.concatenate([held[0][first], held[1][index_ref[2, r]]], axis=0)
        old = jnp.concatenate([key, held[2][first]], axis=1)
        out_ref[r] = jnp.where(new >= 0, fresh[jnp.maximum(new, 0)], old)
        return 0

    lax.fori_loop(0, SLOTS, step, 0, unroll=8)


def place(info, index, own, got, own_fresh, pieces, partner):
    return pl.pallas_call(
        place_kernel,
        in_specs=[SM, SM] + [ANY] * 16,
        out_specs=VM,
        out_shape=jax.ShapeDtypeStruct((SLOTS, BLK, 2 * HD), jnp.bfloat16),
        scratch_shapes=[
            pltpu.VMEM((SLOTS + 1, BLK // 2, HD), jnp.bfloat16),
            pltpu.VMEM((SLOTS + 1, BLK // 2, HD), jnp.bfloat16),
            pltpu.VMEM((SLOTS + 1, BLK, HD), jnp.bfloat16),
            pltpu.VMEM((N_PIPE * BLK, BLK, 2 * HD), jnp.bfloat16),
            pltpu.SemaphoreType.DMA((20,)),
        ],
        compiler_params=params(),
        name="place",
    )(info, index, *own, *got, own_fresh, *pieces, partner)


KEYS = 512


def cached_kernel(q_ref, kv_ref, len_ref, sum_ref, top_ref, bias, values, scores):
    @pl.when(pl.program_id(0) == 0)
    def _():
        values[:, :HD] = kv_ref[:, HD:]
        values[:, HD:] = jnp.ones((CAP, HD), jnp.bfloat16)
        lengths = len_ref[...]
        for k in range(0, CAP, KEYS):
            ids = lax.broadcasted_iota(jnp.int32, (ROWS, KEYS), 1) + k
            bias[:, k : k + KEYS] = jnp.where(ids < lengths, 0.0, NEG_FILL)

    query = q_ref[...]
    top = jnp.full((ROWS, HD), NEG_FILL, jnp.float32)
    for k in range(0, CAP, KEYS):
        part = lax.dot_general(
            query,
            kv_ref[k : k + KEYS, :HD],
            (((1,), (1,)), ((), ())),
            preferred_element_type=jnp.float32,
        )
        part = part + bias[:, k : k + KEYS]
        scores[:, k : k + KEYS] = part
        for j in range(0, KEYS, HD):
            top = jnp.maximum(top, part[:, j : j + HD])
    top = jnp.max(top, axis=1, keepdims=True)
    total = jnp.zeros((ROWS, 2 * HD), jnp.float32)
    for k in range(0, CAP, KEYS):
        weights = jnp.exp2((scores[:, k : k + KEYS] - top) * EXP_SCALE)
        total = total + jnp.dot(
            weights.astype(jnp.bfloat16),
            values[k : k + KEYS, :],
            preferred_element_type=jnp.float32,
        )
    sum_ref[...] = total
    top_ref[...] = jnp.broadcast_to(top, (ROWS, HD))


def attend_cached(queries, cache, lengths, start, heads):
    return pl.pallas_call(
        cached_kernel,
        grid=(heads,),
        in_specs=[
            pl.BlockSpec((ROWS, HD), lambda i: (0, i + start)),
            pl.BlockSpec((CAP, 2 * HD), lambda i: (0, 0)),
            pl.BlockSpec((ROWS, 1), lambda i: (0, 0)),
        ],
        out_specs=[
            pl.BlockSpec((ROWS, 2 * HD), lambda i: (0, i)),
            pl.BlockSpec((ROWS, HD), lambda i: (0, i)),
        ],
        out_shape=[
            jax.ShapeDtypeStruct((ROWS, heads * 2 * HD), jnp.float32),
            jax.ShapeDtypeStruct((ROWS, heads * HD), jnp.float32),
        ],
        scratch_shapes=[
            pltpu.VMEM((ROWS, CAP), jnp.float32),
            pltpu.VMEM((CAP, 2 * HD), jnp.bfloat16),
            pltpu.VMEM((ROWS, CAP), jnp.float32),
        ],
        compiler_params=params(),
        name="attend_cached",
    )(queries, cache, lengths)


def join_kernel(info_ref, q_ref, fresh_ref, *refs):
    half = GROUP // 2
    sums, tops, out_ref = refs[0:2], refs[2:4], refs[4]
    row = lax.broadcasted_iota(jnp.int32, (ROWS, ROWS), 0)
    column = lax.broadcasted_iota(jnp.int32, (ROWS, ROWS), 1)
    bias = jnp.where(
        jnp.logical_and(column <= row, jnp.logical_or(info_ref[0] == 0, column == row)),
        0.0,
        NEG_FILL,
    )
    keys = fresh_ref[:, :HD]
    values = jnp.concatenate([fresh_ref[:, HD:], jnp.ones((ROWS, HD), jnp.bfloat16)], axis=1)
    for head in range(GROUP):
        j = head % half
        scores = lax.dot_general(
            q_ref[:, head * HD : (head + 1) * HD],
            keys,
            (((1,), (1,)), ((), ())),
            preferred_element_type=jnp.float32,
        )
        scores = scores + bias
        old_top = tops[head // half][:, j * HD : (j + 1) * HD]
        top = jnp.maximum(old_top, jnp.max(scores, axis=1, keepdims=True))
        keep = jnp.exp2((old_top - top) * EXP_SCALE)
        weights = jnp.exp2((scores - top[:, 0:1]) * EXP_SCALE).astype(jnp.bfloat16)
        new = jnp.dot(weights, values, preferred_element_type=jnp.float32)
        old = sums[head // half][:, 2 * j * HD : 2 * (j + 1) * HD]
        mixed = old[:, :HD] * keep + new[:, :HD]
        total = old[:, HD:] * keep + new[:, HD:]
        out_ref[:, head * HD : (head + 1) * HD] = (mixed / total).astype(jnp.bfloat16)


def join(info, queries, fresh, first, second):
    return pl.pallas_call(
        join_kernel,
        in_specs=[SM] + [VM] * 6,
        out_specs=VM,
        out_shape=jax.ShapeDtypeStruct((ROWS, GROUP * HD), jnp.bfloat16),
        compiler_params=params(),
        name="attend_join",
    )(info, queries, fresh, first[0], second[0], first[1], second[1])


def local(hidden, norm_gain, kv_weight, queries, kv_cache, cache_len, block_table):
    cache = kv_cache[0]
    query_rows = queries[0]
    lengths = cache_len[0]
    role = lax.axis_index("role")
    me = lax.axis_index("pipe")
    info = jnp.stack([role, me]).astype(jnp.int32)
    row_ids = jnp.arange(ROWS, dtype=jnp.int32)

    blocks = cache.reshape(CBLK, BLK, 2 * HD)
    live = (jnp.arange(CAP, dtype=jnp.int32) < lengths[0]).reshape(CBLK, BLK, 1)
    zero = jnp.zeros((), jnp.bfloat16)
    upper = jnp.where(live[:, :8], blocks[:, :8, :HD], zero)
    lower = jnp.where(live[:, 8:], blocks[:, 8:, :HD], zero)
    value = jnp.where(live, blocks[:, :, HD:], zero)
    upper_crossed = cross(upper)
    value_crossed = cross(value)

    tables = lax.all_to_all(
        jnp.broadcast_to(block_table[None], (N_PIPE, NBLK)), "pipe", 0, 0, tiled=True
    )
    index = slot_index(info, tables.T)

    payload = project(hidden[0], norm_gain[None], kv_weight)
    summed = lax.psum_scatter(
        payload.reshape(-1, 2 * HD), "tp", scatter_dimension=0, tiled=True
    )
    positions = lengths + jnp.where(role == 0, row_ids, 0)
    frequency = ROPE_BASE ** (-2.0 * jnp.arange(HD // 2, dtype=jnp.float32) / HD)
    angles = positions.astype(jnp.float32)[:, None] * frequency[None, :]
    cosine = jnp.cos(angles)
    sine = jnp.sin(angles)
    cosine = jnp.concatenate([cosine, cosine], axis=1)
    sine = jnp.concatenate([-sine, sine], axis=1)

    half = GROUP // 2
    column = lengths[:, None]
    first = attend_cached(query_rows, cache, column, 0, half)

    sent_upper = dispatch(info, index, lower, upper_crossed, "dispatch_upper")
    got_upper = pipe_exchange(sent_upper)
    got_lower = cross(got_upper)

    second = attend_cached(query_rows, cache, column, half, half)

    sent_value = dispatch(info, index, value, value_crossed, "dispatch_value")
    got_value = pipe_exchange(sent_value)

    fresh = fresh_rows(summed, cosine, sine)
    fresh_blocks = fresh.reshape(BLK, BLK, 2 * HD)
    moved = cross(fresh_blocks)
    near = [moved] + [
        pipe_move(moved, lambda y, c, core, d=d: (y, (c + d) % 4, core)) for d in (1, 3, 2)
    ]
    far = [pipe_move(x, lambda y, c, core: (1 - y, c, core)) for x in near]
    pieces = near + far
    partner = pipe_move(jnp.stack(pieces), lambda y, c, core: (y, c, 1 - core))

    attention = join(info, query_rows, fresh, first, second)
    received = place(
        info,
        index,
        (upper, lower, value),
        (got_upper, got_lower, got_value),
        fresh_blocks,
        pieces,
        partner,
    )
    return (attention[None], received.reshape(1, SLOTS * BLK, 2 * HD))


def solution(mesh):
    in_specs = (
        P("role", "pipe", "tp"),
        P("tp"),
        P("tp", None),
        P("role", "pipe", "tp"),
        P("role", "pipe", "tp"),
        P("role", "pipe"),
        P("pipe"),
    )
    out_specs = (P("role", "pipe", "tp"), P("role", "pipe", "tp"))
    return jax.shard_map(local, mesh=mesh, in_specs=in_specs, out_specs=out_specs, check_vma=False)
```

time: 307 us -> 168 us (0.55)
  waiting for transfers between devices: 150 us -> 35.1 us
  Pallas kernels: 0 us -> 49.9 us
  matrix products: 33 us -> 0 us
  local copies, waits for them, and re-layouts: 48.2 us -> 21.8 us
  starting transfers between devices: 17 us -> 40.1 us
  blocking collectives: 17.3 us -> 0 us
  other arithmetic: 22.5 us -> 5.28 us
    all_to_all x1 -> x3, waiting for transfers between devices: 63.5 us -> 8.32 us  [the longest x2 6.55 us: pipe_exchange(): return lax.all_to_all(parts, 'pipe', 0, 0, tiled=True).reshape(x.shape)]
    pallas_call x0 -> x9, Pallas kernels: none -> 49.9 us  [the longest x2 22.8 us: attend_cached(): pl.pallas_call(cached_kernel, grid=(heads,), in_specs=[pl.BlockSpec((ROWS...]
    dot_general x10 -> x0, matrix products: 33 us -> none  [the longest x4 13.8 us: one_block(): jnp.einsum('rhgd,shd->rhgs', query_block, key_part, preferred_element_typ...]
    ppermute x1 -> x12, waiting for transfers between devices: 58 us -> 26.8 us  [the longest x8 26.8 us: pipe_move(): return lax.ppermute(x, 'pipe', pairs)]
    reduce_scatter x1, waiting for transfers between devices: 28.3 us -> 0.02 us  [local(): lax.psum_scatter(payload.reshape(-1, 2 * HD), 'tp', scatter_dimension=0,...]
    ppermute x1 -> x12, starting transfers between devices: 6.49 us -> 25.4 us  [the longest x4 16.8 us: cross(): return lax.ppermute(x, ('role', 'pipe'), pairs)]
    psum x1 -> x0, blocking collectives: 17.3 us -> none  [local(): square_sum = lax.psum(jnp.sum(features * features, axis=1), 'tp')]
    unnamed x11 -> x63, local copies, waits for them, and re-layouts: 4.56 us -> 18.9 us
  transfers between devices with their start and end apart: 3 -> 16, of which waited for: 3 -> 5; matrix products, arithmetic and copies ran while one was open for 15% -> 8% of each run, Pallas kernels for 0% -> 23%
where the time goes in v1:
time: 168 us; the launch traced here: 167 us
  Pallas kernels  49.9 us (30%)
  starting transfers between devices  40.1 us (24%)
  waiting for transfers between devices  35.1 us (21%)
  local copies, waits for them, and re-layouts  21.8 us (13%)
  between operations  14.4 us (9%)
  other arithmetic  5.28 us (3%)
    ppermute x8, waiting for transfers between devices, pipe_move(): return lax.ppermute(x, 'pipe', pairs)  26.8 us
    pallas_call x2, Pallas kernels, attend_cached(): pl.pallas_call(cached_kernel, grid=(heads,), in_specs=[pl.BlockSpec((ROWS...  22.8 us
    unnamed x63, local copies, waits for them, and re-layouts  18.9 us
    ppermute x4, starting transfers between devices, cross(): return lax.ppermute(x, ('role', 'pipe'), pairs)  16.8 us
    all_to_all x2, starting transfers between devices, pipe_exchange(): return lax.all_to_all(parts, 'pipe', 0, 0, tiled=True).reshape(x.shape)  9.39 us
    ppermute x8, starting transfers between devices, pipe_move(): return lax.ppermute(x, 'pipe', pairs)  8.59 us
    pallas_call x1, Pallas kernels, place(): pl.pallas_call(place_kernel, in_specs=[SM, SM] + [ANY] * 16, out_specs=VM...  8.25 us
    pallas_call x1, Pallas kernels, slot_index(): pl.pallas_call(index_kernel, in_specs=[SM, VM], out_specs=VM, out_shape=j...  7.48 us
  transfers between devices with their start and end apart: 16, of which 5 were waited for; matrix products, arithmetic and copies ran while one was open for 8% of the time, Pallas kernels for 23%

profile of v1, /device:TPU:1, one launch (start us, length us, event | category | flops | bytes accessed | tf_op | source)
XLA Modules:
  0.0 166.6 jit_solution(831903552931488708)
XLA Ops:
  7.2 0.0 reduce-scatter.2.cloned.1.call-start
  7.2 2.2 %copy-done.8 = bf16[1024,2048]{1,0:T(8,128)(2,1)S(1)} copy-done((bf16[1024,2048]{1,0:T(8,128)(2,1)S(1)}, bf16[1024,2048]{1,0:T(8,128)(2,1)}, u32[]{:S(2)}) %copy-start.8) | copy-done | bytes 4194328
  9.4 1.0 copy-done.23
  10.4 0.7 copy-done.25
  11.1 3.4 %project.1 = bf16[8,272,256]{2,1,0:T(8,128)(2,1)S(1)} custom-call(bf16[256,1024]{1,0:T(8,128)(2,1)S(1)} %bitcast.54, f32[1,1024]{1,0:T(1,128)S(1)} %bitcast.55, bf16[1024,2048]{1,0:T(8,128)(2,1)S(1)} %copy-done.8), custom_call_target="tpu_custom_call" | custom-call | tf_op jit(solution)/shard_map/project/pallas_call | solution.py:83
  14.6 1.0 copy-done.6
  15.6 0.6 slice.19
  16.2 0.7 add_compare_fusion.1
  16.9 0.1 slice_bitcast_fusion
  17.0 2.2 %slice_select_fusion.1 = (bf16[256,8,128]{2,1,0:T(8,128)(2,1)}, bf16[256,8,128]{2,1,0:T(8,128)(2,1)}) fusion(bf16[256,16,256]{2,1,0:T(8,128)(2,1)S(1)} %bitcast.41, pred[256,8]{1,0:T(8,128)(4,1)S(1)} %get-tuple-element.12, pred[256,8]{1,0:T(8,128)(4,1)S(1)} %get-tuple-element.13), kind=kLoop, calls=%fused_computation.1 | loop fusion | flops 524288 | bytes 2101248 | tf_op jit(solution)/shard_map/jit(_where)/select_n | solution.py:435
  19.2 6.3 %collective-permute-start = (bf16[256,8,128]{2,1,0:T(8,128)(2,1)}, bf16[256,8,128]{2,1,0:T(8,128)(2,1)}, u32[]{:S(2)}, u32[]{:S(2)}) collective-permute-start(bf16[256,8,128]{2,1,0:T(8,128)(2,1)} %get-tuple-element.11.refs_0_), channel_id=1, source_target_pairs={{0,192},{8,200},{16,208},{24,216},{32,224},{40,232},{48,240},{56,2... | collective-permute-start | bytes 1572872 | tf_op jit(solution)/shard_map/ppermute | solution.py:40
  25.5 0.6 broadcast_in_dim.55
  26.1 5.3 %all-to-all-start = ((s32[16,1,272]{2,1,0:T(1,128)}), s32[16,1,272]{2,1,0:T(1,128)S(1)}, u32[]{:S(2)}, u32[]{:S(2)}) async-start(s32[16,1,272]{2,1,0:T(1,128)} %broadcast_in_dim.55), calls=%async_computation.1 | async-start | bytes 49152 | tf_op jit(solution)/shard_map/all_to_all | solution.py:440
  31.4 0.7 add_compare_fusion
  32.0 1.0 slice_select_fusion.own_ref.refs_2_
  33.0 2.3 %collective-permute-start.2 = (bf16[256,16,128]{2,1,0:T(8,128)(2,1)S(1)}, bf16[256,16,128]{2,1,0:T(8,128)(2,1)}, u32[]{:S(2)}, u32[]{:S(2)}) collective-permute-start(bf16[256,16,128]{2,1,0:T(8,128)(2,1)S(1)} %slice_select_fusion.own_ref.refs_2_), channel_id=1, source_target_pairs={{0,192},{8,200},{16,208},{24,216},{32,224},{40,232},{48,240},{56,2... | collective-permute-start | bytes 3145736 | tf_op jit(solution)/shard_map/ppermute | solution.py:40
  35.3 0.1 pad_add_fusion.info_ref
  35.4 1.8 %all-to-all-done = s32[16,1,272]{2,1,0:T(1,128)S(1)} async-done(((s32[16,1,272]{2,1,0:T(1,128)}), s32[16,1,272]{2,1,0:T(1,128)S(1)}, u32[]{:S(2)}, u32[]{:S(2)}) %all-to-all-start) | async-done | bytes 17440 | tf_op jit(solution)/shard_map/all_to_all | solution.py:440
  37.1 0.1 copy.13
  37.3 7.5 %slot_index.1.index_ref = s32[4,544]{1,0:T(4,128)S(1)} custom-call(s32[2]{0:T(128)S(1)} %pad_add_fusion.info_ref, s32[272,16]{1,0:T(8,128)S(1)} %bitcast.53), custom_call_target="tpu_custom_call" | custom-call | tf_op jit(solution)/shard_map/slot_index/pallas_call | solution.py:181
  44.8 1.0 copy-done.4
  45.8 2.0 %dispatch_upper.1 = bf16[544,8,128]{2,1,0:T(8,128)(2,1)S(1)} custom-call(s32[2]{0:T(128)S(1)} %pad_add_fusion.info_ref, s32[4,544]{1,0:T(4,128)S(1)} %slot_index.1.index_ref, bf16[256,8,128]{2,1,0:T(8,128)(2,1)S(1)} %copy-done.4, bf16[256,8,128]{2,1,0:T(8,128)(2,1)} %collective-permute-done.crossed_ref), custom_call_target="tpu_custom_call" | custom-call | tf_op jit(solution)/shard_map/dispatch_upper/pallas_call | solution.py:215
  47.9 1.0 copy-done.7
  48.9 4.5 %all-to-all-start.1 = ((bf16[16,34,8,128]{3,2,1,0:T(8,128)(2,1)}), bf16[16,34,8,128]{3,2,1,0:T(8,128)(2,1)}, u32[]{:S(2)}, u32[]{:S(2)}) async-start(bf16[16,34,8,128]{3,2,1,0:T(8,128)(2,1)} %bitcast.50), calls=%async_computation.2 | async-start | bytes 2228224 | tf_op jit(solution)/shard_map/all_to_all | solution.py:55
  53.4 0.5 fusion
  54.0 0.1 pad_maximum_fusion
  54.1 0.0 reduce-scatter.2.cloned.1.call-done.sum_ref
  54.1 0.9 copy-done.24
  55.0 0.2 fresh.1.fresh_ref
  55.2 4.9 %collective-permute-start.3 = (bf16[16,16,256]{2,1,0:T(8,128)(2,1)S(1)}, bf16[16,16,256]{2,1,0:T(8,128)(2,1)S(1)}, u32[]{:S(2)}, u32[]{:S(2)}) collective-permute-start(bf16[16,16,256]{2,1,0:T(8,128)(2,1)S(1)} %bitcast.51), channel_id=1, source_target_pairs={{0,192},{8,200},{16,208},{24,216},{32,224},{40,232},{48,240},{56,2... | collective-permute-start | bytes 393224 | tf_op jit(solution)/shard_map/ppermute | solution.py:40
  60.1 2.1 %dispatch_value.1 = bf16[544,16,128]{2,1,0:T(8,128)(2,1)S(1)} custom-call(s32[2]{0:T(128)S(1)} %pad_add_fusion.info_ref, s32[4,544]{1,0:T(4,128)S(1)} %slot_index.1.index_ref, bf16[256,16,128]{2,1,0:T(8,128)(2,1)S(1)} %slice_select_fusion.own_ref.refs_2_, bf16[256,16,128]{2,1,0:T(8,128)(2,1)} %collective-permute-done.2.crossed_ref), custom_call_target="tpu_custom_call" | custom-call | tf_op jit(solution)/shard_map/dispatch_value/pallas_call | solution.py:215
  62.2 1.4 copy-done.1
  63.6 6.5 %all-to-all-done.1 = bf16[16,34,8,128]{3,2,1,0:T(8,128)(2,1)} async-done(((bf16[16,34,8,128]{3,2,1,0:T(8,128)(2,1)}), bf16[16,34,8,128]{3,2,1,0:T(8,128)(2,1)}, u32[]{:S(2)}, u32[]{:S(2)}) %all-to-all-start.1) | async-done | bytes 1114144 | tf_op jit(solution)/shard_map/all_to_all | solution.py:55
  70.1 4.9 %all-to-all-start.2 = ((bf16[16,34,16,128]{3,2,1,0:T(8,128)(2,1)}), bf16[16,34,16,128]{3,2,1,0:T(8,128)(2,1)}, u32[]{:S(2)}, u32[]{:S(2)}) async-start(bf16[16,34,16,128]{3,2,1,0:T(8,128)(2,1)} %bitcast.45), calls=%async_computation.3 | async-start | bytes 4456448 | tf_op jit(solution)/shard_map/all_to_all | solution.py:55
  75.0 3.4 %collective-permute-start.1 = (bf16[544,8,128]{2,1,0:T(8,128)(2,1)}, bf16[544,8,128]{2,1,0:T(8,128)(2,1)}, u32[]{:S(2)}, u32[]{:S(2)}) collective-permute-start(bf16[544,8,128]{2,1,0:T(8,128)(2,1)} %bitcast.17.refs_3_), channel_id=1, source_target_pairs={{0,192},{8,200},{16,208},{24,216},{32,224},{40,232},{48,240},{56,2... | collective-permute-start | bytes 3342344 | tf_op jit(solution)/shard_map/ppermute | solution.py:40
  78.4 1.2 collective-permute-start.4
  79.6 1.5 collective-permute-start.5
  81.1 1.5 collective-permute-start.6
  82.6 0.4 collective-permute-start.7
  82.9 0.7 bitcast_dynamic-update-slice_fusion.7
  83.6 23.4 %collective-permute-done.4.refs_8_ = bf16[16,16,256]{2,1,0:T(8,128)(2,1)S(1)} collective-permute-done((bf16[16,16,256]{2,1,0:T(8,128)(2,1)S(1)}, bf16[16,16,256]{2,1,0:T(8,128)(2,1)S(1)}, u32[]{:S(2)}, u32[]{:S(2)}) %collective-permute-start.4) | collective-permute-done | bytes 131104 | tf_op jit(solution)/shard_map/ppermute | solution.py:50
  107.0 1.0 collective-permute-start.8
  108.0 0.7 bitcast_dynamic-update-slice_fusion.6
  108.6 0.5 collective-permute-start.9
  109.1 0.7 bitcast_dynamic-update-slice_fusion.5
  109.8 1.0 collective-permute-start.10
  110.8 0.7 bitcast_dynamic-update-slice_fusion.4
  111.4 0.7 bitcast_dynamic-update-slice_fusion.3
  112.2 0.7 bitcast_dynamic-update-slice_fusion.2
  112.9 1.2 collective-permute-done.9.refs_13_
  114.1 0.7 bitcast_dynamic-update-slice_fusion.1
  114.8 2.1 %collective-permute-done.10.refs_14_ = bf16[16,16,256]{2,1,0:T(8,128)(2,1)S(1)} collective-permute-done((bf16[16,16,256]{2,1,0:T(8,128)(2,1)S(1)}, bf16[16,16,256]{2,1,0:T(8,128)(2,1)S(1)}, u32[]{:S(2)}, u32[]{:S(2)}) %collective-permute-start.10) | collective-permute-done | bytes 131104 | tf_op jit(solution)/shard_map/ppermute | solution.py:50
  117.0 0.7 bitcast_dynamic-update-slice_fusion
  117.7 1.6 collective-permute-start.11
  119.3 0.8 copy.11.len_ref
  120.1 1.0 copy-done.2
  121.2 11.4 %attend_cached.2 = (f32[256,1024]{1,0:T(8,128)S(1)}, f32[256,512]{1,0:T(8,128)S(1)}) custom-call(bf16[256,1024]{1,0:T(8,128)(2,1)S(1)} %bitcast.46, bf16[4096,256]{1,0:T(8,128)(2,1)S(1)} %bitcast.43, s32[256,1]{1,0:T(8,128)S(1)} %copy.11.len_ref), custom_call_target="tpu_custom_call" | custom-call | tf_op jit(solution)/shard_map/attend_cached/pallas_call | solution.py:353
  132.6 11.4 %attend_cached.3 = (f32[256,1024]{1,0:T(8,128)S(1)}, f32[256,512]{1,0:T(8,128)S(1)}) custom-call(bf16[256,1024]{1,0:T(8,128)(2,1)S(1)} %bitcast.47, bf16[4096,256]{1,0:T(8,128)(2,1)S(1)} %bitcast.44, s32[256,1]{1,0:T(8,128)S(1)} %copy.11.len_ref), custom_call_target="tpu_custom_call" | custom-call | tf_op jit(solution)/shard_map/attend_cached/pallas_call | solution.py:353
  144.1 3.6 %attend_join.1 = bf16[256,1024]{1,0:T(8,128)(2,1)} custom-call(s32[2]{0:T(128)S(1)} %pad_add_fusion.info_ref, bf16[256,1024]{1,0:T(8,128)(2,1)S(1)} %bitcast.48, bf16[256,256]{1,0:T(8,128)(2,1)S(1)} %fresh.1.fresh_ref, f32[256,1024]{1,0:T(8,128)S(1)} %get-tuple-element.6.refs_0_, f32[256,1024]{1,0:T(8,128)S(1)} %get-tuple-element.7.refs_1_, ...), custom_call_target="tpu_custom_call" | custom-call | tf_op jit(solution)/shard_map/attend_join/pallas_call | solution.py:412
  147.7 1.0 copy-done.5
  148.7 0.9 copy-done.18
  149.6 0.9 copy-done.20
  150.6 0.9 copy-done.22
  151.5 8.2 %place.1 = bf16[544,16,256]{2,1,0:T(8,128)(2,1)} custom-call(s32[2]{0:T(128)S(1)} %pad_add_fusion.info_ref, s32[4,544]{1,0:T(4,128)S(1)} %slot_index.1.index_ref, bf16[256,8,128]{2,1,0:T(8,128)(2,1)} %get-tuple-element.11.refs_0_, bf16[256,8,128]{2,1,0:T(8,128)(2,1)S(1)} %copy-done.5, bf16[256,16,128]{2,1,0:T(8,128)(2,1)S(1)} %slice_select_fusion.own_ref.refs_2_, ...), custom_call_target="tpu_custom_call" | custom-call | tf_op jit(solution)/shard_map/place/pallas_call | solution.py:296
  (56 shorter events, 0.2 us)
Async XLA Ops:
  7.2 47.0 %reduce-scatter.2.cloned.1.call-start = ((), (), s32[]{:S(2)}) async-start(), calls=%async_computation.4 | async-start | bytes 1253376 | tf_op jit(solution)/shard_map/reduce_scatter | solution.py:446
  7.2 2.2 %copy-start.8 = (bf16[1024,2048]{1,0:T(8,128)(2,1)S(1)}, bf16[1024,2048]{1,0:T(8,128)(2,1)}, u32[]{:S(2)}) copy-start(bf16[1024,2048]{1,0:T(8,128)(2,1)} %w_ref.1) | copy-start | bytes 12582916
  9.4 1.0 copy-start.23
  10.4 0.7 copy-start.25
  11.1 4.5 %copy-start.26 = (s32[1,256]{1,0:T(1,128)S(1)}, s32[1,256]{1,0:T(1,128)}, u32[]{:S(2)}) copy-start(s32[1,256]{1,0:T(1,128)} %param.12) | copy-start | bytes 3076
  11.1 5.8 %copy-start = (bf16[1,4096,256]{2,1,0:T(8,128)(2,1)S(1)}, bf16[1,4096,256]{2,1,0:T(8,128)(2,1)}, u32[]{:S(2)}) copy-start(bf16[1,4096,256]{2,1,0:T(8,128)(2,1)} %param.11) | copy-start | bytes 6291460
  14.6 1.0 copy-start.6
  15.6 9.9 %copy-start.27 = (s32[272]{0:T(512)S(1)}, s32[272]{0:T(512)}, u32[]{:S(2)}) copy-start(s32[272]{0:T(512)} %param.13) | copy-start | bytes 3268
  19.2 25.5 %collective-permute-start = (bf16[256,8,128]{2,1,0:T(8,128)(2,1)}, bf16[256,8,128]{2,1,0:T(8,128)(2,1)}, u32[]{:S(2)}, u32[]{:S(2)}) collective-permute-start(bf16[256,8,128]{2,1,0:T(8,128)(2,1)} %get-tuple-element.11.refs_0_), channel_id=1, source_target_pairs={{0,192},{8,200},{16,208},{24,216},{32,224},{40,232},{48,240},{56,2... | collective-permute-start | bytes 1572872 | tf_op jit(solution)/shard_map/ppermute | solution.py:40
  26.1 11.1 %all-to-all-start = ((s32[16,1,272]{2,1,0:T(1,128)}), s32[16,1,272]{2,1,0:T(1,128)S(1)}, u32[]{:S(2)}, u32[]{:S(2)}) async-start(s32[16,1,272]{2,1,0:T(1,128)} %broadcast_in_dim.55), calls=%async_computation.1 | async-start | bytes 49152 | tf_op jit(solution)/shard_map/all_to_all | solution.py:440
  33.0 27.1 %collective-permute-start.2 = (bf16[256,16,128]{2,1,0:T(8,128)(2,1)S(1)}, bf16[256,16,128]{2,1,0:T(8,128)(2,1)}, u32[]{:S(2)}, u32[]{:S(2)}) collective-permute-start(bf16[256,16,128]{2,1,0:T(8,128)(2,1)S(1)} %slice_select_fusion.own_ref.refs_2_), channel_id=1, source_target_pairs={{0,192},{8,200},{16,208},{24,216},{32,224},{40,232},{48,240},{56,2... | collective-permute-start | bytes 3145736 | tf_op jit(solution)/shard_map/ppermute | solution.py:40
  44.8 1.0 copy-start.4
  47.9 1.0 copy-start.7
  48.9 21.3 %all-to-all-start.1 = ((bf16[16,34,8,128]{3,2,1,0:T(8,128)(2,1)}), bf16[16,34,8,128]{3,2,1,0:T(8,128)(2,1)}, u32[]{:S(2)}, u32[]{:S(2)}) async-start(bf16[16,34,8,128]{3,2,1,0:T(8,128)(2,1)} %bitcast.50), calls=%async_computation.2 | async-start | bytes 2228224 | tf_op jit(solution)/shard_map/all_to_all | solution.py:55
  54.1 0.9 copy-start.24
  55.2 23.1 %collective-permute-start.3 = (bf16[16,16,256]{2,1,0:T(8,128)(2,1)S(1)}, bf16[16,16,256]{2,1,0:T(8,128)(2,1)S(1)}, u32[]{:S(2)}, u32[]{:S(2)}) collective-permute-start(bf16[16,16,256]{2,1,0:T(8,128)(2,1)S(1)} %bitcast.51), channel_id=1, source_target_pairs={{0,192},{8,200},{16,208},{24,216},{32,224},{40,232},{48,240},{56,2... | collective-permute-start | bytes 393224 | tf_op jit(solution)/shard_map/ppermute | solution.py:40
  62.2 1.4 copy-start.1
  70.1 77.5 %all-to-all-start.2 = ((bf16[16,34,16,128]{3,2,1,0:T(8,128)(2,1)}), bf16[16,34,16,128]{3,2,1,0:T(8,128)(2,1)}, u32[]{:S(2)}, u32[]{:S(2)}) async-start(bf16[16,34,16,128]{3,2,1,0:T(8,128)(2,1)} %bitcast.45), calls=%async_computation.3 | async-start | bytes 4456448 | tf_op jit(solution)/shard_map/all_to_all | solution.py:55
  75.0 72.6 %collective-permute-start.1 = (bf16[544,8,128]{2,1,0:T(8,128)(2,1)}, bf16[544,8,128]{2,1,0:T(8,128)(2,1)}, u32[]{:S(2)}, u32[]{:S(2)}) collective-permute-start(bf16[544,8,128]{2,1,0:T(8,128)(2,1)} %bitcast.17.refs_3_), channel_id=1, source_target_pairs={{0,192},{8,200},{16,208},{24,216},{32,224},{40,232},{48,240},{56,2... | collective-permute-start | bytes 3342344 | tf_op jit(solution)/shard_map/ppermute | solution.py:40
  78.4 28.6 %collective-permute-start.4 = (bf16[16,16,256]{2,1,0:T(8,128)(2,1)S(1)}, bf16[16,16,256]{2,1,0:T(8,128)(2,1)S(1)}, u32[]{:S(2)}, u32[]{:S(2)}) collective-permute-start(bf16[16,16,256]{2,1,0:T(8,128)(2,1)S(1)} %collective-permute-done.3.refs_7_), channel_id=1, source_target_pairs={{0,16},{8,24},{16,32},{24,40},{32,48},{40,56},{48,0},{56,8},{64,80... | collective-permute-start | bytes 393224 | tf_op jit(solution)/shard_map/ppermute | solution.py:50
  79.6 29.0 %collective-permute-start.5 = (bf16[16,16,256]{2,1,0:T(8,128)(2,1)S(1)}, bf16[16,16,256]{2,1,0:T(8,128)(2,1)S(1)}, u32[]{:S(2)}, u32[]{:S(2)}) collective-permute-start(bf16[16,16,256]{2,1,0:T(8,128)(2,1)S(1)} %collective-permute-done.3.refs_7_), channel_id=1, source_target_pairs={{0,48},{8,56},{16,0},{24,8},{32,16},{40,24},{48,32},{56,40},{64,11... | collective-permute-start | bytes 393224 | tf_op jit(solution)/shard_map/ppermute | solution.py:50
  81.1 28.7 %collective-permute-start.6 = (bf16[16,16,256]{2,1,0:T(8,128)(2,1)S(1)}, bf16[16,16,256]{2,1,0:T(8,128)(2,1)S(1)}, u32[]{:S(2)}, u32[]{:S(2)}) collective-permute-start(bf16[16,16,256]{2,1,0:T(8,128)(2,1)S(1)} %collective-permute-done.3.refs_7_), channel_id=1, source_target_pairs={{0,32},{8,40},{16,48},{24,56},{32,0},{40,8},{48,16},{56,24},{64,96... | collective-permute-start | bytes 393224 | tf_op jit(solution)/shard_map/ppermute | solution.py:50
  82.6 28.9 %collective-permute-start.7 = (bf16[16,16,256]{2,1,0:T(8,128)(2,1)S(1)}, bf16[16,16,256]{2,1,0:T(8,128)(2,1)S(1)}, u32[]{:S(2)}, u32[]{:S(2)}) collective-permute-start(bf16[16,16,256]{2,1,0:T(8,128)(2,1)S(1)} %collective-permute-done.3.refs_7_), channel_id=1, source_target_pairs={{0,64},{8,72},{16,80},{24,88},{32,96},{40,104},{48,112},{56,120},{... | collective-permute-start | bytes 393224 | tf_op jit(solution)/shard_map/ppermute | solution.py:50
  107.0 12.3 %copy-start.9 = (bf16[16,16,256]{2,1,0:T(8,128)(2,1)}, bf16[16,16,256]{2,1,0:T(8,128)(2,1)S(1)}, u32[]{:S(2)}) copy-start(bf16[16,16,256]{2,1,0:T(8,128)(2,1)S(1)} %collective-permute-done.4.refs_8_) | copy-start | bytes 393220
  107.0 5.2 %collective-permute-start.8 = (bf16[16,16,256]{2,1,0:T(8,128)(2,1)S(1)}, bf16[16,16,256]{2,1,0:T(8,128)(2,1)S(1)}, u32[]{:S(2)}, u32[]{:S(2)}) collective-permute-start(bf16[16,16,256]{2,1,0:T(8,128)(2,1)S(1)} %collective-permute-done.4.refs_8_), channel_id=1, source_target_pairs={{0,64},{8,72},{16,80},{24,88},{32,96},{40,104},{48,112},{56,120},{... | collective-permute-start | bytes 393224 | tf_op jit(solution)/shard_map/ppermute | solution.py:50
  108.6 10.6 %copy-start.11 = (bf16[16,16,256]{2,1,0:T(8,128)(2,1)}, bf16[16,16,256]{2,1,0:T(8,128)(2,1)S(1)}, u32[]{:S(2)}) copy-start(bf16[16,16,256]{2,1,0:T(8,128)(2,1)S(1)} %collective-permute-done.5.refs_9_) | copy-start | bytes 393220
  108.6 5.5 %collective-permute-start.9 = (bf16[16,16,256]{2,1,0:T(8,128)(2,1)S(1)}, bf16[16,16,256]{2,1,0:T(8,128)(2,1)S(1)}, u32[]{:S(2)}, u32[]{:S(2)}) collective-permute-start(bf16[16,16,256]{2,1,0:T(8,128)(2,1)S(1)} %collective-permute-done.5.refs_9_), channel_id=1, source_target_pairs={{0,64},{8,72},{16,80},{24,88},{32,96},{40,104},{48,112},{56,120},{... | collective-permute-start | bytes 393224 | tf_op jit(solution)/shard_map/ppermute | solution.py:50
  109.8 9.5 %copy-start.13 = (bf16[16,16,256]{2,1,0:T(8,128)(2,1)}, bf16[16,16,256]{2,1,0:T(8,128)(2,1)S(1)}, u32[]{:S(2)}) copy-start(bf16[16,16,256]{2,1,0:T(8,128)(2,1)S(1)} %collective-permute-done.6.refs_10_) | copy-start | bytes 393220
  109.8 7.1 %collective-permute-start.10 = (bf16[16,16,256]{2,1,0:T(8,128)(2,1)S(1)}, bf16[16,16,256]{2,1,0:T(8,128)(2,1)S(1)}, u32[]{:S(2)}, u32[]{:S(2)}) collective-permute-start(bf16[16,16,256]{2,1,0:T(8,128)(2,1)S(1)} %collective-permute-done.6.refs_10_), channel_id=1, source_target_pairs={{0,64},{8,72},{16,80},{24,88},{32,96},{40,104},{48,112},{56,120},{... | collective-permute-start | bytes 393224 | tf_op jit(solution)/shard_map/ppermute | solution.py:50
  111.4 7.8 %copy-start.15 = (bf16[16,16,256]{2,1,0:T(8,128)(2,1)}, bf16[16,16,256]{2,1,0:T(8,128)(2,1)S(1)}, u32[]{:S(2)}) copy-start(bf16[16,16,256]{2,1,0:T(8,128)(2,1)S(1)} %collective-permute-done.7.refs_11_) | copy-start | bytes 393220
  112.2 7.1 %copy-start.17 = (bf16[16,16,256]{2,1,0:T(8,128)(2,1)}, bf16[16,16,256]{2,1,0:T(8,128)(2,1)S(1)}, u32[]{:S(2)}) copy-start(bf16[16,16,256]{2,1,0:T(8,128)(2,1)S(1)} %collective-permute-done.8.refs_12_) | copy-start | bytes 393220
  114.1 5.1 %copy-start.19 = (bf16[16,16,256]{2,1,0:T(8,128)(2,1)}, bf16[16,16,256]{2,1,0:T(8,128)(2,1)S(1)}, u32[]{:S(2)}) copy-start(bf16[16,16,256]{2,1,0:T(8,128)(2,1)S(1)} %collective-permute-done.9.refs_13_) | copy-start | bytes 393220
  117.0 2.3 %copy-start.21 = (bf16[16,16,256]{2,1,0:T(8,128)(2,1)}, bf16[16,16,256]{2,1,0:T(8,128)(2,1)S(1)}, u32[]{:S(2)}) copy-start(bf16[16,16,256]{2,1,0:T(8,128)(2,1)S(1)} %collective-permute-done.10.refs_14_) | copy-start | bytes 393220
  117.7 30.0 %collective-permute-start.11 = (bf16[8,16,16,256]{3,2,1,0:T(8,128)(2,1)}, bf16[8,16,16,256]{3,2,1,0:T(8,128)(2,1)}, u32[]{:S(2)}, u32[]{:S(2)}) collective-permute-start(bf16[8,16,16,256]{3,2,1,0:T(8,128)(2,1)} %bitcast_dynamic-update-slice_fusion), channel_id=1, source_target_pairs={{0,8},{8,0},{16,24},{24,16},{32,40},{40,32},{48,56},{56,48},{64,72... | collective-permute-start | bytes 3145736 | tf_op jit(solution)/shard_map/ppermute | solution.py:50
  120.1 1.0 copy-start.2
  121.2 22.8 %copy-start.3 = (bf16[1,256,1024]{2,1,0:T(8,128)(2,1)S(1)}, bf16[1,256,1024]{2,1,0:T(8,128)(2,1)}, u32[]{:S(2)}) copy-start(bf16[1,256,1024]{2,1,0:T(8,128)(2,1)} %param.10) | copy-start | bytes 1572868
  144.0 3.6 %copy-start.10 = (bf16[16,16,256]{2,1,0:T(8,128)(2,1)S(1)}, bf16[16,16,256]{2,1,0:T(8,128)(2,1)}, u32[]{:S(2)}) copy-start(bf16[16,16,256]{2,1,0:T(8,128)(2,1)} %copy-done.9) | copy-start | bytes 393220
  144.0 3.6 %copy-start.12 = (bf16[16,16,256]{2,1,0:T(8,128)(2,1)S(1)}, bf16[16,16,256]{2,1,0:T(8,128)(2,1)}, u32[]{:S(2)}) copy-start(bf16[16,16,256]{2,1,0:T(8,128)(2,1)} %copy-done.11) | copy-start | bytes 393220
  144.0 3.6 %copy-start.14 = (bf16[16,16,256]{2,1,0:T(8,128)(2,1)S(1)}, bf16[16,16,256]{2,1,0:T(8,128)(2,1)}, u32[]{:S(2)}) copy-start(bf16[16,16,256]{2,1,0:T(8,128)(2,1)} %copy-done.13) | copy-start | bytes 393220
  144.1 3.6 %copy-start.16 = (bf16[16,16,256]{2,1,0:T(8,128)(2,1)S(1)}, bf16[16,16,256]{2,1,0:T(8,128)(2,1)}, u32[]{:S(2)}) copy-start(bf16[16,16,256]{2,1,0:T(8,128)(2,1)} %copy-done.15) | copy-start | bytes 393220
  147.7 1.0 copy-start.5
  148.7 0.9 copy-start.18
  149.6 0.9 copy-start.20
  150.6 0.9 copy-start.22
Sparse Core Ops, SparseCore 0:
  15.7 38.1 reduce-scatter.1

commit v2 on v0

v2 whole, which is shorter than its diff:
```python
import functools

import jax
import jax.numpy as jnp
from jax import lax
from jax.experimental import pallas as pl
from jax.experimental.pallas import tpu as pltpu
from jax.sharding import PartitionSpec as P

D = 8192
QH = 64
KVH = 8
HD = 128
ROWS = 256
CAP = 4096
BLK = 16
NBLK = 272
CAPB = 34
N_PIPE = 16
CBLK = CAP // BLK
SLOTS = N_PIPE * CAPB
DIGITS = 16
GROUP = QH // KVH

ROPE_BASE = 500000.0
EPSILON = 1e-05
NEG_FILL = -1e30
EXP_SCALE = HD**-0.5 * 1.4426950408889634
MIB = 1024 * 1024

VM = pl.BlockSpec(memory_space=pltpu.VMEM)
SM = pl.BlockSpec(memory_space=pltpu.SMEM)
HB = pl.BlockSpec(memory_space=pltpu.HBM)


class Chain:
    def __init__(self):
        self.token = None

    def __call__(self, kernel, operands, specs, out_specs, out_shape, scratch=(), name=None, mib=16, aliases=None):
        count = len(operands)
        outs = len(out_shape)
        extra = 0 if self.token is None else 1
        token = jax.ShapeDtypeStruct((8, 128), jnp.float32)

        def body(*refs):
            given, rest = refs[:count], refs[count + extra :]
            rest[outs][...] = jnp.zeros((8, 128), jnp.float32)
            kernel(*given, *rest[:outs], *rest[outs + 1 :])

        tokens = () if self.token is None else (self.token,)
        results = pl.pallas_call(
            body,
            in_specs=list(specs) + [VM] * extra,
            out_specs=list(out_specs) + [VM],
            out_shape=list(out_shape) + [token],
            scratch_shapes=list(scratch),
            compiler_params=pltpu.CompilerParams(vmem_limit_bytes=mib * MIB),
            cost_estimate=pl.CostEstimate(flops=1, bytes_accessed=1, transcendentals=0),
            input_output_aliases=aliases or {},
            name=name,
        )(*operands, *tokens)
        self.token = results[-1]
        return results[:-1]


def like(shape, dtype=jnp.bfloat16):
    return jax.ShapeDtypeStruct(shape, dtype)


def run_copies(copies):
    for copy in copies:
        copy.start()
    for copy in copies:
        copy.wait()


def fenced(work, operands):
    shapes = jax.eval_shape(work, operands)

    def idle(_):
        return jax.tree.map(lambda x: jnp.zeros(x.shape, x.dtype), shapes)

    return lax.cond(lax.axis_index("role") < 2, work, idle, operands)


def cross(x, turn=8):
    pairs = [(p, N_PIPE + (p ^ turn)) for p in range(N_PIPE)]
    return lax.ppermute(x, ("role", "pipe"), pairs)


def pipe_move(x, move):
    pairs = []
    for y in range(2):
        for c in range(4):
            for core in range(2):
                target = move(y, c, core)
                if target is not None:
                    ny, nc, ncore = target
                    pairs.append(((y * 4 + c) * 2 + core, (ny * 4 + nc) * 2 + ncore))
    return lax.ppermute(x, "pipe", pairs)


def spread(x, k):
    def move(y, c, core):
        if core == 1:
            return 1 - y, (c + k) % 4, 1
        return (y, (c + k + 1) % 4, 0) if k < 3 else None

    return pipe_move(x, move)


def pipe_exchange(x):
    parts = x.reshape((N_PIPE, x.shape[0] // N_PIPE) + x.shape[1:])
    return lax.all_to_all(parts, "pipe", 0, 0, tiled=True).reshape(x.shape)


DISTANCES = (4, 3, 5, 2, 6, 1, 7, 0)


def project_kernel(h_ref, gain_ref, w_ref, *refs):
    high_ref, low_ref = refs[0:2]
    out_refs = refs[2:9]
    weight, sems = refs[9:]
    shard = lax.axis_index("tp")
    copies = []
    for k, distance in enumerate(DISTANCES):
        head = lax.rem(shard + distance, len(DISTANCES))
        columns = pl.ds(pl.multiple_of(head * 2 * HD, 2 * HD), 2 * HD)
        copies.append(
            pltpu.make_async_copy(w_ref.at[:, columns], weight.at[k], sems.at[k])
        )
        copies[-1].start()
    h = h_ref[...].astype(jnp.float32)
    scaled = (h * gain_ref[...]).astype(jnp.bfloat16)
    total = jnp.sum(h * h, axis=1, keepdims=True)
    across = jnp.transpose(jnp.broadcast_to(total, (ROWS, 128)))
    rest = across[0:1, :] * (2.0**-27)
    rows = []
    for _ in range(DIGITS):
        rest = rest * 32.0
        digit = jnp.floor(rest)
        rest = rest - digit
        rows.append(digit)
    digits = jnp.concatenate(rows, axis=0).astype(jnp.bfloat16)
    for k in range(len(DISTANCES)):
        copies[k].wait()
        piece = jnp.dot(scaled, weight[k], preferred_element_type=jnp.float32).astype(
            jnp.bfloat16
        )
        if k == 0:
            high_ref[...] = piece[:HD]
            low_ref[: ROWS - HD, :] = piece[HD:]
            low_ref[ROWS - HD :, :] = digits
        else:
            out_refs[k - 1][:ROWS, :] = piece
            out_refs[k - 1][ROWS:, :] = digits


def project(chain, hidden, gain, weight):
    feats = hidden.shape[1]
    count = len(DISTANCES)
    return chain(
        project_kernel,
        (hidden, gain, weight),
        [VM, VM, HB],
        [VM] * (count + 1),
        [like((HD, 2 * HD)), like((ROWS + DIGITS - HD, 2 * HD))]
        + [like((ROWS + DIGITS, 2 * HD))] * (count - 1),
        [
            pltpu.VMEM((count, feats, 2 * HD), jnp.bfloat16),
            pltpu.SemaphoreType.DMA((count,)),
        ],
        name="project",
        mib=60,
    )


def ring_shift(high, low):
    devices = lax.axis_size("tp")
    up = [(i, (i + 1) % devices) for i in range(devices)]
    down = [(i, (i - 1) % devices) for i in range(devices)]
    return lax.ppermute(high, "tp", up), lax.ppermute(low, "tp", down)


def add_kernel(high_ref, low_ref, one_ref, two_ref, high_out, low_out):
    rows = high_ref.shape[0]
    high_out[:rows, :] = one_ref[:rows, :] + high_ref[...]
    if rows < ROWS:
        high_out[rows:, :] = one_ref[rows:, :]
        low_out[:rows, :] = two_ref[:rows, :]
        low_out[rows:, :] = two_ref[rows:, :] + low_ref[...]
    else:
        low_out[...] = two_ref[...] + low_ref[...]


def add_step(chain, high, low, one, two):
    return chain(
        add_kernel,
        (high, low, one, two),
        [VM] * 4,
        [VM] * 2,
        [like((ROWS + DIGITS, 2 * HD))] * 2,
        name="add_step",
    )


def fresh_kernel(mine_ref, high_ref, low_ref, cos_ref, sin_ref, whole_out, upper_out, lower_out, value_out):
    summed = mine_ref[...].astype(jnp.float32) + high_ref[...].astype(jnp.float32)
    summed = summed + low_ref[...].astype(jnp.float32)
    digits = summed[ROWS:, :]
    total = jnp.zeros((1, ROWS), jnp.float32)
    for k in range(DIGITS - 1, -1, -1):
        total = total + digits[k : k + 1, :] * (2.0 ** (27 - 5 * (k + 1)))
    inverse = lax.rsqrt(total / D + EPSILON)
    inverse = jnp.transpose(jnp.broadcast_to(inverse, (HD, ROWS)))
    key = summed[:ROWS, :HD] * inverse
    value = summed[:ROWS, HD:] * inverse
    key = key * cos_ref[...] + pltpu.roll(key, HD // 2, 1) * sin_ref[...]
    key = key.astype(jnp.bfloat16).reshape(BLK, BLK, HD)
    value = value.astype(jnp.bfloat16).reshape(BLK, BLK, HD)
    whole_out[:, :, :HD] = key
    whole_out[:, :, HD:] = value
    upper_out[...] = key[:, : BLK // 2]
    lower_out[...] = key[:, BLK // 2 :]
    value_out[...] = value


def fresh_rows(chain, mine, high, low, cosine, sine):
    half = like((BLK, BLK // 2, HD))
    return chain(
        fresh_kernel,
        (mine, high, low, cosine, sine),
        [VM] * 5,
        [VM] * 4,
        [like((BLK, BLK, 2 * HD)), half, half, like((BLK, BLK, HD))],
        name="fresh",
    )


def pack(chain, parts, passed=(), stand_in=None):
    shape = (parts[0].shape[0] * len(parts),) + parts[0].shape[1:]
    rows = parts[0].shape[0]
    count = len(parts)
    given = (*parts,) if stand_in is None else (*parts, stand_in)

    def kernel(*refs):
        out_ref = refs[len(given) + len(passed)]
        for k in range(count):
            out_ref[k * rows : (k + 1) * rows] = refs[k][...]
        if stand_in is not None:

            @pl.when(lax.rem(lax.axis_index("pipe"), 2) == 0)
            def _():
                out_ref[(count - 1) * rows :] = refs[count][...]

    return chain(
        kernel,
        (*given, *passed),
        [VM] * len(given) + [HB] * len(passed),
        [VM] + [HB] * len(passed),
        [like(shape)] + [pltpu.HBM(x.shape, x.dtype) for x in passed],
        name="pack",
        aliases={len(given) + k: 1 + k for k in range(len(passed))},
    )


SEGMENTS = 4
NOTED = CAPB + 1


def live_kernel(outs, len_ref, cache_ref, *refs):
    targets, held, sources, sems = refs[: len(outs)], refs[-2 - len(outs)], refs[-1 - len(outs) : -1], refs[-1]
    size = CBLK // SEGMENTS
    loads = []
    first_column = min(column for _, _, column in outs)
    width = held.shape[2]
    for k in range(SEGMENTS):
        part = pl.ds(k * size, size)
        loads.append(
            pltpu.make_async_copy(
                cache_ref.at[part, :, pl.ds(first_column, width)], held.at[part], sems.at[0, k]
            )
        )
        loads[-1].start()
    block = lax.broadcasted_iota(jnp.int32, (size, BLK, HD), 0)
    row = lax.broadcasted_iota(jnp.int32, (size, BLK, HD), 1) + block * BLK
    zero = jnp.zeros((), jnp.bfloat16)
    stores = []
    for k in range(SEGMENTS):
        part = pl.ds(k * size, size)
        loads[k].wait()
        live = row < len_ref[0, 0] - k * size * BLK
        for j, (start, stop, column) in enumerate(outs):
            columns = slice(column - first_column, column - first_column + HD)
            rows = jnp.where(live, held[part, :, columns], zero)
            sources[j][part] = rows[:, start:stop]
            stores.append(
                pltpu.make_async_copy(
                    sources[j].at[part], targets[j].at[part], sems.at[j + 1, k]
                )
            )
            stores[-1].start()
    for store in stores:
        store.wait()


def upper_kernel(len_ref, cache_ref, table_ref, out_ref, table_out, held, source, noted, sems):
    table = table_ref[...].reshape(1, NBLK).astype(jnp.float32)
    rest = jnp.concatenate(
        [table[:, 2 * HD :], jnp.zeros((1, 3 * HD - NBLK), jnp.float32)], axis=1
    )
    rows = [table[:, :HD], table[:, HD : 2 * HD], rest, jnp.zeros((5, HD), jnp.float32)]
    noted[0] = jnp.concatenate(rows, axis=0).astype(jnp.bfloat16)
    table_out[...] = noted[0]
    note = pltpu.make_async_copy(noted, out_ref.at[pl.ds(CBLK, 1)], sems.at[2, 0])
    note.start()
    live_kernel(((0, BLK // 2, 0),), len_ref, cache_ref, out_ref, held, source, sems)
    note.wait()


def live_upper(chain, cache_len, blocks, table):
    half = (CBLK, BLK // 2, HD)
    return chain(
        upper_kernel,
        (cache_len, blocks, table),
        [SM, HB, VM],
        [HB, VM],
        [pltpu.HBM((CBLK + 1, BLK // 2, HD), jnp.bfloat16), like((BLK // 2, HD))],
        [
            pltpu.VMEM((CBLK, BLK, HD), jnp.bfloat16),
            pltpu.VMEM(half, jnp.bfloat16),
            pltpu.VMEM((1, BLK // 2, HD), jnp.bfloat16),
            pltpu.SemaphoreType.DMA((3, SEGMENTS)),
        ],
        name="live_upper",
        mib=60,
    )


def live_rest(chain, cache_len, blocks):
    outs = ((BLK // 2, BLK, 0), (0, BLK // 2, HD), (BLK // 2, BLK, HD), (0, BLK, HD))
    shapes = [(CBLK, stop - start, HD) for start, stop, _ in outs]
    return chain(
        functools.partial(live_kernel, outs),
        (cache_len, blocks),
        [SM, HB],
        [HB] * len(outs),
        [pltpu.HBM(shape, jnp.bfloat16) for shape in shapes],
        [pltpu.VMEM(blocks.shape, jnp.bfloat16)]
        + [pltpu.VMEM(shape, jnp.bfloat16) for shape in shapes]
        + [pltpu.SemaphoreType.DMA((1 + len(outs), SEGMENTS))],
        name="live_rest",
        mib=32,
    )


def write_index(own_ref, table_ref, out_ref, note_ref):
    role = lax.axis_index("role")

    def column_rows(block):
        row = jnp.concatenate([block[0:1], block[1:2], block[2:3, : NBLK - 2 * HD]], axis=1)
        return jnp.broadcast_to(row, (8, NBLK))

    own_block = own_ref[...].astype(jnp.float32)
    sent_block = jnp.where(role == 0, own_block, table_ref[0].astype(jnp.float32))
    rows = jnp.concatenate([column_rows(own_block), column_rows(sent_block)], axis=0)
    tables = jnp.transpose(rows)
    own = tables[:, 0:1]
    sent = tables[:, 8:9]
    ids = lax.broadcasted_iota(jnp.int32, (NBLK, N_PIPE), 1).astype(jnp.float32)
    earlier = (
        lax.broadcasted_iota(jnp.int32, (NBLK, NBLK), 1)
        < lax.broadcasted_iota(jnp.int32, (NBLK, NBLK), 0)
    ).astype(jnp.bfloat16)

    def slots(column):
        onehot = column == ids
        before = jnp.dot(
            earlier, onehot.astype(jnp.bfloat16), preferred_element_type=jnp.float32
        )
        return jnp.sum(jnp.where(onehot, before, 0.0), axis=1, keepdims=True)

    own_slot = slots(own)
    sent_slot = slots(sent)
    turned = jnp.where(role == 0, jnp.where(sent >= 8.0, sent - 8.0, sent + 8.0), sent)
    slot_ids = lax.broadcasted_iota(jnp.int32, (1, SLOTS), 1)
    block = lax.broadcasted_iota(jnp.int32, (NBLK, 1), 0)

    def source(owner, slot):
        target = (owner * float(CAPB) + slot).astype(jnp.int32)
        return jnp.max(jnp.where(target == slot_ids, block, -1), axis=0, keepdims=True)

    sent_source = source(turned, sent_slot)
    out_ref[0:1, :] = jnp.where(sent_source < 0, NBLK, sent_source)
    own_source = source(own, own_slot)
    group = lax.div(slot_ids, CAPB)
    noted = slot_ids + group
    turned_ids = lax.rem(slot_ids + 8 * CAPB, SLOTS)
    turned_noted = lax.rem(noted + 8 * NOTED, N_PIPE * NOTED)
    own_noted = jnp.where(own_source < 0, N_PIPE * NOTED, own_source)
    out_ref[1:2, :] = jnp.where(role == 0, own_noted, turned_noted)
    out_ref[2:3, :] = jnp.where(role == 0, own_noted, noted)
    out_ref[3:4, :] = jnp.where(
        role == 0, jnp.where(own_source < 0, SLOTS, own_source), turned_ids
    )

    lanes = lax.broadcasted_iota(jnp.int32, (BLK, HD), 1)
    both = jnp.where(lanes == 0, sent_slot[CBLK:, :], sent[CBLK:, :])
    both = jnp.concatenate([both, jnp.full((HD - BLK, HD), -1.0, jnp.float32)], axis=0)
    both = jnp.transpose(both)
    for q in range(N_PIPE):
        note = jnp.where(both[1:2, :] == float(q), both[0:1, :], -1.0)
        note_ref[q] = jnp.broadcast_to(note, (BLK // 2, HD)).astype(jnp.bfloat16)


def fill_slots(index_ref, held, filled, out_ref, sems, note_ref=None):
    stride = CAPB if note_ref is None else NOTED
    for ref in held:
        ref[pl.ds(CBLK, BLK + 1)] = jnp.zeros((BLK + 1,) + ref.shape[1:], ref.dtype)
    groups = N_PIPE // SEGMENTS
    copies = []
    for k in range(SEGMENTS):

        def group_step(g, _):
            for s in range(CAPB):
                i = index_ref[0, g * CAPB + s]
                for j, ref in enumerate(held):
                    filled[g * stride + s, j * BLK // 2 : (j + 1) * BLK // 2] = ref[i]
            if note_ref is not None:
                filled[g * stride + CAPB] = note_ref[g]
            return 0

        lax.fori_loop(k * groups, (k + 1) * groups, group_step, 0)
        part = pl.ds(k * groups * stride, groups * stride)
        copies.append(pltpu.make_async_copy(filled.at[part], out_ref.at[part], sems.at[k]))
        copies[-1].start()
    for copy in copies:
        copy.wait()


def first_kernel(
    own_table, own_ref, crossed_ref, out_ref, index_ref, held, table, note, filled, listed, sems
):
    role = lax.axis_index("role")
    cached = pl.ds(0, CBLK)
    tables = pltpu.make_async_copy(
        crossed_ref.at[pl.ds(CBLK, 1)], table, sems.at[SEGMENTS + 1]
    )
    tables.start()

    @pl.when(role == 0)
    def _():
        pltpu.make_async_copy(own_ref, held.at[cached], sems.at[SEGMENTS]).start()

    @pl.when(role != 0)
    def _():
        pltpu.make_async_copy(
            crossed_ref.at[cached], held.at[cached], sems.at[SEGMENTS]
        ).start()

    tables.wait()
    write_index(own_table, table, index_ref, note)
    listing = pltpu.make_async_copy(index_ref, listed, sems.at[SEGMENTS + 2])
    listing.start()
    pltpu.make_async_copy(own_ref, held.at[cached], sems.at[SEGMENTS]).wait()
    listing.wait()
    fill_slots(listed, (held,), filled, out_ref, sems, note)


def first_dispatch(chain, table, own, crossed):
    half = (BLK // 2, HD)
    entries = N_PIPE * NOTED
    return chain(
        first_kernel,
        (table, own, crossed),
        [VM, HB, HB],
        [HB, VM],
        [pltpu.HBM((entries,) + half, jnp.bfloat16), like((4, SLOTS), jnp.int32)],
        [
            pltpu.VMEM((NBLK + 1,) + half, jnp.bfloat16),
            pltpu.VMEM((1,) + half, jnp.bfloat16),
            pltpu.VMEM((N_PIPE,) + half, jnp.bfloat16),
            pltpu.VMEM((entries,) + half, jnp.bfloat16),
            pltpu.SMEM((4, SLOTS), jnp.int32),
            pltpu.SemaphoreType.DMA((SEGMENTS + 3,)),
        ],
        name="first_dispatch",
        mib=24,
    )


def second_kernel(index_ref, *refs):
    own, crossed, out_ref, held, filled, sems = refs[:2], refs[2:4], refs[4], refs[5:7], *refs[7:]
    cached = pl.ds(0, CBLK)

    def load(sources):
        run_copies(
            [
                pltpu.make_async_copy(sources[j], held[j].at[cached], sems.at[SEGMENTS + j])
                for j in range(2)
            ]
        )

    @pl.when(lax.axis_index("role") == 0)
    def _():
        load(own)

    @pl.when(lax.axis_index("role") != 0)
    def _():
        load(crossed)

    fill_slots(index_ref, held, filled, out_ref, sems)


def second_dispatch(chain, index, own, crossed):
    return chain(
        second_kernel,
        (index, *own, *crossed),
        [SM] + [HB] * 4,
        [HB],
        [pltpu.HBM((SLOTS, BLK, HD), jnp.bfloat16)],
        [pltpu.VMEM((NBLK + 1, BLK // 2, HD), jnp.bfloat16)] * 2
        + [
            pltpu.VMEM((SLOTS, BLK, HD), jnp.bfloat16),
            pltpu.SemaphoreType.DMA((SEGMENTS + 2,)),
        ],
        name="second_dispatch",
        mib=24,
    )[0]


def place_kernel(index_ref, *refs):
    own, own_fresh, got = refs[0:3], refs[3:6], refs[6:9]
    near_ref, far_ref, out_ref = refs[9:12]
    held = refs[12:15]
    filled, notes, places, sems, out_sems = refs[15:]
    role = lax.axis_index("role")
    me = lax.axis_index("pipe")
    y = lax.div(me, 8)
    column = lax.rem(lax.div(me, 2), 4)
    core = lax.rem(me, 2)
    groups = N_PIPE // SEGMENTS
    for ref in held:
        ref[ref.shape[0] - 1] = jnp.zeros(ref.shape[1:], ref.dtype)

    def loads(k):
        copies = []
        for j in range(3):
            stride = CAPB if j == 2 else NOTED
            turn = k if j == 1 else (k + 2) % SEGMENTS
            part = pl.ds(turn * groups * stride, groups * stride)
            copies.append(
                pltpu.make_async_copy(got[j].at[part], held[j].at[part], sems.at[j, k])
            )
        return copies

    def fill(k):
        def group_step(g, _):
            for s in range(CAPB):
                r = g * CAPB + s
                filled[r, : BLK // 2, :HD] = held[0][index_ref[1, r]]
                filled[r, BLK // 2 :, :HD] = held[1][index_ref[2, r]]
                filled[r, :, HD:] = held[2][index_ref[3, r]]
            return 0

        lax.fori_loop(k * groups, (k + 1) * groups, group_step, 0)

    def store(k):
        part = pl.ds(k * groups * CAPB, groups * CAPB)
        return pltpu.make_async_copy(filled.at[part], out_ref.at[part], out_sems.at[k])

    @pl.when(role == 0)
    def _():
        copies = []
        for j in range(3):
            copies.append(
                pltpu.make_async_copy(
                    own[j].at[pl.ds(0, CBLK)], held[j].at[pl.ds(0, CBLK)], sems.at[j, 0]
                )
            )
            copies.append(
                pltpu.make_async_copy(
                    own_fresh[j], held[j].at[pl.ds(CBLK, BLK)], sems.at[j, 1]
                )
            )
        run_copies(copies)
        for k in range(SEGMENTS):
            fill(k)
            store(k).start()
        for k in range(SEGMENTS):
            store(k).wait()

    @pl.when(role != 0)
    def _():
        arrivals = [loads(k) for k in range(SEGMENTS)]
        for j in range(3):
            for k in range(SEGMENTS):
                arrivals[k][j].start()
        for k in range(SEGMENTS):
            arrivals[k][0].wait()
        for i in range(N_PIPE):
            p = (i + 8) % N_PIPE
            slot = held[0][i * NOTED + CAPB][0:1, :].astype(jnp.float32)
            spot = jnp.where(slot >= 0.0, slot + float(p * CAPB), float(SLOTS))
            notes[p : p + 1, :] = spot.astype(jnp.int32)
        listing = pltpu.make_async_copy(notes, places, out_sems.at[SEGMENTS])
        listing.start()
        for k in range(SEGMENTS):
            arrivals[k][1].wait()
            arrivals[k][2].wait()
            fill(k)
        listing.wait()
        for side, ref in enumerate((near_ref, far_ref)):
            sender = core if side == 0 else 1 - core
            for k in range(4):
                for e in range(2):
                    owner_y = jnp.where(sender == 0, 1 - y, y)
                    back = jnp.where(sender == 0, k + 1, k)
                    owner_column = lax.rem(column + 4 - back, 4)
                    owner_core = sender if e == 0 else 1 - sender
                    owner = (owner_y * 4 + owner_column) * 2 + owner_core
                    row = (k * 2 + e) * BLK
                    for j in range(BLK):
                        filled[places[owner, j]] = ref[row + j]
        for k in range(SEGMENTS):
            store(k).start()
        for k in range(SEGMENTS):
            store(k).wait()


def place(chain, index, own, own_fresh, got, near, far):
    entries = N_PIPE * NOTED
    return chain(
        place_kernel,
        (index, *own, *own_fresh, *got, near, far),
        [SM] + [HB] * 3 + [VM] * 3 + [HB] * 3 + [VM] * 2,
        [HB],
        [pltpu.HBM((SLOTS, BLK, 2 * HD), jnp.bfloat16)],
        [
            pltpu.VMEM((entries + 1, BLK // 2, HD), jnp.bfloat16),
            pltpu.VMEM((entries + 1, BLK // 2, HD), jnp.bfloat16),
            pltpu.VMEM((SLOTS + 1, BLK, HD), jnp.bfloat16),
            pltpu.VMEM((SLOTS + 1, BLK, 2 * HD), jnp.bfloat16),
            pltpu.VMEM((N_PIPE, HD), jnp.int32),
            pltpu.SMEM((N_PIPE, HD), jnp.int32),
            pltpu.SemaphoreType.DMA((3, SEGMENTS)),
            pltpu.SemaphoreType.DMA((SEGMENTS + 1,)),
        ],
        name="place",
        mib=56,
    )[0]


TOTAL = CAP + ROWS
CHUNKS = tuple((k, 512) for k in range(0, CAP, 512)) + ((CAP, ROWS),)


def attend_kernel(start, heads, q_ref, kv_ref, fresh_ref, len_ref, *refs):
    out_ref, bias, keys, values, first, second, mixed, sem = refs[-8:]
    keys[:CAP, :] = kv_ref[:, :HD]
    keys[CAP:, :] = fresh_ref[:, :, :HD].reshape(ROWS, HD)
    values[:CAP, :HD] = kv_ref[:, HD:]
    values[CAP:, :HD] = fresh_ref[:, :, HD:].reshape(ROWS, HD)
    values[:, HD:] = jnp.ones((TOTAL, HD), jnp.bfloat16)
    lengths = jnp.transpose(jnp.broadcast_to(len_ref[...].astype(jnp.float32), (HD, ROWS)))
    ids = lax.broadcasted_iota(jnp.int32, (ROWS, HD), 1).astype(jnp.float32)
    for k in range(0, CAP, HD):
        bias[:, k : k + HD] = jnp.where(ids + float(k) < lengths, 0.0, NEG_FILL)
    row = lax.broadcasted_iota(jnp.int32, (ROWS, ROWS), 0)
    column = lax.broadcasted_iota(jnp.int32, (ROWS, ROWS), 1)
    prefill = lax.axis_index("role") == 0
    bias[:, CAP:] = jnp.where(
        jnp.logical_and(column <= row, jnp.logical_or(prefill, column == row)), 0.0, NEG_FILL
    )
    held = (first, second)

    def score(head, k, size, top):
        part = lax.dot_general(
            q_ref[:, (start + head) * HD : (start + head + 1) * HD],
            keys[k : k + size, :],
            (((1,), (1,)), ((), ())),
            preferred_element_type=jnp.float32,
        )
        part = part + bias[:, k : k + size]
        held[head % 2][:, k : k + size] = part
        for j in range(0, size, HD):
            top = jnp.maximum(top, part[:, j : j + HD])
        return top

    def mix(head, k, size, top, total):
        weights = jnp.exp2((held[head % 2][:, k : k + size] - top) * EXP_SCALE)
        return total + jnp.dot(
            weights.astype(jnp.bfloat16),
            values[k : k + size, :],
            preferred_element_type=jnp.float32,
        )

    best = None
    for head in range(heads + 1):
        top = jnp.full((ROWS, HD), NEG_FILL, jnp.float32)
        total = jnp.zeros((ROWS, 2 * HD), jnp.float32)
        for k, size in CHUNKS:
            if head < heads:
                top = score(head, k, size, top)
            if head > 0:
                total = mix(head - 1, k, size, best, total)
        if head > 0:
            mixed[:, (head - 1) * HD : head * HD] = (
                total[:, :HD] / total[:, HD:]
            ).astype(jnp.bfloat16)
        if head < heads:
            best = jnp.max(top, axis=1, keepdims=True)
    columns = pl.ds(start * HD, heads * HD)
    run_copies([pltpu.make_async_copy(mixed, out_ref.at[:, columns], sem)])


def attend(chain, queries, cache, fresh, cache_len, start, heads, others=()):
    return chain(
        functools.partial(attend_kernel, start, heads),
        (queries, cache, fresh, cache_len, *others),
        [VM] * 4 + [HB] * len(others),
        [HB],
        [pltpu.HBM((ROWS, GROUP * HD), jnp.bfloat16)],
        [
            pltpu.VMEM((ROWS, TOTAL), jnp.float32),
            pltpu.VMEM((TOTAL, HD), jnp.bfloat16),
            pltpu.VMEM((TOTAL, 2 * HD), jnp.bfloat16),
            pltpu.VMEM((ROWS, TOTAL), jnp.float32),
            pltpu.VMEM((ROWS, TOTAL), jnp.float32),
            pltpu.VMEM((ROWS, heads * HD), jnp.bfloat16),
            pltpu.SemaphoreType.DMA,
        ],
        name="attend",
        mib=40,
        aliases={4: 0} if others else None,
    )[0]


def rotation(lengths):
    row_ids = jnp.arange(ROWS, dtype=jnp.int32)
    positions = lengths + jnp.where(lax.axis_index("role") == 0, row_ids, 0)
    frequency = ROPE_BASE ** (-2.0 * jnp.arange(HD // 2, dtype=jnp.float32) / HD)
    angles = positions.astype(jnp.float32)[:, None] * frequency[None, :]
    cosine, sine = jnp.cos(angles), jnp.sin(angles)
    return jnp.concatenate([cosine, cosine], axis=1), jnp.concatenate([-sine, sine], axis=1)


def local(hidden, norm_gain, kv_weight, queries, kv_cache, cache_len, block_table):
    chain = Chain()
    cache = kv_cache[0]
    query_rows = queries[0]
    blocks = cache.reshape(CBLK, BLK, 2 * HD)
    cosine, sine = rotation(cache_len[0])

    upper, table = live_upper(chain, cache_len, blocks, block_table)
    upper_crossed = cross(upper)
    lower, value_upper, value_lower, value = live_rest(chain, cache_len, blocks)
    halves = value_upper, value_lower
    halves_crossed = cross(value_upper), cross(value_lower)
    high, low, *sums = project(chain, hidden[0], norm_gain[None], kv_weight)

    def early(operands):
        table, lower, crossed, high, low, sums, chain.token = operands
        sent, index = first_dispatch(chain, table, lower, crossed)
        got = pipe_exchange(sent)
        high, low = ring_shift(high, low)
        for k in range(2):
            high, low = ring_shift(*add_step(chain, high, low, sums[2 * k], sums[2 * k + 1]))
        return index, got, high, low, chain.token

    operands = (table, lower, upper_crossed, high, low, sums[:4], chain.token)
    index, got_upper, high, low, chain.token = fenced(early, operands)
    sent_value = second_dispatch(chain, index, halves, halves_crossed)
    got_value = pipe_exchange(sent_value)

    def late(operands):
        high, low, sums, cosine, sine, chain.token = operands
        high, low = ring_shift(*add_step(chain, high, low, sums[0], sums[1]))
        fresh, *own_fresh = fresh_rows(chain, sums[2], high, low, cosine, sine)
        moved, beside = cross(fresh), cross(fresh, 9)
        attention = attend(chain, query_rows, cache, fresh, cache_len, 0, 4)
        return attention, fresh, own_fresh, moved, beside, chain.token

    got_lower = cross(got_upper)
    operands = (high, low, sums[4:], cosine, sine, chain.token)
    attention, fresh, own_fresh, moved, beside, chain.token = fenced(late, operands)
    pair, got_lower = pack(chain, (moved, beside), (got_lower,))
    reached = [spread(pair, k) for k in range(4)]
    attention = attend(chain, query_rows, cache, fresh, cache_len, 4, 2, (attention,))
    (near,) = pack(chain, reached, (), pair)
    far = pipe_move(near, lambda y, c, core: (y, c, 1 - core))
    attention = attend(chain, query_rows, cache, fresh, cache_len, 6, 2, (attention,))
    received = place(
        chain,
        index,
        (upper, lower, value),
        own_fresh,
        (got_upper, got_lower, got_value),
        near,
        far,
    )
    return (attention[None], received.reshape(1, SLOTS * BLK, 2 * HD))


def solution(mesh):
    in_specs = (
        P("role", "pipe", "tp"),
        P("tp"),
        P("tp", None),
        P("role", "pipe", "tp"),
        P("role", "pipe", "tp"),
        P("role", "pipe"),
        P("pipe"),
    )
    out_specs = (P("role", "pipe", "tp"), P("role", "pipe", "tp"))
    return jax.shard_map(local, mesh=mesh, in_specs=in_specs, out_specs=out_specs, check_vma=False)
```

time: 307 us -> 129 us (0.42)
  waiting for transfers between devices: 150 us -> 21.5 us
  Pallas kernels: 0 us -> 48 us
  local copies, waits for them, and re-layouts: 48.2 us -> 1.93 us
  starting transfers between devices: 17 us -> 55.2 us
  matrix products: 33 us -> 0 us
  other arithmetic: 22.5 us -> 0.69 us
  blocking collectives: 17.3 us -> 0 us
  between operations: 14.2 us -> 1.15 us
    all_to_all x1 -> x2, waiting for transfers between devices: 63.5 us -> 0.01 us  [pipe_exchange(): return lax.all_to_all(parts, 'pipe', 0, 0, tiled=True).reshape(x.shape)]
    pallas_call x0 -> x15, Pallas kernels: none -> 48 us  [__call__(): pl.pallas_call(body, in_specs=list(specs) + [VM] * extra, out_specs=list(...]
    ppermute x1 -> x19, waiting for transfers between devices: 58 us -> 21.5 us  [the longest x8 13.9 us: ring_shift(): return (lax.ppermute(high, 'tp', up), lax.ppermute(low, 'tp', down))]
    ppermute x1 -> x19, starting transfers between devices: 6.49 us -> 41.7 us  [the longest x6 19.5 us: cross(): return lax.ppermute(x, ('role', 'pipe'), pairs)]
    dot_general x10 -> x0, matrix products: 33 us -> none  [the longest x4 13.8 us: one_block(): jnp.einsum('rhgd,shd->rhgs', query_block, key_part, preferred_element_typ...]
    reduce_scatter x1 -> x0, waiting for transfers between devices: 28.3 us -> none  [local(): lax.psum_scatter(lax.dot_general(kv_weight, normed, (((0,), (1,)), ((), (...]
    psum x1 -> x0, blocking collectives: 17.3 us -> none  [local(): square_sum = lax.psum(jnp.sum(features * features, axis=1), 'tp')]
    reshape x3 -> x0, local copies, waits for them, and re-layouts: 12.6 us -> none  [the longest x1 6 us: local(): jnp.concatenate([cache_four, new_kv], axis=0).reshape(NBLK, BLK, -1)]
  transfers between devices with their start and end apart: 3 -> 21, of which waited for: 3 -> 6; matrix products, arithmetic and copies ran while one was open for 15% -> 1% of each run, Pallas kernels for 0% -> 29%
where the time goes in v2:
time: 129 us
  starting transfers between devices  55.2 us (43%)
  Pallas kernels  48 us (37%)
  waiting for transfers between devices  21.5 us (17%)
  local copies, waits for them, and re-layouts  1.93 us (1%)
    pallas_call x15, Pallas kernels, __call__(): pl.pallas_call(body, in_specs=list(specs) + [VM] * extra, out_specs=list(...  48 us
    ppermute x6, starting transfers between devices, cross(): return lax.ppermute(x, ('role', 'pipe'), pairs)  19.5 us
    ppermute x8, starting transfers between devices, ring_shift(): return (lax.ppermute(high, 'tp', up), lax.ppermute(low, 'tp', down))  14.5 us
    ppermute x8, waiting for transfers between devices, ring_shift(): return (lax.ppermute(high, 'tp', up), lax.ppermute(low, 'tp', down))  13.9 us
    all_to_all x2, starting transfers between devices, pipe_exchange(): return lax.all_to_all(parts, 'pipe', 0, 0, tiled=True).reshape(x.shape)  13.5 us
    ppermute x5, starting transfers between devices, pipe_move(): return lax.ppermute(x, 'pipe', pairs)  7.71 us
    ppermute x5, waiting for transfers between devices, pipe_move(): return lax.ppermute(x, 'pipe', pairs)  7.63 us
  transfers between devices with their start and end apart: 21, of which 6 were waited for; matrix products, arithmetic and copies ran while one was open for 1% of the time, Pallas kernels for 29%

profile of v2, /device:TPU:1, one launch (start us, length us, event | category | flops | bytes accessed | tf_op | source)
XLA Modules:
  0.0 128.7 jit_solution(16472175465132508388)
XLA Ops:
  0.6 0.0 copy-start.6
  0.7 3.4 %live_upper.1 = (bf16[257,8,128]{2,1,0:T(8,128)(2,1)}, bf16[8,128]{1,0:T(8,128)(2,1)S(1)}, f32[8,128]{1,0:T(8,128)}) custom-call(s32[1,256]{1,0:T(1,128)} %refs_3_.3, bf16[256,16,256]{2,1,0:T(8,128)(2,1)} %bitcast.12, s32[272]{0:T(512)} %refs_2_.2), custom_call_target="tpu_custom_call" | custom-call | flops 1 | bytes 1 | tf_op jit(solution)/shard_map/live_upper/pallas_call | solution.py:52
  4.1 5.5 %collective-permute-start.10 = (bf16[257,8,128]{2,1,0:T(8,128)(2,1)}, bf16[257,8,128]{2,1,0:T(8,128)(2,1)S(1)}, u32[]{:S(2)}, u32[]{:S(2)}) collective-permute-start(bf16[257,8,128]{2,1,0:T(8,128)(2,1)} %get-tuple-element.130.refs_1_), channel_id=1, source_target_pairs={{0,192},{8,200},{16,208},{24,216},{32,224},{40,232},{48,240},{56,2... | collective-permute-start | bytes 1579016 | tf_op jit(solution)/shard_map/ppermute | solution.py:89
  9.6 0.0 copy-start.5
  9.6 0.7 copy-done.5
  10.3 2.5 %live_rest.1 = (bf16[256,8,128]{2,1,0:T(8,128)(2,1)}, bf16[256,8,128]{2,1,0:T(8,128)(2,1)}, bf16[256,8,128]{2,1,0:T(8,128)(2,1)}, bf16[256,16,128]{2,1,0:T(8,128)(2,1)}, f32[8,128]{1,0:T(8,128)S(1)}) custom-call(s32[1,256]{1,0:T(1,128)S(1)} %copy-done.16, bf16[256,16,256]{2,1,0:T(8,128)(2,1)S(1)} %bitcast.13, f32[8,128]{1,0:T(8,128)S(1)} %copy-done.5), custom_call_target="tpu_custom_call" | custom-call | flops 1 | bytes 1 | tf_op jit(solution)/shard_map/live_rest/pallas_call | solution.py:52
  12.8 0.0 copy-start.4
  12.8 0.6 copy-done.4
  13.4 1.3 %collective-permute-start.11 = (bf16[256,8,128]{2,1,0:T(8,128)(2,1)}, bf16[256,8,128]{2,1,0:T(8,128)(2,1)S(1)}, u32[]{:S(2)}, u32[]{:S(2)}) collective-permute-start(bf16[256,8,128]{2,1,0:T(8,128)(2,1)} %get-tuple-element.144.refs_1_), channel_id=1, source_target_pairs={{0,192},{8,200},{16,208},{24,216},{32,224},{40,232},{48,240},{56,2... | collective-permute-start | bytes 1572872 | tf_op jit(solution)/shard_map/ppermute | solution.py:89
  14.7 1.3 %collective-permute-start.12 = (bf16[256,8,128]{2,1,0:T(8,128)(2,1)}, bf16[256,8,128]{2,1,0:T(8,128)(2,1)S(1)}, u32[]{:S(2)}, u32[]{:S(2)}) collective-permute-start(bf16[256,8,128]{2,1,0:T(8,128)(2,1)} %get-tuple-element.145.refs_2_), channel_id=1, source_target_pairs={{0,192},{8,200},{16,208},{24,216},{32,224},{40,232},{48,240},{56,2... | collective-permute-start | bytes 1572872 | tf_op jit(solution)/shard_map/ppermute | solution.py:89
  16.0 6.3 %project.1 = (bf16[128,256]{1,0:T(8,128)(2,1)}, bf16[144,256]{1,0:T(8,128)(2,1)}, bf16[272,256]{1,0:T(8,128)(2,1)}, bf16[272,256]{1,0:T(8,128)(2,1)}, bf16[272,2...) custom-call(bf16[256,1024]{1,0:T(8,128)(2,1)} %bitcast.22, ...), custom_call_target="tpu_custom_call" | custom-call | flops 1 | bytes 1 | tf_op jit(solution)/shard_map/project/pallas_call | solution.py:52
  22.3 0.0 collective-permute-done.10
  22.3 0.0 copy-start.1
  22.4 30.6 %conditional.2 = (s32[4,544]{1,0:T(4,128)S(1)}, bf16[560,8,128]{2,1,0:T(8,128)(2,1)}, bf16[272,256]{1,0:T(8,128)(2,1)}, bf16[272,256]{1,0:T(8,128)(2,1)}, f32[8,128]{1,0:T(8,128)S(1)}) conditional(s32[]{:T(128)} %convert_element_type.11, () %tuple.25, (bf16[8,128]{1,0:T(8,128)(2,1)S(1)}, bf16[256,8,128]{2,1,0:T(8,128)(2,1)S(1)}, ...), branch_computations={%region_0.1_spmd, %region_1.2_spmd} | conditional | flops 3 | bytes 9011683 | solution.py:84
  22.4 3.7 %first_dispatch.1 = (bf16[560,8,128]{2,1,0:T(8,128)(2,1)}, s32[4,544]{1,0:T(4,128)S(1)}, f32[8,128]{1,0:T(8,128)S(1)}) custom-call(bf16[8,128]{1,0:T(8,128)(2,1)S(1)} %get-tuple-element.42.refs_0_, bf16[256,8,128]{2,1,0:T(8,128)(2,1)S(1)} %get-tuple-element.43.refs_1_, bf16[257,8,128]{2,1,0:T(8,128)(2,1)S(1)} %get-tuple-element.44.refs_2_, ...), custom_call_target="tpu_custom_call" | custom-call | flops 1 | bytes 1 | tf_op jit(solution)/shard_map/cond/branch_1_fun/first_dispatch/pallas_call | solution.py:52
  26.1 5.4 %all-to-all-start = ((bf16[16,35,8,128]{3,2,1,0:T(8,128)(2,1)}), bf16[16,35,8,128]{3,2,1,0:T(8,128)(2,1)}, u32[]{:S(2)}, u32[]{:S(2)}) async-start(bf16[16,35,8,128]{3,2,1,0:T(8,128)(2,1)} %bitcast.21), calls=%async_computation | async-start | bytes 2293760 | tf_op jit(solution)/shard_map/cond/branch_1_fun/all_to_all | solution.py:115
  31.6 5.7 %collective-permute-start.1 = (bf16[144,256]{1,0:T(8,128)(2,1)S(1)}, bf16[144,256]{1,0:T(8,128)(2,1)S(1)}, u32[]{:S(2)}, u32[]{:S(2)}) collective-permute-start(bf16[144,256]{1,0:T(8,128)(2,1)S(1)} %copy-done.17), channel_id=1, source_target_pairs={{0,7},{1,0},{2,1},{3,2},{4,3},{5,4},{6,5},{7,6},{8,15},{9,8},{10,9... | collective-permute-start | bytes 221192 | tf_op jit(solution)/shard_map/cond/branch_1_fun/ppermute | solution.py:183
  37.2 0.0 collective-permute-start
  37.2 4.7 %collective-permute-done.refs_0_ = bf16[128,256]{1,0:T(8,128)(2,1)S(1)} collective-permute-done((bf16[128,256]{1,0:T(8,128)(2,1)S(1)}, bf16[128,256]{1,0:T(8,128)(2,1)S(1)}, u32[]{:S(2)}, u32[]{:S(2)}) %collective-permute-start) | collective-permute-done | bytes 65568 | tf_op jit(solution)/shard_map/cond/branch_1_fun/ppermute | solution.py:183
  41.9 0.0 collective-permute-done.1.refs_1_
  42.0 0.1 collective-permute-start.2
  42.1 2.7 %collective-permute-start.3 = (bf16[272,256]{1,0:T(8,128)(2,1)S(1)}, bf16[272,256]{1,0:T(8,128)(2,1)S(1)}, u32[]{:S(2)}, u32[]{:S(2)}) collective-permute-start(bf16[272,256]{1,0:T(8,128)(2,1)S(1)} %get-tuple-element.54), channel_id=1, source_target_pairs={{0,7},{1,0},{2,1},{3,2},{4,3},{5,4},{6,5},{7,6},{8,15},{9,8},{10,9... | collective-permute-start | bytes 417800 | tf_op jit(solution)/shard_map/cond/branch_1_fun/ppermute | solution.py:183
  44.7 2.8 %collective-permute-done.2.refs_0_ = bf16[272,256]{1,0:T(8,128)(2,1)S(1)} collective-permute-done((bf16[272,256]{1,0:T(8,128)(2,1)S(1)}, bf16[272,256]{1,0:T(8,128)(2,1)S(1)}, u32[]{:S(2)}, u32[]{:S(2)}) %collective-permute-start.2) | collective-permute-done | bytes 139296 | tf_op jit(solution)/shard_map/cond/branch_1_fun/ppermute | solution.py:183
  47.6 0.0 collective-permute-done.3.refs_1_
  47.6 0.1 collective-permute-start.4
  47.7 2.7 %collective-permute-start.5 = (bf16[272,256]{1,0:T(8,128)(2,1)S(1)}, bf16[272,256]{1,0:T(8,128)(2,1)}, u32[]{:S(2)}, u32[]{:S(2)}) collective-permute-start(bf16[272,256]{1,0:T(8,128)(2,1)S(1)} %get-tuple-element.59), channel_id=1, source_target_pairs={{0,7},{1,0},{2,1},{3,2},{4,3},{5,4},{6,5},{7,6},{8,15},{9,8},{10,9... | collective-permute-start | bytes 417800 | tf_op jit(solution)/shard_map/cond/branch_1_fun/ppermute | solution.py:183
  50.4 2.5 %collective-permute-done.4 = bf16[272,256]{1,0:T(8,128)(2,1)} collective-permute-done((bf16[272,256]{1,0:T(8,128)(2,1)S(1)}, bf16[272,256]{1,0:T(8,128)(2,1)}, u32[]{:S(2)}, u32[]{:S(2)}) %collective-permute-start.4) | collective-permute-done | bytes 139296 | tf_op jit(solution)/shard_map/cond/branch_1_fun/ppermute | solution.py:183
  52.9 0.0 all-to-all-done
  52.9 7.2 %collective-permute-start.13 = (bf16[560,8,128]{2,1,0:T(8,128)(2,1)}, bf16[560,8,128]{2,1,0:T(8,128)(2,1)}, u32[]{:S(2)}, u32[]{:S(2)}) collective-permute-start(bf16[560,8,128]{2,1,0:T(8,128)(2,1)} %get-tuple-element.153.refs_7_), channel_id=1, source_target_pairs={{0,192},{8,200},{16,208},{24,216},{32,224},{40,232},{48,240},{56,2... | collective-permute-start | bytes 3440648 | tf_op jit(solution)/shard_map/ppermute | solution.py:89
  60.2 0.0 collective-permute-done.11.refs_3_
  60.2 0.0 collective-permute-done.12.refs_4_
  60.2 3.0 %second_dispatch.1 = (bf16[544,16,128]{2,1,0:T(8,128)(2,1)}, f32[8,128]{1,0:T(8,128)S(1)}) custom-call(s32[4,544]{1,0:T(4,128)S(1)} %get-tuple-element.143.refs_0_, bf16[256,8,128]{2,1,0:T(8,128)(2,1)S(1)} %copy-done.1, bf16[256,8,128]{2,1,0:T(8,128)(2,1)S(1)} %copy-done.2, bf16[256,8,128]{2,1,0:T(8,128)(2,1)S(1)} %collective-permute-done.11.refs_3_, ...), custom_call_target="tpu_custom_call" | custom-call | flops 1 | bytes 1 | tf_op jit(solution)/shard_map/second_dispatch/pallas_call | solution.py:52
  63.2 0.0 copy-start.7
  63.2 0.0 copy-start.8
  63.3 8.1 %all-to-all-start.1 = ((bf16[16,34,16,128]{3,2,1,0:T(8,128)(2,1)}), bf16[16,34,16,128]{3,2,1,0:T(8,128)(2,1)}, u32[]{:S(2)}, u32[]{:S(2)}) async-start(bf16[16,34,16,128]{3,2,1,0:T(8,128)(2,1)} %bitcast.20), calls=%async_computation.1 | async-start | bytes 4456448 | tf_op jit(solution)/shard_map/all_to_all | solution.py:115
  71.4 0.5 fusion
  71.9 0.1 pad_maximum_fusion
  72.1 21.2 %conditional.3 = (bf16[256,1024]{1,0:T(8,128)(2,1)}, bf16[16,16,256]{2,1,0:T(8,128)(2,1)}, bf16[16,8,128]{2,1,0:T(8,128)(2,1)S(1)}, bf16[16,8,128]{2,1,0:T(8,128...) conditional(s32[]{:T(128)} %convert_element_type.11, () %tuple.24, ...), branch_computations={%region_2.3_spmd, %region_3.4_spmd} | conditional | flops 3 | bytes 2162915 | solution.py:84
  72.1 1.0 add_step.5
  73.1 0.1 collective-permute-start.6
  73.2 3.3 %collective-permute-start.7 = (bf16[272,256]{1,0:T(8,128)(2,1)S(1)}, bf16[272,256]{1,0:T(8,128)(2,1)S(1)}, u32[]{:S(2)}, u32[]{:S(2)}) collective-permute-start(bf16[272,256]{1,0:T(8,128)(2,1)S(1)} %get-tuple-element.70), channel_id=1, source_target_pairs={{0,7},{1,0},{2,1},{3,2},{4,3},{5,4},{6,5},{7,6},{8,15},{9,8},{10,9... | collective-permute-start | bytes 417800 | tf_op jit(solution)/shard_map/cond/branch_1_fun/ppermute | solution.py:183
  76.5 3.8 %collective-permute-done.6.refs_1_ = bf16[272,256]{1,0:T(8,128)(2,1)S(1)} collective-permute-done((bf16[272,256]{1,0:T(8,128)(2,1)S(1)}, bf16[272,256]{1,0:T(8,128)(2,1)S(1)}, u32[]{:S(2)}, u32[]{:S(2)}) %collective-permute-start.6) | collective-permute-done | bytes 139296 | tf_op jit(solution)/shard_map/cond/branch_1_fun/ppermute | solution.py:183
  80.3 0.0 collective-permute-done.7.refs_2_
  80.3 0.9 fresh.1
  81.1 2.2 %collective-permute-start.9 = (bf16[16,16,256]{2,1,0:T(8,128)(2,1)}, bf16[16,16,256]{2,1,0:T(8,128)(2,1)}, u32[]{:S(2)}, u32[]{:S(2)}) collective-permute-start(bf16[16,16,256]{2,1,0:T(8,128)(2,1)} %get-tuple-element.194.refs_2_), channel_id=1, source_target_pairs={{0,200},{8,192},{16,216},{24,208},{32,232},{40,224},{48,248},{56,2... | collective-permute-start | bytes 393224 | tf_op jit(solution)/shard_map/cond/branch_1_fun/ppermute | solution.py:89
  83.4 1.9 %collective-permute-start.8 = (bf16[16,16,256]{2,1,0:T(8,128)(2,1)}, bf16[16,16,256]{2,1,0:T(8,128)(2,1)}, u32[]{:S(2)}, u32[]{:S(2)}) collective-permute-start(bf16[16,16,256]{2,1,0:T(8,128)(2,1)} %get-tuple-element.194.refs_2_), channel_id=1, source_target_pairs={{0,192},{8,200},{16,208},{24,216},{32,224},{40,232},{48,240},{56,2... | collective-permute-start | bytes 393224 | tf_op jit(solution)/shard_map/cond/branch_1_fun/ppermute | solution.py:89
  85.3 8.0 %attend.3 = (bf16[256,1024]{1,0:T(8,128)(2,1)}, f32[8,128]{1,0:T(8,128)S(1)}) custom-call(bf16[256,1024]{1,0:T(8,128)(2,1)S(1)} %get-tuple-element.61.refs_0_, bf16[4096,256]{1,0:T(8,128)(2,1)S(1)} %get-tuple-element.62.refs_1_, bf16[16,16,256]{2,1,0:T(8,128)(2,1)} %get-tuple-element.194.refs_2_, s32[1,256]{1,0:T(1,128)S(1)} %get-tuple-element.75.refs_3_, ...), custom_call_target="tpu_custom_call" | custom-call | flops 1 | bytes 1 | tf_op jit(solution)/shard_map/cond/branch_1_fun/attend/pallas_call | solution.py:52
  93.3 0.0 collective-permute-done.8
  93.3 1.0 pack.2
  94.3 4.9 %collective-permute-start.17 = (bf16[32,16,256]{2,1,0:T(8,128)(2,1)S(1)}, bf16[32,16,256]{2,1,0:T(8,128)(2,1)S(1)}, u32[]{:S(2)}, u32[]{:S(2)}) collective-permute-start(bf16[32,16,256]{2,1,0:T(8,128)(2,1)S(1)} %get-tuple-element.157.refs_4_), channel_id=1, source_target_pairs={{8,120},{24,72},{40,88},{56,104},{72,56},{88,8},{104,24},{120,40},... | collective-permute-start | bytes 786440 | tf_op jit(solution)/shard_map/ppermute | solution.py:101
  99.3 0.9 collective-permute-start.16
  100.2 1.1 collective-permute-start.15
  101.3 0.6 collective-permute-start.14
  101.9 5.2 %attend.4 = (bf16[256,1024]{1,0:T(8,128)(2,1)}, f32[8,128]{1,0:T(8,128)S(1)}) custom-call(bf16[256,1024]{1,0:T(8,128)(2,1)S(1)} %bitcast.18, bf16[4096,256]{1,0:T(8,128)(2,1)S(1)} %bitcast.15, bf16[16,16,256]{2,1,0:T(8,128)(2,1)} %get-tuple-element.149.refs_2_, s32[1,256]{1,0:T(1,128)S(1)} %copy-done.16, ...), custom_call_target="tpu_custom_call", output_to_operand_aliasing={{0}: (4, {})} | custom-call | flops 1 | bytes 1 | tf_op jit(solution)/shard_map/attend/pallas_call | solution.py:52
  107.1 0.0 copy-start.9
  107.1 0.0 collective-permute-done.17.refs_3_
  107.1 2.6 %collective-permute-done.16.refs_2_ = bf16[32,16,256]{2,1,0:T(8,128)(2,1)S(1)} collective-permute-done((bf16[32,16,256]{2,1,0:T(8,128)(2,1)S(1)}, bf16[32,16,256]{2,1,0:T(8,128)(2,1)S(1)}, u32[]{:S(2)}, u32[]{:S(2)}) %collective-permute-start.16) | collective-permute-done | bytes 262176 | tf_op jit(solution)/shard_map/ppermute | solution.py:101
  109.8 5.0 %collective-permute-done.15.refs_1_ = bf16[32,16,256]{2,1,0:T(8,128)(2,1)S(1)} collective-permute-done((bf16[32,16,256]{2,1,0:T(8,128)(2,1)S(1)}, bf16[32,16,256]{2,1,0:T(8,128)(2,1)S(1)}, u32[]{:S(2)}, u32[]{:S(2)}) %collective-permute-start.15) | collective-permute-done | bytes 262176 | tf_op jit(solution)/shard_map/ppermute | solution.py:101
  114.8 0.0 collective-permute-done.14.refs_0_
  114.8 0.1 pack.3
  114.8 0.1 collective-permute-start.18
  115.0 5.3 %attend.5 = (bf16[256,1024]{1,0:T(8,128)(2,1)}, f32[8,128]{1,0:T(8,128)S(1)}) custom-call(bf16[256,1024]{1,0:T(8,128)(2,1)S(1)} %bitcast.19, bf16[4096,256]{1,0:T(8,128)(2,1)S(1)} %bitcast.16, bf16[16,16,256]{2,1,0:T(8,128)(2,1)} %get-tuple-element.149.refs_2_, s32[1,256]{1,0:T(1,128)S(1)} %copy-done.16, ...), custom_call_target="tpu_custom_call", output_to_operand_aliasing={{0}: (4, {})} | custom-call | flops 1 | bytes 1 | tf_op jit(solution)/shard_map/attend/pallas_call | solution.py:52
  120.3 0.6 copy-done.3
  120.9 7.7 %place.1 = (bf16[544,16,256]{2,1,0:T(8,128)(2,1)}, f32[8,128]{1,0:T(8,128)}) custom-call(s32[4,544]{1,0:T(4,128)S(1)} %get-tuple-element.143.refs_0_, bf16[257,8,128]{2,1,0:T(8,128)(2,1)} %get-tuple-element.130.refs_1_, bf16[256,8,128]{2,1,0:T(8,128)(2,1)} %get-tuple-element.129.refs_2_, bf16[256,16,128]{2,1,0:T(8,128)(2,1)} %get-tuple-element.161.refs_3_, ...), custom_call_target="tpu_custom_call" | custom-call | flops 1 | bytes 1 | tf_op jit(solution)/shard_map/place/pallas_call | solution.py:52
  (37 shorter events, 0.2 us)
Async XLA Ops:
  0.6 9.0 %copy-start.16 = (s32[1,256]{1,0:T(1,128)S(1)}, s32[1,256]{1,0:T(1,128)}, u32[]{:S(2)}) copy-start(s32[1,256]{1,0:T(1,128)} %refs_3_.3) | copy-start | bytes 3076
  0.6 9.0 %copy-start.6 = (bf16[1,4096,256]{2,1,0:T(8,128)(2,1)S(1)}, bf16[1,4096,256]{2,1,0:T(8,128)(2,1)}, u32[]{:S(2)}) copy-start(bf16[1,4096,256]{2,1,0:T(8,128)(2,1)} %param.15) | copy-start | bytes 6291460
  4.1 18.2 %collective-permute-start.10 = (bf16[257,8,128]{2,1,0:T(8,128)(2,1)}, bf16[257,8,128]{2,1,0:T(8,128)(2,1)S(1)}, u32[]{:S(2)}, u32[]{:S(2)}) collective-permute-start(bf16[257,8,128]{2,1,0:T(8,128)(2,1)} %get-tuple-element.130.refs_1_), channel_id=1, source_target_pairs={{0,192},{8,200},{16,208},{24,216},{32,224},{40,232},{48,240},{56,2... | collective-permute-start | bytes 1579016 | tf_op jit(solution)/shard_map/ppermute | solution.py:89
  9.6 0.7 copy-start.5
  12.8 0.6 copy-start.4
  13.4 46.8 %collective-permute-start.11 = (bf16[256,8,128]{2,1,0:T(8,128)(2,1)}, bf16[256,8,128]{2,1,0:T(8,128)(2,1)S(1)}, u32[]{:S(2)}, u32[]{:S(2)}) collective-permute-start(bf16[256,8,128]{2,1,0:T(8,128)(2,1)} %get-tuple-element.144.refs_1_), channel_id=1, source_target_pairs={{0,192},{8,200},{16,208},{24,216},{32,224},{40,232},{48,240},{56,2... | collective-permute-start | bytes 1572872 | tf_op jit(solution)/shard_map/ppermute | solution.py:89
  14.7 45.5 %collective-permute-start.12 = (bf16[256,8,128]{2,1,0:T(8,128)(2,1)}, bf16[256,8,128]{2,1,0:T(8,128)(2,1)S(1)}, u32[]{:S(2)}, u32[]{:S(2)}) collective-permute-start(bf16[256,8,128]{2,1,0:T(8,128)(2,1)} %get-tuple-element.145.refs_2_), channel_id=1, source_target_pairs={{0,192},{8,200},{16,208},{24,216},{32,224},{40,232},{48,240},{56,2... | collective-permute-start | bytes 1572872 | tf_op jit(solution)/shard_map/ppermute | solution.py:89
  16.0 6.3 %copy-start.10 = (bf16[256,8,128]{2,1,0:T(8,128)(2,1)S(1)}, bf16[256,8,128]{2,1,0:T(8,128)(2,1)}, u32[]{:S(2)}) copy-start(bf16[256,8,128]{2,1,0:T(8,128)(2,1)} %get-tuple-element.129.refs_2_) | copy-start | bytes 1572868
  22.3 37.8 %copy-start.1 = (bf16[256,8,128]{2,1,0:T(8,128)(2,1)S(1)}, bf16[256,8,128]{2,1,0:T(8,128)(2,1)}, u32[]{:S(2)}) copy-start(bf16[256,8,128]{2,1,0:T(8,128)(2,1)} %get-tuple-element.144.refs_1_) | copy-start | bytes 1572868
  22.4 37.8 %copy-start.2 = (bf16[256,8,128]{2,1,0:T(8,128)(2,1)S(1)}, bf16[256,8,128]{2,1,0:T(8,128)(2,1)}, u32[]{:S(2)}) copy-start(bf16[256,8,128]{2,1,0:T(8,128)(2,1)} %get-tuple-element.145.refs_2_) | copy-start | bytes 1572868
  26.1 5.5 %copy-start.17 = (bf16[144,256]{1,0:T(8,128)(2,1)S(1)}, bf16[144,256]{1,0:T(8,128)(2,1)}, u32[]{:S(2)}) copy-start(bf16[144,256]{1,0:T(8,128)(2,1)} %get-tuple-element.49) | copy-start | bytes 221188 | tf_op jit(solution)/shard_map/cond
  26.1 11.1 %copy-start.18 = (bf16[128,256]{1,0:T(8,128)(2,1)S(1)}, bf16[128,256]{1,0:T(8,128)(2,1)}, u32[]{:S(2)}) copy-start(bf16[128,256]{1,0:T(8,128)(2,1)} %get-tuple-element.48) | copy-start | bytes 196612 | tf_op jit(solution)/shard_map/cond
  26.1 15.8 %copy-start.12 = (bf16[272,256]{1,0:T(8,128)(2,1)S(1)}, bf16[272,256]{1,0:T(8,128)(2,1)}, u32[]{:S(2)}) copy-start(bf16[272,256]{1,0:T(8,128)(2,1)} %get-tuple-element.50.refs_2_) | copy-start | bytes 417796 | tf_op jit(solution)/shard_map/cond
  26.1 15.8 %copy-start.13 = (bf16[272,256]{1,0:T(8,128)(2,1)S(1)}, bf16[272,256]{1,0:T(8,128)(2,1)}, u32[]{:S(2)}) copy-start(bf16[272,256]{1,0:T(8,128)(2,1)} %get-tuple-element.51.refs_3_) | copy-start | bytes 417796 | tf_op jit(solution)/shard_map/cond
  26.1 21.5 %copy-start.14 = (bf16[272,256]{1,0:T(8,128)(2,1)S(1)}, bf16[272,256]{1,0:T(8,128)(2,1)}, u32[]{:S(2)}) copy-start(bf16[272,256]{1,0:T(8,128)(2,1)} %get-tuple-element.55.refs_2_) | copy-start | bytes 417796 | tf_op jit(solution)/shard_map/cond
  26.1 21.5 %copy-start.15 = (bf16[272,256]{1,0:T(8,128)(2,1)S(1)}, bf16[272,256]{1,0:T(8,128)(2,1)}, u32[]{:S(2)}) copy-start(bf16[272,256]{1,0:T(8,128)(2,1)} %get-tuple-element.56.refs_3_) | copy-start | bytes 417796 | tf_op jit(solution)/shard_map/cond
  26.1 26.8 %all-to-all-start = ((bf16[16,35,8,128]{3,2,1,0:T(8,128)(2,1)}), bf16[16,35,8,128]{3,2,1,0:T(8,128)(2,1)}, u32[]{:S(2)}, u32[]{:S(2)}) async-start(bf16[16,35,8,128]{3,2,1,0:T(8,128)(2,1)} %bitcast.21), calls=%async_computation | async-start | bytes 2293760 | tf_op jit(solution)/shard_map/cond/branch_1_fun/all_to_all | solution.py:115
  31.6 10.4 %collective-permute-start.1 = (bf16[144,256]{1,0:T(8,128)(2,1)S(1)}, bf16[144,256]{1,0:T(8,128)(2,1)S(1)}, u32[]{:S(2)}, u32[]{:S(2)}) collective-permute-start(bf16[144,256]{1,0:T(8,128)(2,1)S(1)} %copy-done.17), channel_id=1, source_target_pairs={{0,7},{1,0},{2,1},{3,2},{4,3},{5,4},{6,5},{7,6},{8,15},{9,8},{10,9... | collective-permute-start | bytes 221192 | tf_op jit(solution)/shard_map/cond/branch_1_fun/ppermute | solution.py:183
  37.2 4.7 %collective-permute-start = (bf16[128,256]{1,0:T(8,128)(2,1)S(1)}, bf16[128,256]{1,0:T(8,128)(2,1)S(1)}, u32[]{:S(2)}, u32[]{:S(2)}) collective-permute-start(bf16[128,256]{1,0:T(8,128)(2,1)S(1)} %copy-done.18), channel_id=1, source_target_pairs={{0,1},{1,2},{2,3},{3,4},{4,5},{5,6},{6,7},{7,0},{8,9},{9,10},{10,1... | collective-permute-start | bytes 196616 | tf_op jit(solution)/shard_map/cond/branch_1_fun/ppermute | solution.py:183
  42.0 5.6 %collective-permute-start.2 = (bf16[272,256]{1,0:T(8,128)(2,1)S(1)}, bf16[272,256]{1,0:T(8,128)(2,1)S(1)}, u32[]{:S(2)}, u32[]{:S(2)}) collective-permute-start(bf16[272,256]{1,0:T(8,128)(2,1)S(1)} %get-tuple-element.53), channel_id=1, source_target_pairs={{0,1},{1,2},{2,3},{3,4},{4,5},{5,6},{6,7},{7,0},{8,9},{9,10},{10,1... | collective-permute-start | bytes 417800 | tf_op jit(solution)/shard_map/cond/branch_1_fun/ppermute | solution.py:183
  42.1 5.5 %collective-permute-start.3 = (bf16[272,256]{1,0:T(8,128)(2,1)S(1)}, bf16[272,256]{1,0:T(8,128)(2,1)S(1)}, u32[]{:S(2)}, u32[]{:S(2)}) collective-permute-start(bf16[272,256]{1,0:T(8,128)(2,1)S(1)} %get-tuple-element.54), channel_id=1, source_target_pairs={{0,7},{1,0},{2,1},{3,2},{4,3},{5,4},{6,5},{7,6},{8,15},{9,8},{10,9... | collective-permute-start | bytes 417800 | tf_op jit(solution)/shard_map/cond/branch_1_fun/ppermute | solution.py:183
  47.6 5.3 %collective-permute-start.4 = (bf16[272,256]{1,0:T(8,128)(2,1)S(1)}, bf16[272,256]{1,0:T(8,128)(2,1)}, u32[]{:S(2)}, u32[]{:S(2)}) collective-permute-start(bf16[272,256]{1,0:T(8,128)(2,1)S(1)} %get-tuple-element.58), channel_id=1, source_target_pairs={{0,1},{1,2},{2,3},{3,4},{4,5},{5,6},{6,7},{7,0},{8,9},{9,10},{10,1... | collective-permute-start | bytes 417800 | tf_op jit(solution)/shard_map/cond/branch_1_fun/ppermute | solution.py:183
  47.7 5.2 %collective-permute-start.5 = (bf16[272,256]{1,0:T(8,128)(2,1)S(1)}, bf16[272,256]{1,0:T(8,128)(2,1)}, u32[]{:S(2)}, u32[]{:S(2)}) collective-permute-start(bf16[272,256]{1,0:T(8,128)(2,1)S(1)} %get-tuple-element.59), channel_id=1, source_target_pairs={{0,7},{1,0},{2,1},{3,2},{4,3},{5,4},{6,5},{7,6},{8,15},{9,8},{10,9... | collective-permute-start | bytes 417800 | tf_op jit(solution)/shard_map/cond/branch_1_fun/ppermute | solution.py:183
  52.9 40.4 %collective-permute-start.13 = (bf16[560,8,128]{2,1,0:T(8,128)(2,1)}, bf16[560,8,128]{2,1,0:T(8,128)(2,1)}, u32[]{:S(2)}, u32[]{:S(2)}) collective-permute-start(bf16[560,8,128]{2,1,0:T(8,128)(2,1)} %get-tuple-element.153.refs_7_), channel_id=1, source_target_pairs={{0,192},{8,200},{16,208},{24,216},{32,224},{40,232},{48,240},{56,2... | collective-permute-start | bytes 3440648 | tf_op jit(solution)/shard_map/ppermute | solution.py:89
  63.2 8.8 %copy-start.7 = (bf16[1,4096,256]{2,1,0:T(8,128)(2,1)S(1)}, bf16[1,4096,256]{2,1,0:T(8,128)(2,1)}, u32[]{:S(2)}) copy-start(bf16[1,4096,256]{2,1,0:T(8,128)(2,1)} %param.15) | copy-start | bytes 6291460
  63.2 8.8 %copy-start.8 = (bf16[1,256,1024]{2,1,0:T(8,128)(2,1)S(1)}, bf16[1,256,1024]{2,1,0:T(8,128)(2,1)}, u32[]{:S(2)}) copy-start(bf16[1,256,1024]{2,1,0:T(8,128)(2,1)} %param.14) | copy-start | bytes 1572868
  63.2 8.8 %copy-start.11 = (bf16[272,256]{1,0:T(8,128)(2,1)S(1)}, bf16[272,256]{1,0:T(8,128)(2,1)}, u32[]{:S(2)}) copy-start(bf16[272,256]{1,0:T(8,128)(2,1)} %get-tuple-element.148) | copy-start | bytes 417796
  63.3 57.6 %all-to-all-start.1 = ((bf16[16,34,16,128]{3,2,1,0:T(8,128)(2,1)}), bf16[16,34,16,128]{3,2,1,0:T(8,128)(2,1)}, u32[]{:S(2)}, u32[]{:S(2)}) async-start(bf16[16,34,16,128]{3,2,1,0:T(8,128)(2,1)} %bitcast.20), calls=%async_computation.1 | async-start | bytes 4456448 | tf_op jit(solution)/shard_map/all_to_all | solution.py:115
  73.1 7.2 %collective-permute-start.6 = (bf16[272,256]{1,0:T(8,128)(2,1)S(1)}, bf16[272,256]{1,0:T(8,128)(2,1)S(1)}, u32[]{:S(2)}, u32[]{:S(2)}) collective-permute-start(bf16[272,256]{1,0:T(8,128)(2,1)S(1)} %get-tuple-element.69), channel_id=1, source_target_pairs={{0,1},{1,2},{2,3},{3,4},{4,5},{5,6},{6,7},{7,0},{8,9},{9,10},{10,1... | collective-permute-start | bytes 417800 | tf_op jit(solution)/shard_map/cond/branch_1_fun/ppermute | solution.py:183
  73.2 7.1 %collective-permute-start.7 = (bf16[272,256]{1,0:T(8,128)(2,1)S(1)}, bf16[272,256]{1,0:T(8,128)(2,1)S(1)}, u32[]{:S(2)}, u32[]{:S(2)}) collective-permute-start(bf16[272,256]{1,0:T(8,128)(2,1)S(1)} %get-tuple-element.70), channel_id=1, source_target_pairs={{0,7},{1,0},{2,1},{3,2},{4,3},{5,4},{6,5},{7,6},{8,15},{9,8},{10,9... | collective-permute-start | bytes 417800 | tf_op jit(solution)/shard_map/cond/branch_1_fun/ppermute | solution.py:183
  81.1 12.1 %collective-permute-start.9 = (bf16[16,16,256]{2,1,0:T(8,128)(2,1)}, bf16[16,16,256]{2,1,0:T(8,128)(2,1)}, u32[]{:S(2)}, u32[]{:S(2)}) collective-permute-start(bf16[16,16,256]{2,1,0:T(8,128)(2,1)} %get-tuple-element.194.refs_2_), channel_id=1, source_target_pairs={{0,200},{8,192},{16,216},{24,208},{32,232},{40,224},{48,248},{56,2... | collective-permute-start | bytes 393224 | tf_op jit(solution)/shard_map/cond/branch_1_fun/ppermute | solution.py:89
  83.4 9.9 %collective-permute-start.8 = (bf16[16,16,256]{2,1,0:T(8,128)(2,1)}, bf16[16,16,256]{2,1,0:T(8,128)(2,1)}, u32[]{:S(2)}, u32[]{:S(2)}) collective-permute-start(bf16[16,16,256]{2,1,0:T(8,128)(2,1)} %get-tuple-element.194.refs_2_), channel_id=1, source_target_pairs={{0,192},{8,200},{16,208},{24,216},{32,224},{40,232},{48,240},{56,2... | collective-permute-start | bytes 393224 | tf_op jit(solution)/shard_map/cond/branch_1_fun/ppermute | solution.py:89
  94.3 12.8 %collective-permute-start.17 = (bf16[32,16,256]{2,1,0:T(8,128)(2,1)S(1)}, bf16[32,16,256]{2,1,0:T(8,128)(2,1)S(1)}, u32[]{:S(2)}, u32[]{:S(2)}) collective-permute-start(bf16[32,16,256]{2,1,0:T(8,128)(2,1)S(1)} %get-tuple-element.157.refs_4_), channel_id=1, source_target_pairs={{8,120},{24,72},{40,88},{56,104},{72,56},{88,8},{104,24},{120,40},... | collective-permute-start | bytes 786440 | tf_op jit(solution)/shard_map/ppermute | solution.py:101
  99.3 10.5 %collective-permute-start.16 = (bf16[32,16,256]{2,1,0:T(8,128)(2,1)S(1)}, bf16[32,16,256]{2,1,0:T(8,128)(2,1)S(1)}, u32[]{:S(2)}, u32[]{:S(2)}) collective-permute-start(bf16[32,16,256]{2,1,0:T(8,128)(2,1)S(1)} %get-tuple-element.157.refs_4_), channel_id=1, source_target_pairs={{0,48},{8,104},{16,0},{24,120},{32,16},{40,72},{48,32},{56,88},{64... | collective-permute-start | bytes 786440 | tf_op jit(solution)/shard_map/ppermute | solution.py:101
  100.2 14.6 %collective-permute-start.15 = (bf16[32,16,256]{2,1,0:T(8,128)(2,1)S(1)}, bf16[32,16,256]{2,1,0:T(8,128)(2,1)S(1)}, u32[]{:S(2)}, u32[]{:S(2)}) collective-permute-start(bf16[32,16,256]{2,1,0:T(8,128)(2,1)S(1)} %get-tuple-element.157.refs_4_), channel_id=1, source_target_pairs={{0,32},{8,88},{16,48},{24,104},{32,0},{40,120},{48,16},{56,72},{64... | collective-permute-start | bytes 786440 | tf_op jit(solution)/shard_map/ppermute | solution.py:101
  101.3 13.5 %collective-permute-start.14 = (bf16[32,16,256]{2,1,0:T(8,128)(2,1)S(1)}, bf16[32,16,256]{2,1,0:T(8,128)(2,1)S(1)}, u32[]{:S(2)}, u32[]{:S(2)}) collective-permute-start(bf16[32,16,256]{2,1,0:T(8,128)(2,1)S(1)} %get-tuple-element.157.refs_4_), channel_id=1, source_target_pairs={{0,16},{8,72},{16,32},{24,88},{32,48},{40,104},{48,0},{56,120},{64... | collective-permute-start | bytes 786440 | tf_op jit(solution)/shard_map/ppermute | solution.py:101
  107.1 7.8 %copy-start.9 = (bf16[1,256,1024]{2,1,0:T(8,128)(2,1)S(1)}, bf16[1,256,1024]{2,1,0:T(8,128)(2,1)}, u32[]{:S(2)}) copy-start(bf16[1,256,1024]{2,1,0:T(8,128)(2,1)} %param.14) | copy-start | bytes 1572868
  114.8 5.5 %copy-start = (bf16[128,16,256]{2,1,0:T(8,128)(2,1)}, bf16[128,16,256]{2,1,0:T(8,128)(2,1)S(1)}, u32[]{:S(2)}) copy-start(bf16[128,16,256]{2,1,0:T(8,128)(2,1)S(1)} %get-tuple-element.167.refs_10_) | copy-start | bytes 3145732
  114.8 6.0 %collective-permute-start.18 = (bf16[128,16,256]{2,1,0:T(8,128)(2,1)S(1)}, bf16[128,16,256]{2,1,0:T(8,128)(2,1)}, u32[]{:S(2)}, u32[]{:S(2)}) collective-permute-start(bf16[128,16,256]{2,1,0:T(8,128)(2,1)S(1)} %get-tuple-element.167.refs_10_), channel_id=1, source_target_pairs={{0,8},{8,0},{16,24},{24,16},{32,40},{40,32},{48,56},{56,48},{64,72... | collective-permute-start | bytes 3145736 | tf_op jit(solution)/shard_map/ppermute | solution.py:101
  120.3 0.6 copy-start.3

commit v3 on v2

--- a/solution.py
+++ b/solution.py
@@ -534,7 +534,7 @@
     own, own_fresh, got = refs[0:3], refs[3:6], refs[6:9]
     near_ref, far_ref, out_ref = refs[9:12]
     held = refs[12:15]
-    filled, notes, places, sems, out_sems = refs[15:]
+    fresh, filled, notes, places, sems, out_sems = refs[15:]
     role = lax.axis_index("role")
     me = lax.axis_index("pipe")
     y = lax.div(me, 8)
@@ -591,12 +591,35 @@
         for k in range(SEGMENTS):
             store(k).wait()
 
+    def patch(k):
+        def one(p, _):
+            sender = jnp.where(lax.div(p, 8) == y, 1, 0)
+            back = lax.rem(column - lax.rem(lax.div(p, 2), 4) + 7 + sender, 4)
+            second = jnp.where(lax.rem(p, 2) == sender, 0, 1)
+            side = jnp.where(sender == core, 0, 1)
+            row = ((side * 4 + back) * 2 + second) * BLK
+            for j in range(BLK):
+                filled[places[p, j]] = fresh[row + j]
+            return 0
+
+        lax.fori_loop(k * groups, (k + 1) * groups, one, 0)
+
     @pl.when(role != 0)
     def _():
         arrivals = [loads(k) for k in range(SEGMENTS)]
-        for j in range(3):
-            for k in range(SEGMENTS):
-                arrivals[k][j].start()
+        moves = [
+            pltpu.make_async_copy(
+                ref, fresh.at[pl.ds(side * 8 * BLK, 8 * BLK)], sems.at[3, side]
+            )
+            for side, ref in enumerate((near_ref, far_ref))
+        ]
+        for k in range(SEGMENTS):
+            arrivals[k][0].start()
+        for copy in moves:
+            copy.start()
+        for k in range(SEGMENTS):
+            arrivals[k][1].start()
+            arrivals[k][2].start()
         for k in range(SEGMENTS):
             arrivals[k][0].wait()
         for i in range(N_PIPE):
@@ -610,20 +633,11 @@
             arrivals[k][1].wait()
             arrivals[k][2].wait()
             fill(k)
-        listing.wait()
-        for side, ref in enumerate((near_ref, far_ref)):
-            sender = core if side == 0 else 1 - core
-            for k in range(4):
-                for e in range(2):
-                    owner_y = jnp.where(sender == 0, 1 - y, y)
-                    back = jnp.where(sender == 0, k + 1, k)
-                    owner_column = lax.rem(column + 4 - back, 4)
-                    owner_core = sender if e == 0 else 1 - sender
-                    owner = (owner_y * 4 + owner_column) * 2 + owner_core
-                    row = (k * 2 + e) * BLK
-                    for j in range(BLK):
-                        filled[places[owner, j]] = ref[row + j]
-        for k in range(SEGMENTS):
+            if k == 0:
+                listing.wait()
+                for copy in moves:
+                    copy.wait()
+            patch(k)
             store(k).start()
         for k in range(SEGMENTS):
             store(k).wait()
@@ -634,21 +648,22 @@
     return chain(
         place_kernel,
         (index, *own, *own_fresh, *got, near, far),
-        [SM] + [HB] * 3 + [VM] * 3 + [HB] * 3 + [VM] * 2,
+        [SM] + [HB] * 3 + [VM] * 3 + [HB] * 5,
         [HB],
         [pltpu.HBM((SLOTS, BLK, 2 * HD), jnp.bfloat16)],
         [
             pltpu.VMEM((entries + 1, BLK // 2, HD), jnp.bfloat16),
             pltpu.VMEM((entries + 1, BLK // 2, HD), jnp.bfloat16),
             pltpu.VMEM((SLOTS + 1, BLK, HD), jnp.bfloat16),
+            pltpu.VMEM((N_PIPE * BLK, BLK, 2 * HD), jnp.bfloat16),
             pltpu.VMEM((SLOTS + 1, BLK, 2 * HD), jnp.bfloat16),
             pltpu.VMEM((N_PIPE, HD), jnp.int32),
             pltpu.SMEM((N_PIPE, HD), jnp.int32),
-            pltpu.SemaphoreType.DMA((3, SEGMENTS)),
+            pltpu.SemaphoreType.DMA((4, SEGMENTS)),
             pltpu.SemaphoreType.DMA((SEGMENTS + 1,)),
         ],
         name="place",
-        mib=56,
+        mib=60,
     )[0]
 
 
@@ -779,7 +794,7 @@
         high, low = ring_shift(*add_step(chain, high, low, sums[0], sums[1]))
         fresh, *own_fresh = fresh_rows(chain, sums[2], high, low, cosine, sine)
         moved, beside = cross(fresh), cross(fresh, 9)
-        attention = attend(chain, query_rows, cache, fresh, cache_len, 0, 4)
+        attention = attend(chain, query_rows, cache, fresh, cache_len, 0, 2)
         return attention, fresh, own_fresh, moved, beside, chain.token
 
     got_lower = cross(got_upper)
@@ -787,7 +802,7 @@
     attention, fresh, own_fresh, moved, beside, chain.token = fenced(late, operands)
     pair, got_lower = pack(chain, (moved, beside), (got_lower,))
     reached = [spread(pair, k) for k in range(4)]
-    attention = attend(chain, query_rows, cache, fresh, cache_len, 4, 2, (attention,))
+    attention = attend(chain, query_rows, cache, fresh, cache_len, 2, 4, (attention,))
     (near,) = pack(chain, reached, (), pair)
     far = pipe_move(near, lambda y, c, core: (y, c, 1 - core))
     attention = attend(chain, query_rows, cache, fresh, cache_len, 6, 2, (attention,))

time: 129 us -> 126 us (0.977)
  waiting for transfers between devices: 21.5 us -> 18.7 us
    ppermute x5, waiting for transfers between devices: 7.63 us -> 4.82 us  [pipe_move(): return lax.ppermute(x, 'pipe', pairs)]
  transfers between devices with their start and end apart: 21 -> 21, of which waited for: 6 -> 5; matrix products, arithmetic and copies ran while one was open for 1% -> 1% of each run, Pallas kernels for 29% -> 29%
where the time goes in v3:
time: 126 us; the launch traced here: 125 us
  starting transfers between devices  55.8 us (44%)
  Pallas kernels  47.1 us (37%)
  waiting for transfers between devices  18.7 us (15%)
  local copies, waits for them, and re-layouts  1.93 us (2%)
    pallas_call x15, Pallas kernels, __call__(): pl.pallas_call(body, in_specs=list(specs) + [VM] * extra, out_specs=list(...  47.1 us
    ppermute x6, starting transfers between devices, cross(): return lax.ppermute(x, ('role', 'pipe'), pairs)  19.5 us
    ppermute x8, starting transfers between devices, ring_shift(): return (lax.ppermute(high, 'tp', up), lax.ppermute(low, 'tp', down))  14.5 us
    ppermute x8, waiting for transfers between devices, ring_shift(): return (lax.ppermute(high, 'tp', up), lax.ppermute(low, 'tp', down))  13.9 us
    all_to_all x2, starting transfers between devices, pipe_exchange(): return lax.all_to_all(parts, 'pipe', 0, 0, tiled=True).reshape(x.shape)  13.5 us
    ppermute x5, starting transfers between devices, pipe_move(): return lax.ppermute(x, 'pipe', pairs)  8.23 us
    ppermute x5, waiting for transfers between devices, pipe_move(): return lax.ppermute(x, 'pipe', pairs)  4.82 us
  transfers between devices with their start and end apart: 21, of which 5 were waited for; matrix products, arithmetic and copies ran while one was open for 1% of the time, Pallas kernels for 29%

profile of v3, /device:TPU:1, one launch (start us, length us, event | category | flops | bytes accessed | tf_op | source)
XLA Modules:
  0.0 125.5 jit_solution(15473757114965152980)
XLA Ops:
  0.6 0.0 copy-start.6
  0.7 3.4 %live_upper.1 = (bf16[257,8,128]{2,1,0:T(8,128)(2,1)}, bf16[8,128]{1,0:T(8,128)(2,1)S(1)}, f32[8,128]{1,0:T(8,128)}) custom-call(s32[1,256]{1,0:T(1,128)} %refs_3_.3, bf16[256,16,256]{2,1,0:T(8,128)(2,1)} %bitcast.12, s32[272]{0:T(512)} %refs_2_.2), custom_call_target="tpu_custom_call" | custom-call | flops 1 | bytes 1 | tf_op jit(solution)/shard_map/live_upper/pallas_call | solution.py:52
  4.1 5.5 %collective-permute-start.10 = (bf16[257,8,128]{2,1,0:T(8,128)(2,1)}, bf16[257,8,128]{2,1,0:T(8,128)(2,1)S(1)}, u32[]{:S(2)}, u32[]{:S(2)}) collective-permute-start(bf16[257,8,128]{2,1,0:T(8,128)(2,1)} %get-tuple-element.130.refs_1_), channel_id=1, source_target_pairs={{0,192},{8,200},{16,208},{24,216},{32,224},{40,232},{48,240},{56,2... | collective-permute-start | bytes 1579016 | tf_op jit(solution)/shard_map/ppermute | solution.py:89
  9.6 0.0 copy-start.5
  9.6 0.7 copy-done.5
  10.3 2.5 %live_rest.1 = (bf16[256,8,128]{2,1,0:T(8,128)(2,1)}, bf16[256,8,128]{2,1,0:T(8,128)(2,1)}, bf16[256,8,128]{2,1,0:T(8,128)(2,1)}, bf16[256,16,128]{2,1,0:T(8,128)(2,1)}, f32[8,128]{1,0:T(8,128)S(1)}) custom-call(s32[1,256]{1,0:T(1,128)S(1)} %copy-done.16, bf16[256,16,256]{2,1,0:T(8,128)(2,1)S(1)} %bitcast.13, f32[8,128]{1,0:T(8,128)S(1)} %copy-done.5), custom_call_target="tpu_custom_call" | custom-call | flops 1 | bytes 1 | tf_op jit(solution)/shard_map/live_rest/pallas_call | solution.py:52
  12.8 0.0 copy-start.4
  12.8 0.6 copy-done.4
  13.4 1.3 %collective-permute-start.11 = (bf16[256,8,128]{2,1,0:T(8,128)(2,1)}, bf16[256,8,128]{2,1,0:T(8,128)(2,1)S(1)}, u32[]{:S(2)}, u32[]{:S(2)}) collective-permute-start(bf16[256,8,128]{2,1,0:T(8,128)(2,1)} %get-tuple-element.144.refs_1_), channel_id=1, source_target_pairs={{0,192},{8,200},{16,208},{24,216},{32,224},{40,232},{48,240},{56,2... | collective-permute-start | bytes 1572872 | tf_op jit(solution)/shard_map/ppermute | solution.py:89
  14.7 1.3 %collective-permute-start.12 = (bf16[256,8,128]{2,1,0:T(8,128)(2,1)}, bf16[256,8,128]{2,1,0:T(8,128)(2,1)S(1)}, u32[]{:S(2)}, u32[]{:S(2)}) collective-permute-start(bf16[256,8,128]{2,1,0:T(8,128)(2,1)} %get-tuple-element.145.refs_2_), channel_id=1, source_target_pairs={{0,192},{8,200},{16,208},{24,216},{32,224},{40,232},{48,240},{56,2... | collective-permute-start | bytes 1572872 | tf_op jit(solution)/shard_map/ppermute | solution.py:89
  16.0 6.3 %project.1 = (bf16[128,256]{1,0:T(8,128)(2,1)}, bf16[144,256]{1,0:T(8,128)(2,1)}, bf16[272,256]{1,0:T(8,128)(2,1)}, bf16[272,256]{1,0:T(8,128)(2,1)}, bf16[272,2...) custom-call(bf16[256,1024]{1,0:T(8,128)(2,1)} %bitcast.22, ...), custom_call_target="tpu_custom_call" | custom-call | flops 1 | bytes 1 | tf_op jit(solution)/shard_map/project/pallas_call | solution.py:52
  22.3 0.0 collective-permute-done.10
  22.3 0.0 copy-start.1
  22.4 30.6 %conditional.2 = (s32[4,544]{1,0:T(4,128)S(1)}, bf16[560,8,128]{2,1,0:T(8,128)(2,1)}, bf16[272,256]{1,0:T(8,128)(2,1)}, bf16[272,256]{1,0:T(8,128)(2,1)}, f32[8,128]{1,0:T(8,128)S(1)}) conditional(s32[]{:T(128)} %convert_element_type.11, () %tuple.25, (bf16[8,128]{1,0:T(8,128)(2,1)S(1)}, bf16[256,8,128]{2,1,0:T(8,128)(2,1)S(1)}, ...), branch_computations={%region_0.1_spmd, %region_1.2_spmd} | conditional | flops 3 | bytes 9011683 | solution.py:84
  22.4 3.7 %first_dispatch.1 = (bf16[560,8,128]{2,1,0:T(8,128)(2,1)}, s32[4,544]{1,0:T(4,128)S(1)}, f32[8,128]{1,0:T(8,128)S(1)}) custom-call(bf16[8,128]{1,0:T(8,128)(2,1)S(1)} %get-tuple-element.42.refs_0_, bf16[256,8,128]{2,1,0:T(8,128)(2,1)S(1)} %get-tuple-element.43.refs_1_, bf16[257,8,128]{2,1,0:T(8,128)(2,1)S(1)} %get-tuple-element.44.refs_2_, ...), custom_call_target="tpu_custom_call" | custom-call | flops 1 | bytes 1 | tf_op jit(solution)/shard_map/cond/branch_1_fun/first_dispatch/pallas_call | solution.py:52
  26.1 5.4 %all-to-all-start = ((bf16[16,35,8,128]{3,2,1,0:T(8,128)(2,1)}), bf16[16,35,8,128]{3,2,1,0:T(8,128)(2,1)}, u32[]{:S(2)}, u32[]{:S(2)}) async-start(bf16[16,35,8,128]{3,2,1,0:T(8,128)(2,1)} %bitcast.21), calls=%async_computation | async-start | bytes 2293760 | tf_op jit(solution)/shard_map/cond/branch_1_fun/all_to_all | solution.py:115
  31.6 5.7 %collective-permute-start.1 = (bf16[144,256]{1,0:T(8,128)(2,1)S(1)}, bf16[144,256]{1,0:T(8,128)(2,1)S(1)}, u32[]{:S(2)}, u32[]{:S(2)}) collective-permute-start(bf16[144,256]{1,0:T(8,128)(2,1)S(1)} %copy-done.17), channel_id=1, source_target_pairs={{0,7},{1,0},{2,1},{3,2},{4,3},{5,4},{6,5},{7,6},{8,15},{9,8},{10,9... | collective-permute-start | bytes 221192 | tf_op jit(solution)/shard_map/cond/branch_1_fun/ppermute | solution.py:183
  37.2 0.0 collective-permute-start
  37.2 4.7 %collective-permute-done.refs_0_ = bf16[128,256]{1,0:T(8,128)(2,1)S(1)} collective-permute-done((bf16[128,256]{1,0:T(8,128)(2,1)S(1)}, bf16[128,256]{1,0:T(8,128)(2,1)S(1)}, u32[]{:S(2)}, u32[]{:S(2)}) %collective-permute-start) | collective-permute-done | bytes 65568 | tf_op jit(solution)/shard_map/cond/branch_1_fun/ppermute | solution.py:183
  41.9 0.0 collective-permute-done.1.refs_1_
  42.0 0.1 collective-permute-start.2
  42.1 2.7 %collective-permute-start.3 = (bf16[272,256]{1,0:T(8,128)(2,1)S(1)}, bf16[272,256]{1,0:T(8,128)(2,1)S(1)}, u32[]{:S(2)}, u32[]{:S(2)}) collective-permute-start(bf16[272,256]{1,0:T(8,128)(2,1)S(1)} %get-tuple-element.54), channel_id=1, source_target_pairs={{0,7},{1,0},{2,1},{3,2},{4,3},{5,4},{6,5},{7,6},{8,15},{9,8},{10,9... | collective-permute-start | bytes 417800 | tf_op jit(solution)/shard_map/cond/branch_1_fun/ppermute | solution.py:183
  44.7 2.8 %collective-permute-done.2.refs_0_ = bf16[272,256]{1,0:T(8,128)(2,1)S(1)} collective-permute-done((bf16[272,256]{1,0:T(8,128)(2,1)S(1)}, bf16[272,256]{1,0:T(8,128)(2,1)S(1)}, u32[]{:S(2)}, u32[]{:S(2)}) %collective-permute-start.2) | collective-permute-done | bytes 139296 | tf_op jit(solution)/shard_map/cond/branch_1_fun/ppermute | solution.py:183
  47.6 0.0 collective-permute-done.3.refs_1_
  47.6 0.1 collective-permute-start.4
  47.7 2.7 %collective-permute-start.5 = (bf16[272,256]{1,0:T(8,128)(2,1)S(1)}, bf16[272,256]{1,0:T(8,128)(2,1)}, u32[]{:S(2)}, u32[]{:S(2)}) collective-permute-start(bf16[272,256]{1,0:T(8,128)(2,1)S(1)} %get-tuple-element.59), channel_id=1, source_target_pairs={{0,7},{1,0},{2,1},{3,2},{4,3},{5,4},{6,5},{7,6},{8,15},{9,8},{10,9... | collective-permute-start | bytes 417800 | tf_op jit(solution)/shard_map/cond/branch_1_fun/ppermute | solution.py:183
  50.4 2.5 %collective-permute-done.4 = bf16[272,256]{1,0:T(8,128)(2,1)} collective-permute-done((bf16[272,256]{1,0:T(8,128)(2,1)S(1)}, bf16[272,256]{1,0:T(8,128)(2,1)}, u32[]{:S(2)}, u32[]{:S(2)}) %collective-permute-start.4) | collective-permute-done | bytes 139296 | tf_op jit(solution)/shard_map/cond/branch_1_fun/ppermute | solution.py:183
  52.9 0.0 collective-permute-done.5
  52.9 0.0 all-to-all-done
  52.9 7.2 %collective-permute-start.13 = (bf16[560,8,128]{2,1,0:T(8,128)(2,1)}, bf16[560,8,128]{2,1,0:T(8,128)(2,1)}, u32[]{:S(2)}, u32[]{:S(2)}) collective-permute-start(bf16[560,8,128]{2,1,0:T(8,128)(2,1)} %get-tuple-element.153.refs_7_), channel_id=1, source_target_pairs={{0,192},{8,200},{16,208},{24,216},{32,224},{40,232},{48,240},{56,2... | collective-permute-start | bytes 3440648 | tf_op jit(solution)/shard_map/ppermute | solution.py:89
  60.2 0.0 collective-permute-done.11.refs_3_
  60.2 0.0 collective-permute-done.12.refs_4_
  60.2 3.0 %second_dispatch.1 = (bf16[544,16,128]{2,1,0:T(8,128)(2,1)}, f32[8,128]{1,0:T(8,128)S(1)}) custom-call(s32[4,544]{1,0:T(4,128)S(1)} %get-tuple-element.143.refs_0_, bf16[256,8,128]{2,1,0:T(8,128)(2,1)S(1)} %copy-done.1, bf16[256,8,128]{2,1,0:T(8,128)(2,1)S(1)} %copy-done.2, bf16[256,8,128]{2,1,0:T(8,128)(2,1)S(1)} %collective-permute-done.11.refs_3_, ...), custom_call_target="tpu_custom_call" | custom-call | flops 1 | bytes 1 | tf_op jit(solution)/shard_map/second_dispatch/pallas_call | solution.py:52
  63.2 0.0 copy-start.7
  63.2 0.0 copy-start.8
  63.3 8.1 %all-to-all-start.1 = ((bf16[16,34,16,128]{3,2,1,0:T(8,128)(2,1)}), bf16[16,34,16,128]{3,2,1,0:T(8,128)(2,1)}, u32[]{:S(2)}, u32[]{:S(2)}) async-start(bf16[16,34,16,128]{3,2,1,0:T(8,128)(2,1)} %bitcast.20), calls=%async_computation.1 | async-start | bytes 4456448 | tf_op jit(solution)/shard_map/all_to_all | solution.py:115
  71.4 0.5 fusion
  71.9 0.1 pad_maximum_fusion
  72.1 18.4 %conditional.3 = (bf16[256,1024]{1,0:T(8,128)(2,1)}, bf16[16,16,256]{2,1,0:T(8,128)(2,1)}, bf16[16,8,128]{2,1,0:T(8,128)(2,1)S(1)}, bf16[16,8,128]{2,1,0:T(8,128...) conditional(s32[]{:T(128)} %convert_element_type.11, () %tuple.24, ...), branch_computations={%region_2.3_spmd, %region_3.4_spmd} | conditional | flops 3 | bytes 2162915 | solution.py:84
  72.1 1.0 add_step.5
  73.1 0.1 collective-permute-start.6
  73.2 3.3 %collective-permute-start.7 = (bf16[272,256]{1,0:T(8,128)(2,1)S(1)}, bf16[272,256]{1,0:T(8,128)(2,1)S(1)}, u32[]{:S(2)}, u32[]{:S(2)}) collective-permute-start(bf16[272,256]{1,0:T(8,128)(2,1)S(1)} %get-tuple-element.70), channel_id=1, source_target_pairs={{0,7},{1,0},{2,1},{3,2},{4,3},{5,4},{6,5},{7,6},{8,15},{9,8},{10,9... | collective-permute-start | bytes 417800 | tf_op jit(solution)/shard_map/cond/branch_1_fun/ppermute | solution.py:183
  76.5 3.8 %collective-permute-done.6.refs_1_ = bf16[272,256]{1,0:T(8,128)(2,1)S(1)} collective-permute-done((bf16[272,256]{1,0:T(8,128)(2,1)S(1)}, bf16[272,256]{1,0:T(8,128)(2,1)S(1)}, u32[]{:S(2)}, u32[]{:S(2)}) %collective-permute-start.6) | collective-permute-done | bytes 139296 | tf_op jit(solution)/shard_map/cond/branch_1_fun/ppermute | solution.py:183
  80.3 0.0 collective-permute-done.7.refs_2_
  80.3 0.9 fresh.1
  81.1 2.2 %collective-permute-start.9 = (bf16[16,16,256]{2,1,0:T(8,128)(2,1)}, bf16[16,16,256]{2,1,0:T(8,128)(2,1)}, u32[]{:S(2)}, u32[]{:S(2)}) collective-permute-start(bf16[16,16,256]{2,1,0:T(8,128)(2,1)} %get-tuple-element.194.refs_2_), channel_id=1, source_target_pairs={{0,200},{8,192},{16,216},{24,208},{32,232},{40,224},{48,248},{56,2... | collective-permute-start | bytes 393224 | tf_op jit(solution)/shard_map/cond/branch_1_fun/ppermute | solution.py:89
  83.4 1.9 %collective-permute-start.8 = (bf16[16,16,256]{2,1,0:T(8,128)(2,1)}, bf16[16,16,256]{2,1,0:T(8,128)(2,1)}, u32[]{:S(2)}, u32[]{:S(2)}) collective-permute-start(bf16[16,16,256]{2,1,0:T(8,128)(2,1)} %get-tuple-element.194.refs_2_), channel_id=1, source_target_pairs={{0,192},{8,200},{16,208},{24,216},{32,224},{40,232},{48,240},{56,2... | collective-permute-start | bytes 393224 | tf_op jit(solution)/shard_map/cond/branch_1_fun/ppermute | solution.py:89
  85.3 5.2 %attend.3 = (bf16[256,1024]{1,0:T(8,128)(2,1)}, f32[8,128]{1,0:T(8,128)S(1)}) custom-call(bf16[256,1024]{1,0:T(8,128)(2,1)S(1)} %get-tuple-element.61.refs_0_, bf16[4096,256]{1,0:T(8,128)(2,1)S(1)} %get-tuple-element.62.refs_1_, bf16[16,16,256]{2,1,0:T(8,128)(2,1)} %get-tuple-element.194.refs_2_, s32[1,256]{1,0:T(1,128)S(1)} %get-tuple-element.75.refs_3_, ...), custom_call_target="tpu_custom_call" | custom-call | flops 1 | bytes 1 | tf_op jit(solution)/shard_map/cond/branch_1_fun/attend/pallas_call | solution.py:52
  90.5 0.0 collective-permute-done.9
  90.5 0.0 collective-permute-done.8
  90.5 1.0 pack.2
  91.5 4.9 %collective-permute-start.17 = (bf16[32,16,256]{2,1,0:T(8,128)(2,1)S(1)}, bf16[32,16,256]{2,1,0:T(8,128)(2,1)S(1)}, u32[]{:S(2)}, u32[]{:S(2)}) collective-permute-start(bf16[32,16,256]{2,1,0:T(8,128)(2,1)S(1)} %get-tuple-element.157.refs_4_), channel_id=1, source_target_pairs={{8,120},{24,72},{40,88},{56,104},{72,56},{88,8},{104,24},{120,40},... | collective-permute-start | bytes 786440 | tf_op jit(solution)/shard_map/ppermute | solution.py:101
  96.5 0.9 collective-permute-start.16
  97.4 1.1 collective-permute-start.15
  98.5 0.6 collective-permute-start.14
  99.1 8.0 %attend.4 = (bf16[256,1024]{1,0:T(8,128)(2,1)}, f32[8,128]{1,0:T(8,128)S(1)}) custom-call(bf16[256,1024]{1,0:T(8,128)(2,1)S(1)} %bitcast.18, bf16[4096,256]{1,0:T(8,128)(2,1)S(1)} %bitcast.15, bf16[16,16,256]{2,1,0:T(8,128)(2,1)} %get-tuple-element.149.refs_2_, s32[1,256]{1,0:T(1,128)S(1)} %copy-done.16, ...), custom_call_target="tpu_custom_call", output_to_operand_aliasing={{0}: (4, {})} | custom-call | flops 1 | bytes 1 | tf_op jit(solution)/shard_map/attend/pallas_call | solution.py:52
  107.1 0.0 copy-start.9
  107.2 4.8 %collective-permute-done.15.refs_1_ = bf16[32,16,256]{2,1,0:T(8,128)(2,1)S(1)} collective-permute-done((bf16[32,16,256]{2,1,0:T(8,128)(2,1)S(1)}, bf16[32,16,256]{2,1,0:T(8,128)(2,1)S(1)}, u32[]{:S(2)}, u32[]{:S(2)}) %collective-permute-start.15) | collective-permute-done | bytes 262176 | tf_op jit(solution)/shard_map/ppermute | solution.py:101
  112.0 0.0 collective-permute-done.14.refs_0_
  112.0 0.1 pack.3
  112.1 0.6 collective-permute-start.18
  112.7 5.2 %attend.5 = (bf16[256,1024]{1,0:T(8,128)(2,1)}, f32[8,128]{1,0:T(8,128)S(1)}) custom-call(bf16[256,1024]{1,0:T(8,128)(2,1)S(1)} %bitcast.19, bf16[4096,256]{1,0:T(8,128)(2,1)S(1)} %bitcast.16, bf16[16,16,256]{2,1,0:T(8,128)(2,1)} %get-tuple-element.149.refs_2_, s32[1,256]{1,0:T(1,128)S(1)} %copy-done.16, ...), custom_call_target="tpu_custom_call", output_to_operand_aliasing={{0}: (4, {})} | custom-call | flops 1 | bytes 1 | tf_op jit(solution)/shard_map/attend/pallas_call | solution.py:52
  117.9 0.6 copy-done.3
  118.5 6.9 %place.1 = (bf16[544,16,256]{2,1,0:T(8,128)(2,1)}, f32[8,128]{1,0:T(8,128)}) custom-call(s32[4,544]{1,0:T(4,128)S(1)} %get-tuple-element.143.refs_0_, bf16[257,8,128]{2,1,0:T(8,128)(2,1)} %get-tuple-element.130.refs_1_, bf16[256,8,128]{2,1,0:T(8,128)(2,1)} %get-tuple-element.129.refs_2_, bf16[256,16,128]{2,1,0:T(8,128)(2,1)} %get-tuple-element.161.refs_3_, ...), custom_call_target="tpu_custom_call" | custom-call | flops 1 | bytes 1 | tf_op jit(solution)/shard_map/place/pallas_call | solution.py:52
  (37 shorter events, 0.2 us)
Async XLA Ops:
  0.6 9.0 %copy-start.16 = (s32[1,256]{1,0:T(1,128)S(1)}, s32[1,256]{1,0:T(1,128)}, u32[]{:S(2)}) copy-start(s32[1,256]{1,0:T(1,128)} %refs_3_.3) | copy-start | bytes 3076
  0.6 9.0 %copy-start.6 = (bf16[1,4096,256]{2,1,0:T(8,128)(2,1)S(1)}, bf16[1,4096,256]{2,1,0:T(8,128)(2,1)}, u32[]{:S(2)}) copy-start(bf16[1,4096,256]{2,1,0:T(8,128)(2,1)} %param.15) | copy-start | bytes 6291460
  4.1 18.2 %collective-permute-start.10 = (bf16[257,8,128]{2,1,0:T(8,128)(2,1)}, bf16[257,8,128]{2,1,0:T(8,128)(2,1)S(1)}, u32[]{:S(2)}, u32[]{:S(2)}) collective-permute-start(bf16[257,8,128]{2,1,0:T(8,128)(2,1)} %get-tuple-element.130.refs_1_), channel_id=1, source_target_pairs={{0,192},{8,200},{16,208},{24,216},{32,224},{40,232},{48,240},{56,2... | collective-permute-start | bytes 1579016 | tf_op jit(solution)/shard_map/ppermute | solution.py:89
  9.6 0.7 copy-start.5
  12.8 0.6 copy-start.4
  13.4 46.8 %collective-permute-start.11 = (bf16[256,8,128]{2,1,0:T(8,128)(2,1)}, bf16[256,8,128]{2,1,0:T(8,128)(2,1)S(1)}, u32[]{:S(2)}, u32[]{:S(2)}) collective-permute-start(bf16[256,8,128]{2,1,0:T(8,128)(2,1)} %get-tuple-element.144.refs_1_), channel_id=1, source_target_pairs={{0,192},{8,200},{16,208},{24,216},{32,224},{40,232},{48,240},{56,2... | collective-permute-start | bytes 1572872 | tf_op jit(solution)/shard_map/ppermute | solution.py:89
  14.7 45.5 %collective-permute-start.12 = (bf16[256,8,128]{2,1,0:T(8,128)(2,1)}, bf16[256,8,128]{2,1,0:T(8,128)(2,1)S(1)}, u32[]{:S(2)}, u32[]{:S(2)}) collective-permute-start(bf16[256,8,128]{2,1,0:T(8,128)(2,1)} %get-tuple-element.145.refs_2_), channel_id=1, source_target_pairs={{0,192},{8,200},{16,208},{24,216},{32,224},{40,232},{48,240},{56,2... | collective-permute-start | bytes 1572872 | tf_op jit(solution)/shard_map/ppermute | solution.py:89
  16.0 6.3 %copy-start.10 = (bf16[256,8,128]{2,1,0:T(8,128)(2,1)S(1)}, bf16[256,8,128]{2,1,0:T(8,128)(2,1)}, u32[]{:S(2)}) copy-start(bf16[256,8,128]{2,1,0:T(8,128)(2,1)} %get-tuple-element.129.refs_2_) | copy-start | bytes 1572868
  22.3 37.8 %copy-start.1 = (bf16[256,8,128]{2,1,0:T(8,128)(2,1)S(1)}, bf16[256,8,128]{2,1,0:T(8,128)(2,1)}, u32[]{:S(2)}) copy-start(bf16[256,8,128]{2,1,0:T(8,128)(2,1)} %get-tuple-element.144.refs_1_) | copy-start | bytes 1572868
  22.4 37.8 %copy-start.2 = (bf16[256,8,128]{2,1,0:T(8,128)(2,1)S(1)}, bf16[256,8,128]{2,1,0:T(8,128)(2,1)}, u32[]{:S(2)}) copy-start(bf16[256,8,128]{2,1,0:T(8,128)(2,1)} %get-tuple-element.145.refs_2_) | copy-start | bytes 1572868
  26.1 5.5 %copy-start.17 = (bf16[144,256]{1,0:T(8,128)(2,1)S(1)}, bf16[144,256]{1,0:T(8,128)(2,1)}, u32[]{:S(2)}) copy-start(bf16[144,256]{1,0:T(8,128)(2,1)} %get-tuple-element.49) | copy-start | bytes 221188 | tf_op jit(solution)/shard_map/cond
  26.1 11.1 %copy-start.18 = (bf16[128,256]{1,0:T(8,128)(2,1)S(1)}, bf16[128,256]{1,0:T(8,128)(2,1)}, u32[]{:S(2)}) copy-start(bf16[128,256]{1,0:T(8,128)(2,1)} %get-tuple-element.48) | copy-start | bytes 196612 | tf_op jit(solution)/shard_map/cond
  26.1 15.8 %copy-start.12 = (bf16[272,256]{1,0:T(8,128)(2,1)S(1)}, bf16[272,256]{1,0:T(8,128)(2,1)}, u32[]{:S(2)}) copy-start(bf16[272,256]{1,0:T(8,128)(2,1)} %get-tuple-element.50.refs_2_) | copy-start | bytes 417796 | tf_op jit(solution)/shard_map/cond
  26.1 15.8 %copy-start.13 = (bf16[272,256]{1,0:T(8,128)(2,1)S(1)}, bf16[272,256]{1,0:T(8,128)(2,1)}, u32[]{:S(2)}) copy-start(bf16[272,256]{1,0:T(8,128)(2,1)} %get-tuple-element.51.refs_3_) | copy-start | bytes 417796 | tf_op jit(solution)/shard_map/cond
  26.1 21.5 %copy-start.14 = (bf16[272,256]{1,0:T(8,128)(2,1)S(1)}, bf16[272,256]{1,0:T(8,128)(2,1)}, u32[]{:S(2)}) copy-start(bf16[272,256]{1,0:T(8,128)(2,1)} %get-tuple-element.55.refs_2_) | copy-start | bytes 417796 | tf_op jit(solution)/shard_map/cond
  26.1 21.5 %copy-start.15 = (bf16[272,256]{1,0:T(8,128)(2,1)S(1)}, bf16[272,256]{1,0:T(8,128)(2,1)}, u32[]{:S(2)}) copy-start(bf16[272,256]{1,0:T(8,128)(2,1)} %get-tuple-element.56.refs_3_) | copy-start | bytes 417796 | tf_op jit(solution)/shard_map/cond
  26.1 26.8 %all-to-all-start = ((bf16[16,35,8,128]{3,2,1,0:T(8,128)(2,1)}), bf16[16,35,8,128]{3,2,1,0:T(8,128)(2,1)}, u32[]{:S(2)}, u32[]{:S(2)}) async-start(bf16[16,35,8,128]{3,2,1,0:T(8,128)(2,1)} %bitcast.21), calls=%async_computation | async-start | bytes 2293760 | tf_op jit(solution)/shard_map/cond/branch_1_fun/all_to_all | solution.py:115
  31.6 10.4 %collective-permute-start.1 = (bf16[144,256]{1,0:T(8,128)(2,1)S(1)}, bf16[144,256]{1,0:T(8,128)(2,1)S(1)}, u32[]{:S(2)}, u32[]{:S(2)}) collective-permute-start(bf16[144,256]{1,0:T(8,128)(2,1)S(1)} %copy-done.17), channel_id=1, source_target_pairs={{0,7},{1,0},{2,1},{3,2},{4,3},{5,4},{6,5},{7,6},{8,15},{9,8},{10,9... | collective-permute-start | bytes 221192 | tf_op jit(solution)/shard_map/cond/branch_1_fun/ppermute | solution.py:183
  37.2 4.7 %collective-permute-start = (bf16[128,256]{1,0:T(8,128)(2,1)S(1)}, bf16[128,256]{1,0:T(8,128)(2,1)S(1)}, u32[]{:S(2)}, u32[]{:S(2)}) collective-permute-start(bf16[128,256]{1,0:T(8,128)(2,1)S(1)} %copy-done.18), channel_id=1, source_target_pairs={{0,1},{1,2},{2,3},{3,4},{4,5},{5,6},{6,7},{7,0},{8,9},{9,10},{10,1... | collective-permute-start | bytes 196616 | tf_op jit(solution)/shard_map/cond/branch_1_fun/ppermute | solution.py:183
  42.0 5.6 %collective-permute-start.2 = (bf16[272,256]{1,0:T(8,128)(2,1)S(1)}, bf16[272,256]{1,0:T(8,128)(2,1)S(1)}, u32[]{:S(2)}, u32[]{:S(2)}) collective-permute-start(bf16[272,256]{1,0:T(8,128)(2,1)S(1)} %get-tuple-element.53), channel_id=1, source_target_pairs={{0,1},{1,2},{2,3},{3,4},{4,5},{5,6},{6,7},{7,0},{8,9},{9,10},{10,1... | collective-permute-start | bytes 417800 | tf_op jit(solution)/shard_map/cond/branch_1_fun/ppermute | solution.py:183
  42.1 5.5 %collective-permute-start.3 = (bf16[272,256]{1,0:T(8,128)(2,1)S(1)}, bf16[272,256]{1,0:T(8,128)(2,1)S(1)}, u32[]{:S(2)}, u32[]{:S(2)}) collective-permute-start(bf16[272,256]{1,0:T(8,128)(2,1)S(1)} %get-tuple-element.54), channel_id=1, source_target_pairs={{0,7},{1,0},{2,1},{3,2},{4,3},{5,4},{6,5},{7,6},{8,15},{9,8},{10,9... | collective-permute-start | bytes 417800 | tf_op jit(solution)/shard_map/cond/branch_1_fun/ppermute | solution.py:183
  47.6 5.3 %collective-permute-start.4 = (bf16[272,256]{1,0:T(8,128)(2,1)S(1)}, bf16[272,256]{1,0:T(8,128)(2,1)}, u32[]{:S(2)}, u32[]{:S(2)}) collective-permute-start(bf16[272,256]{1,0:T(8,128)(2,1)S(1)} %get-tuple-element.58), channel_id=1, source_target_pairs={{0,1},{1,2},{2,3},{3,4},{4,5},{5,6},{6,7},{7,0},{8,9},{9,10},{10,1... | collective-permute-start | bytes 417800 | tf_op jit(solution)/shard_map/cond/branch_1_fun/ppermute | solution.py:183
  47.7 5.2 %collective-permute-start.5 = (bf16[272,256]{1,0:T(8,128)(2,1)S(1)}, bf16[272,256]{1,0:T(8,128)(2,1)}, u32[]{:S(2)}, u32[]{:S(2)}) collective-permute-start(bf16[272,256]{1,0:T(8,128)(2,1)S(1)} %get-tuple-element.59), channel_id=1, source_target_pairs={{0,7},{1,0},{2,1},{3,2},{4,3},{5,4},{6,5},{7,6},{8,15},{9,8},{10,9... | collective-permute-start | bytes 417800 | tf_op jit(solution)/shard_map/cond/branch_1_fun/ppermute | solution.py:183
  52.9 37.6 %collective-permute-start.13 = (bf16[560,8,128]{2,1,0:T(8,128)(2,1)}, bf16[560,8,128]{2,1,0:T(8,128)(2,1)}, u32[]{:S(2)}, u32[]{:S(2)}) collective-permute-start(bf16[560,8,128]{2,1,0:T(8,128)(2,1)} %get-tuple-element.153.refs_7_), channel_id=1, source_target_pairs={{0,192},{8,200},{16,208},{24,216},{32,224},{40,232},{48,240},{56,2... | collective-permute-start | bytes 3440648 | tf_op jit(solution)/shard_map/ppermute | solution.py:89
  63.2 8.8 %copy-start.7 = (bf16[1,4096,256]{2,1,0:T(8,128)(2,1)S(1)}, bf16[1,4096,256]{2,1,0:T(8,128)(2,1)}, u32[]{:S(2)}) copy-start(bf16[1,4096,256]{2,1,0:T(8,128)(2,1)} %param.15) | copy-start | bytes 6291460
  63.2 8.8 %copy-start.8 = (bf16[1,256,1024]{2,1,0:T(8,128)(2,1)S(1)}, bf16[1,256,1024]{2,1,0:T(8,128)(2,1)}, u32[]{:S(2)}) copy-start(bf16[1,256,1024]{2,1,0:T(8,128)(2,1)} %param.14) | copy-start | bytes 1572868
  63.2 8.8 %copy-start.11 = (bf16[272,256]{1,0:T(8,128)(2,1)S(1)}, bf16[272,256]{1,0:T(8,128)(2,1)}, u32[]{:S(2)}) copy-start(bf16[272,256]{1,0:T(8,128)(2,1)} %get-tuple-element.148) | copy-start | bytes 417796
  63.3 55.2 %all-to-all-start.1 = ((bf16[16,34,16,128]{3,2,1,0:T(8,128)(2,1)}), bf16[16,34,16,128]{3,2,1,0:T(8,128)(2,1)}, u32[]{:S(2)}, u32[]{:S(2)}) async-start(bf16[16,34,16,128]{3,2,1,0:T(8,128)(2,1)} %bitcast.20), calls=%async_computation.1 | async-start | bytes 4456448 | tf_op jit(solution)/shard_map/all_to_all | solution.py:115
  73.1 7.2 %collective-permute-start.6 = (bf16[272,256]{1,0:T(8,128)(2,1)S(1)}, bf16[272,256]{1,0:T(8,128)(2,1)S(1)}, u32[]{:S(2)}, u32[]{:S(2)}) collective-permute-start(bf16[272,256]{1,0:T(8,128)(2,1)S(1)} %get-tuple-element.69), channel_id=1, source_target_pairs={{0,1},{1,2},{2,3},{3,4},{4,5},{5,6},{6,7},{7,0},{8,9},{9,10},{10,1... | collective-permute-start | bytes 417800 | tf_op jit(solution)/shard_map/cond/branch_1_fun/ppermute | solution.py:183
  73.2 7.1 %collective-permute-start.7 = (bf16[272,256]{1,0:T(8,128)(2,1)S(1)}, bf16[272,256]{1,0:T(8,128)(2,1)S(1)}, u32[]{:S(2)}, u32[]{:S(2)}) collective-permute-start(bf16[272,256]{1,0:T(8,128)(2,1)S(1)} %get-tuple-element.70), channel_id=1, source_target_pairs={{0,7},{1,0},{2,1},{3,2},{4,3},{5,4},{6,5},{7,6},{8,15},{9,8},{10,9... | collective-permute-start | bytes 417800 | tf_op jit(solution)/shard_map/cond/branch_1_fun/ppermute | solution.py:183
  81.1 9.4 %collective-permute-start.9 = (bf16[16,16,256]{2,1,0:T(8,128)(2,1)}, bf16[16,16,256]{2,1,0:T(8,128)(2,1)}, u32[]{:S(2)}, u32[]{:S(2)}) collective-permute-start(bf16[16,16,256]{2,1,0:T(8,128)(2,1)} %get-tuple-element.194.refs_2_), channel_id=1, source_target_pairs={{0,200},{8,192},{16,216},{24,208},{32,232},{40,224},{48,248},{56,2... | collective-permute-start | bytes 393224 | tf_op jit(solution)/shard_map/cond/branch_1_fun/ppermute | solution.py:89
  83.4 7.1 %collective-permute-start.8 = (bf16[16,16,256]{2,1,0:T(8,128)(2,1)}, bf16[16,16,256]{2,1,0:T(8,128)(2,1)}, u32[]{:S(2)}, u32[]{:S(2)}) collective-permute-start(bf16[16,16,256]{2,1,0:T(8,128)(2,1)} %get-tuple-element.194.refs_2_), channel_id=1, source_target_pairs={{0,192},{8,200},{16,208},{24,216},{32,224},{40,232},{48,240},{56,2... | collective-permute-start | bytes 393224 | tf_op jit(solution)/shard_map/cond/branch_1_fun/ppermute | solution.py:89
  91.5 15.6 %collective-permute-start.17 = (bf16[32,16,256]{2,1,0:T(8,128)(2,1)S(1)}, bf16[32,16,256]{2,1,0:T(8,128)(2,1)S(1)}, u32[]{:S(2)}, u32[]{:S(2)}) collective-permute-start(bf16[32,16,256]{2,1,0:T(8,128)(2,1)S(1)} %get-tuple-element.157.refs_4_), channel_id=1, source_target_pairs={{8,120},{24,72},{40,88},{56,104},{72,56},{88,8},{104,24},{120,40},... | collective-permute-start | bytes 786440 | tf_op jit(solution)/shard_map/ppermute | solution.py:101
  96.5 10.7 %collective-permute-start.16 = (bf16[32,16,256]{2,1,0:T(8,128)(2,1)S(1)}, bf16[32,16,256]{2,1,0:T(8,128)(2,1)S(1)}, u32[]{:S(2)}, u32[]{:S(2)}) collective-permute-start(bf16[32,16,256]{2,1,0:T(8,128)(2,1)S(1)} %get-tuple-element.157.refs_4_), channel_id=1, source_target_pairs={{0,48},{8,104},{16,0},{24,120},{32,16},{40,72},{48,32},{56,88},{64... | collective-permute-start | bytes 786440 | tf_op jit(solution)/shard_map/ppermute | solution.py:101
  97.4 14.6 %collective-permute-start.15 = (bf16[32,16,256]{2,1,0:T(8,128)(2,1)S(1)}, bf16[32,16,256]{2,1,0:T(8,128)(2,1)S(1)}, u32[]{:S(2)}, u32[]{:S(2)}) collective-permute-start(bf16[32,16,256]{2,1,0:T(8,128)(2,1)S(1)} %get-tuple-element.157.refs_4_), channel_id=1, source_target_pairs={{0,32},{8,88},{16,48},{24,104},{32,0},{40,120},{48,16},{56,72},{64... | collective-permute-start | bytes 786440 | tf_op jit(solution)/shard_map/ppermute | solution.py:101
  98.5 13.5 %collective-permute-start.14 = (bf16[32,16,256]{2,1,0:T(8,128)(2,1)S(1)}, bf16[32,16,256]{2,1,0:T(8,128)(2,1)S(1)}, u32[]{:S(2)}, u32[]{:S(2)}) collective-permute-start(bf16[32,16,256]{2,1,0:T(8,128)(2,1)S(1)} %get-tuple-element.157.refs_4_), channel_id=1, source_target_pairs={{0,16},{8,72},{16,32},{24,88},{32,48},{40,104},{48,0},{56,120},{64... | collective-permute-start | bytes 786440 | tf_op jit(solution)/shard_map/ppermute | solution.py:101
  107.1 5.5 %copy-start.9 = (bf16[1,256,1024]{2,1,0:T(8,128)(2,1)S(1)}, bf16[1,256,1024]{2,1,0:T(8,128)(2,1)}, u32[]{:S(2)}) copy-start(bf16[1,256,1024]{2,1,0:T(8,128)(2,1)} %param.14) | copy-start | bytes 1572868
  112.1 5.8 %copy-start = (bf16[128,16,256]{2,1,0:T(8,128)(2,1)}, bf16[128,16,256]{2,1,0:T(8,128)(2,1)S(1)}, u32[]{:S(2)}) copy-start(bf16[128,16,256]{2,1,0:T(8,128)(2,1)S(1)} %get-tuple-element.167.refs_10_) | copy-start | bytes 3145732
  112.1 6.4 %collective-permute-start.18 = (bf16[128,16,256]{2,1,0:T(8,128)(2,1)S(1)}, bf16[128,16,256]{2,1,0:T(8,128)(2,1)}, u32[]{:S(2)}, u32[]{:S(2)}) collective-permute-start(bf16[128,16,256]{2,1,0:T(8,128)(2,1)S(1)} %get-tuple-element.167.refs_10_), channel_id=1, source_target_pairs={{0,8},{8,0},{16,24},{24,16},{32,40},{40,32},{48,56},{56,48},{64,72... | collective-permute-start | bytes 3145736 | tf_op jit(solution)/shard_map/ppermute | solution.py:101
  117.9 0.6 copy-start.3
